TPU v7x, 32 devices: a whole 2x2x4 slice. The times are simulated.
32 devices in a mesh: row: 4 (over y, x), col: 4 (over z), depth: 2 (over core).
Axes of the slice: x: 2, y: 2, z: 4, core: 2. Of those that a mesh axis runs over, the one named last changes fastest.
Arguments:
- matrix_tiles: bfloat16 [64, 3, 512, 512], P(('row', 'col', 'depth')), may hold values from 0.00029945374 to 0.29882812
- pattern: int32 [64, 3], replicated, may hold values from 0 to 63, as said below
Outputs:
- inflated: bfloat16 [64, 9, 512, 512], P(('row', 'col', 'depth'))
Inputs may be any that keep to these rules, and one draw needn't show every extreme that they name: `pattern`: row i lists 3 different block columns: i itself first, then one at distance exactly 2 from i, then others at distance 1 to 2 from i, all inside the matrix.
All inputs are finite; a program needn't handle non-finite values.
Results may differ from a plain program's by a relative error of at most 0.0071.
Values may be sent and summed in bfloat16 or wider, within the bound.
No kernel may reach another device: no remote copies, remote signals or barrier semaphores. Data moves between devices by JAX's collectives and lax.ppermute only.
A program may use at most 128 MiB of HBM per device.

v0:
```python
import jax
import jax.numpy as jnp
from jax import lax
from jax.sharding import PartitionSpec as P

W = 2


def extended(block, sides, width):
    for axis, dim in sides:
        count = lax.axis_size(axis)
        forward = [(i, i + 1) for i in range(count - 1)]
        backward = [(target, source) for source, target in forward]
        low = lax.ppermute(
            lax.slice_in_dim(block, block.shape[dim] - width, None, axis=dim), axis, forward
        )
        high = lax.ppermute(lax.slice_in_dim(block, 0, width, axis=dim), axis, backward)
        block = jnp.concatenate([low, block, high], axis=dim)
    return block


def shifted(block, axis, distance):
    devices = range(lax.axis_size(axis))
    route = [(i - distance, i) for i in devices if i - distance in devices]
    return lax.ppermute(block, axis, route)


def merge_slots(products, flat_cols):
    slot_count = flat_cols.shape[0]
    matched_entries = flat_cols[:, None] == flat_cols[None, :]
    positions = jnp.arange(slot_count, dtype=jnp.int32)
    earlier = matched_entries & (positions[None, :] < positions[:, None])
    leading = jnp.logical_not(jnp.any(earlier, axis=1))
    weight = (matched_entries & leading[:, None]).astype(jnp.float32)
    return jnp.einsum("op,pac->oac", weight, products, precision=lax.Precision.HIGHEST)


def expand_rows(matrix_tiles, widened, row_cols, out_cols, diagonal_gap):

    def one_row(group_nodes):
        tile_row, targets, cols_row = group_nodes
        fetched = jnp.take(widened, targets - diagonal_gap, axis=0)
        products = jnp.einsum(
            "sab,stbc->stac", tile_row, fetched, preferred_element_type=jnp.float32
        )
        slot_count = cols_row.shape[0] * cols_row.shape[1]
        flattened = products.reshape(slot_count, products.shape[2], products.shape[3])
        merged = merge_slots(flattened, cols_row.reshape(slot_count))
        grown_similarity = merged.astype(jnp.bfloat16)
        squares = jnp.sum(jnp.square(grown_similarity.astype(jnp.float32)), axis=1)
        return (grown_similarity, squares)

    return lax.map(one_row, (matrix_tiles, row_cols, out_cols))


def body(matrix_tiles, pattern):
    rows_here = matrix_tiles.shape[0]
    slot_total = pattern.shape[1] * pattern.shape[1]
    width = matrix_tiles.shape[3]
    scale_factor = float(slot_total * width)
    start = lax.axis_index(("row", "col", "depth")) * rows_here
    widened = extended(matrix_tiles, ((("row", "col", "depth"), 0),), W)
    diagonal_gap = start - W
    row_cols = lax.dynamic_slice_in_dim(pattern, start, rows_here, 0)
    out_cols = jnp.take(pattern, row_cols, axis=0)
    grown_similarity, squares = expand_rows(matrix_tiles, widened, row_cols, out_cols, diagonal_gap)
    flat_cols = out_cols.reshape(rows_here * slot_total)
    square_rows = squares.reshape(rows_here * slot_total, width)
    reach_devices = (2 * W + rows_here - 1) // rows_here
    window_size = (2 * reach_devices + 1) * rows_here
    window_start = start - reach_devices * rows_here
    local_cols = flat_cols - window_start
    selector = (local_cols[:, None] == jnp.arange(window_size, dtype=jnp.int32)[None, :]).astype(
        jnp.float32
    )
    partials = jnp.einsum("nj,nq->jq", selector, square_rows, precision=lax.Precision.HIGHEST)
    partials = partials.reshape(2 * reach_devices + 1, rows_here, width)
    owned = partials[reach_devices]
    distances = [sign * step for step in range(1, reach_devices + 1) for sign in (1, -1)]
    for displacement in distances:
        owned = owned + shifted(
            partials[reach_devices + displacement], ("row", "col", "depth"), displacement
        )
    pieces = []
    for displacement in range(-reach_devices, reach_devices + 1):
        if displacement == 0:
            pieces.append(owned)
        else:
            pieces.append(shifted(owned, ("row", "col", "depth"), -displacement))
    window = jnp.stack(pieces).reshape(window_size, width)
    needed = jnp.take(window, local_cols, axis=0)
    demanded_lines = needed.reshape(rows_here, slot_total, width)

    def power_normalize_line(group_nodes):
        expanded_row, needed_row = group_nodes
        values = expanded_row.astype(jnp.float32)
        return (scale_factor * jnp.square(values) / needed_row[:, None, :]).astype(jnp.bfloat16)

    return lax.map(power_normalize_line, (grown_similarity, demanded_lines))


def solution(mesh):
    return jax.shard_map(
        body,
        mesh=mesh,
        in_specs=(P(("row", "col", "depth"), None, None, None), P()),
        out_specs=P(("row", "col", "depth"), None, None, None),
        check_vma=False,
    )
```

profile of v0, /device:TPU:5, one launch (start us, length us, event | category | flops | bytes accessed | tf_op | source)
XLA Modules:
  0.0 238.6 jit_solution(8664960827045090823)
XLA Ops:
  0.0 3.8 %collective-permute-start = (bf16[2,3,512,512]{3,2,1,0:T(8,128)(2,1)}, bf16[2,3,512,512]{3,2,1,0:T(8,128)(2,1)S(1)}, u32[]{:S(2)}, u32[]{:S(2)}) collective-permute-start(bf16[2,3,512,512]{3,2,1,0:T(8,128)(2,1)} %param.6), channel_id=1, source_target_pairs={{0,1},{1,2},{2,3},{3,4},{4,5},{5,6},{6,7},{7,8},{8,9},{9,10},{10,1... | collective-permute-start | bytes 9437192 | tf_op jit(solution)/shard_map/ppermute | solution.py:14
  3.8 1.9 collective-permute-start.1
  5.7 0.8 copy.16
  7.7 57.9 %collective-permute-done = bf16[2,3,512,512]{3,2,1,0:T(8,128)(2,1)S(1)} collective-permute-done((bf16[2,3,512,512]{3,2,1,0:T(8,128)(2,1)}, bf16[2,3,512,512]{3,2,1,0:T(8,128)(2,1)S(1)}, u32[]{:S(2)}, u32[]{:S(2)}) %collective-permute-start) | collective-permute-done | bytes 3145760 | tf_op jit(solution)/shard_map/ppermute | solution.py:14
  65.7 9.7 %collective-permute-done.1 = bf16[2,3,512,512]{3,2,1,0:T(8,128)(2,1)} collective-permute-done((bf16[2,3,512,512]{3,2,1,0:T(8,128)(2,1)}, bf16[2,3,512,512]{3,2,1,0:T(8,128)(2,1)}, u32[]{:S(2)}, u32[]{:S(2)}) %collective-permute-start.1) | collective-permute-done | bytes 3145760 | tf_op jit(solution)/shard_map/ppermute | solution.py:17
  75.3 7.7 %pad_maximum_fusion = bf16[6,3,512,512]{3,2,1,0:T(8,128)(2,1)} fusion(bf16[2,3,512,512]{3,2,1,0:T(8,128)(2,1)} %collective-permute-done.1, bf16[2,3,512,512]{3,2,1,0:T(8,128)(2,1)} %param.6, bf16[2,3,512,512]{3,2,1,0:T(8,128)(2,1)S(1)} %collective-permute-done), kind=kLoop, calls=%fused_computation.34 | loop fusion | flops 9437184 | bytes 18874368 | tf_op jit(solution)/shard_map/concatenate | solution.py:18
  83.0 4.6 %broadcast.145.clone.1 = bf16[2,9,512,512]{3,2,1,0:T(8,128)(2,1)} broadcast(bf16[]{:T(256)} %constant.89.clone.1), dimensions={} | broadcast | bytes 9437186 | tf_op jit(solution)/shard_map/broadcast.29
  87.6 101.2 %while.22 = (s32[]{:T(128)}, bf16[2,9,512,512]{3,2,1,0:T(8,128)(2,1)}, f32[2,9,512]{2,1,0:T(8,128)S(1)}, s32[2,3,3]{1,0,2:T(2,128)S(1)}, s32[2,3]{1,0:T(2,128)S(...) while((s32[]{:T(128)}, ...), condition=%wide.region_3.4_spmd, body=%wide.region_0.3_spmd.sunk | while | flops 2682516480 | bytes 67722736 | solution.py:53
  87.6 6.8 %gather_fusion = bf16[3,3,512,512]{3,2,1,0:T(8,128)(2,1)} fusion(bf16[6,3,512,512]{3,2,1,0:T(8,128)(2,1)} %get-tuple-element.233, s32[1024]{0:T(1024)S(1)} %pad_clamp_fusion.4), kind=kCustom, calls=%fused_computation.clone.1 | custom fusion | bytes 9437196 | tf_op jit(solution)/shard_map/while/body/eval_jaxpr/jit(_take)/gather | solution.py:42
  94.5 8.3 %fusion.37 = f32[3,3,512,512]{3,2,1,0:T(8,128)} fusion(bf16[3,3,512,512]{3,2,1,0:T(8,128)(2,1)} %gather_fusion, pred[3]{0:T(512)(128)(4,1)S(1)} %compare_and_fusion.6, bf16[2,3,512,512]{3,2,1,0:T(8,128)(2,1)S(1)} %get-tuple-element.234, s32[]{:T(128)} %get-tuple-element.218), kind=kOutput, calls=%fused_computation.9.clone.1 | convolution fusion | flops 2418278400 | bytes 15729156 | tf_op jit(solution)/shard_map/while/body/eval_jaxpr/sab,stbc->stac/dot_general | solution.py:43
  102.8 16.7 %copy.35 = f32[9,512,512]{2,0,1:T(8,128)} copy(f32[9,512,512]{1,2,0:T(8,128)} %bitcast.61) | data formatting | bytes 18874368 | tf_op jit(solution)/shard_map/while/body/eval_jaxpr/reshape | solution.py:47
  119.9 13.2 %multiply_reduce_fusion.2 = (f32[9,512]{1,0:T(8,128)S(1)}, bf16[9,512,512]{2,0,1:T(8,128)(2,1)S(1)}) fusion(f32[9,512,512]{2,0,1:T(8,128)} %copy.35, s32[9]{0:T(128)S(1)} %eq.75, pred[9]{0:T(512)(128)(4,1)S(1)} %not.8), kind=kOutput, calls=%fused_computation.6.clone.1 | convolution fusion | flops 264236704 | bytes 14174253 | tf_op jit(solution)/shard_map/while/body/eval_jaxpr/op,pac->oac/dot_general | solution.py:35
  133.1 5.1 %copy_dynamic-update-slice_fusion.2 = bf16[2,9,512,512]{3,2,1,0:T(8,128)(2,1)} fusion(bf16[2,9,512,512]{3,2,1,0:T(8,128)(2,1)} %get-tuple-element.219, s32[]{:T(128)} %get-tuple-element.218, bf16[1,9,512,512]{3,1,2,0:T(8,128)(2,1)S(1)} %bitcast.62), kind=kLoop, calls=%fused_computation.8.clone.1 | loop fusion | bytes 9437696 | tf_op jit(solution)/shard_map/while/body/jit(dynamic_update_index_in_dim)/dynamic_update_slice | solution.py:53
  138.2 6.8 %gather_fusion = bf16[3,3,512,512]{3,2,1,0:T(8,128)(2,1)} fusion(bf16[6,3,512,512]{3,2,1,0:T(8,128)(2,1)} %get-tuple-element.233, s32[1024]{0:T(1024)S(1)} %pad_clamp_fusion.4), kind=kCustom, calls=%fused_computation.clone.1 | custom fusion | bytes 9437196 | tf_op jit(solution)/shard_map/while/body/eval_jaxpr/jit(_take)/gather | solution.py:42
  145.0 8.3 %fusion.37 = f32[3,3,512,512]{3,2,1,0:T(8,128)} fusion(bf16[3,3,512,512]{3,2,1,0:T(8,128)(2,1)} %gather_fusion, pred[3]{0:T(512)(128)(4,1)S(1)} %compare_and_fusion.6, bf16[2,3,512,512]{3,2,1,0:T(8,128)(2,1)S(1)} %get-tuple-element.234, s32[]{:T(128)} %get-tuple-element.218), kind=kOutput, calls=%fused_computation.9.clone.1 | convolution fusion | flops 2418278400 | bytes 15729156 | tf_op jit(solution)/shard_map/while/body/eval_jaxpr/sab,stbc->stac/dot_general | solution.py:43
  153.4 16.7 %copy.35 = f32[9,512,512]{2,0,1:T(8,128)} copy(f32[9,512,512]{1,2,0:T(8,128)} %bitcast.61) | data formatting | bytes 18874368 | tf_op jit(solution)/shard_map/while/body/eval_jaxpr/reshape | solution.py:47
  170.4 13.2 %multiply_reduce_fusion.2 = (f32[9,512]{1,0:T(8,128)S(1)}, bf16[9,512,512]{2,0,1:T(8,128)(2,1)S(1)}) fusion(f32[9,512,512]{2,0,1:T(8,128)} %copy.35, s32[9]{0:T(128)S(1)} %eq.75, pred[9]{0:T(512)(128)(4,1)S(1)} %not.8), kind=kOutput, calls=%fused_computation.6.clone.1 | convolution fusion | flops 264236704 | bytes 14174253 | tf_op jit(solution)/shard_map/while/body/eval_jaxpr/op,pac->oac/dot_general | solution.py:35
  183.7 5.1 %copy_dynamic-update-slice_fusion.2 = bf16[2,9,512,512]{3,2,1,0:T(8,128)(2,1)} fusion(bf16[2,9,512,512]{3,2,1,0:T(8,128)(2,1)} %get-tuple-element.219, s32[]{:T(128)} %get-tuple-element.218, bf16[1,9,512,512]{3,1,2,0:T(8,128)(2,1)S(1)} %bitcast.62), kind=kLoop, calls=%fused_computation.8.clone.1 | loop fusion | bytes 9437696 | tf_op jit(solution)/shard_map/while/body/jit(dynamic_update_index_in_dim)/dynamic_update_slice | solution.py:53
  189.1 1.9 collective-permute-start.2
  191.0 2.4 %collective-permute-start.3 = (f32[2,512]{1,0:T(2,128)S(1)}, f32[2,512]{1,0:T(2,128)S(1)}, u32[]{:S(2)}, u32[]{:S(2)}) collective-permute-start(f32[2,512]{1,0:T(2,128)S(1)} %get-tuple-element.130), channel_id=1, source_target_pairs={{1,0},{2,1},{3,2},{4,3},{5,4},{6,5},{7,6},{8,7},{9,8},{10,9},{11,1... | collective-permute-start | bytes 12296 | tf_op jit(solution)/shard_map/ppermute | solution.py:25
  193.4 2.2 collective-permute-start.4
  195.6 6.7 %collective-permute-start.5 = (f32[2,512]{1,0:T(2,128)S(1)}, f32[2,512]{1,0:T(2,128)S(1)}, u32[]{:S(2)}, u32[]{:S(2)}) collective-permute-start(f32[2,512]{1,0:T(2,128)S(1)} %get-tuple-element.128), channel_id=1, source_target_pairs={{2,0},{3,1},{4,2},{5,3},{6,4},{7,5},{8,6},{9,7},{10,8},{11,9},{12,... | collective-permute-start | bytes 12296 | tf_op jit(solution)/shard_map/ppermute | solution.py:25
  202.4 0.7 collective-permute-done.5
  203.1 1.9 collective-permute-start.6
  205.0 4.5 %collective-permute-start.7 = (f32[2,512]{1,0:T(2,128)S(1)}, f32[2,512]{1,0:T(2,128)S(1)}, u32[]{:S(2)}, u32[]{:S(2)}) collective-permute-start(f32[2,512]{1,0:T(2,128)S(1)} %fusion.21), channel_id=1, source_target_pairs={{0,1},{1,2},{2,3},{3,4},{4,5},{5,6},{6,7},{7,8},{8,9},{9,10},{10,1... | collective-permute-start | bytes 12296 | tf_op jit(solution)/shard_map/ppermute | solution.py:25
  209.5 3.6 %collective-permute-start.8 = (f32[2,512]{1,0:T(2,128)S(1)}, f32[2,512]{1,0:T(2,128)S(1)}, u32[]{:S(2)}, u32[]{:S(2)}) collective-permute-start(f32[2,512]{1,0:T(2,128)S(1)} %fusion.21), channel_id=1, source_target_pairs={{1,0},{2,1},{3,2},{4,3},{5,4},{6,5},{7,6},{8,7},{9,8},{10,9},{11,1... | collective-permute-start | bytes 12296 | tf_op jit(solution)/shard_map/ppermute | solution.py:25
  213.1 7.5 %collective-permute-start.9 = (f32[2,512]{1,0:T(2,128)S(1)}, f32[2,512]{1,0:T(2,128)S(1)}, u32[]{:S(2)}, u32[]{:S(2)}) collective-permute-start(f32[2,512]{1,0:T(2,128)S(1)} %fusion.21), channel_id=1, source_target_pairs={{2,0},{3,1},{4,2},{5,3},{6,4},{7,5},{8,6},{9,7},{10,8},{11,9},{12,... | collective-permute-start | bytes 12296 | tf_op jit(solution)/shard_map/ppermute | solution.py:25
  220.7 0.7 collective-permute-done.9
  222.1 4.7 %broadcast.145 = bf16[2,9,512,512]{3,2,1,0:T(8,128)(2,1)} broadcast(bf16[]{:T(256)} %constant.89.clone.1), dimensions={} | broadcast | bytes 9437186 | tf_op jit(solution)/shard_map/broadcast.29
  226.8 11.8 %while.23 = (s32[]{:T(128)}, bf16[2,9,512,512]{3,2,1,0:T(8,128)(2,1)}, bf16[2,9,512,512]{3,2,1,0:T(8,128)(2,1)}, f32[2,9,512]{2,1,0:T(8,128)S(1)}, s32[]{:T(128)}) while((s32[]{:T(128)}, bf16[2,9,512,512]{3,2,1,0:T(8,128)(2,1)}, bf16[2,9,512,512]{3,2,1,0:T(8,128)(2,1)}, f32[2,9,512]{2,1,0:T(8,128)S(1)}, s32[]{:T(128)}) %tuple.46), condition=%wide.region_5.6_spmd, body=%wide.region_4.5_spmd.sunk | while | flops 11796482 | bytes 9493057 | solution.py:99
  226.8 5.9 %fusion.39 = bf16[2,9,512,512]{3,2,1,0:T(8,128)(2,1)} fusion(bf16[2,9,512,512]{3,2,1,0:T(8,128)(2,1)} %get-tuple-element.242, s32[]{:T(128)} %get-tuple-element.241, f32[9,512]{1,0:T(8,128)S(1)} %dynamic-slice_bitcast_fusion.2, bf16[2,9,512,512]{3,2,1,0:T(8,128)(2,1)} %get-tuple-element.248), kind=kLoop, calls=%fused_computation.4.clone.1 | loop fusion | flops 11796480 | bytes 9456128 | tf_op jit(solution)/shard_map/while/body/jit(dynamic_update_index_in_dim)/dynamic_update_slice | solution.py:53
  232.7 5.9 %fusion.39 = bf16[2,9,512,512]{3,2,1,0:T(8,128)(2,1)} fusion(bf16[2,9,512,512]{3,2,1,0:T(8,128)(2,1)} %get-tuple-element.242, s32[]{:T(128)} %get-tuple-element.241, f32[9,512]{1,0:T(8,128)S(1)} %dynamic-slice_bitcast_fusion.2, bf16[2,9,512,512]{3,2,1,0:T(8,128)(2,1)} %get-tuple-element.248), kind=kLoop, calls=%fused_computation.4.clone.1 | loop fusion | flops 11796480 | bytes 9456128 | tf_op jit(solution)/shard_map/while/body/jit(dynamic_update_index_in_dim)/dynamic_update_slice | solution.py:53
  (57 shorter events, 3.1 us)
Async XLA Ops:
  0.0 65.7 %collective-permute-start = (bf16[2,3,512,512]{3,2,1,0:T(8,128)(2,1)}, bf16[2,3,512,512]{3,2,1,0:T(8,128)(2,1)S(1)}, u32[]{:S(2)}, u32[]{:S(2)}) collective-permute-start(bf16[2,3,512,512]{3,2,1,0:T(8,128)(2,1)} %param.6), channel_id=1, source_target_pairs={{0,1},{1,2},{2,3},{3,4},{4,5},{5,6},{6,7},{7,8},{8,9},{9,10},{10,1... | collective-permute-start | bytes 9437192 | tf_op jit(solution)/shard_map/ppermute | solution.py:14
  3.8 71.5 %collective-permute-start.1 = (bf16[2,3,512,512]{3,2,1,0:T(8,128)(2,1)}, bf16[2,3,512,512]{3,2,1,0:T(8,128)(2,1)}, u32[]{:S(2)}, u32[]{:S(2)}) collective-permute-start(bf16[2,3,512,512]{3,2,1,0:T(8,128)(2,1)} %param.6), channel_id=1, source_target_pairs={{1,0},{2,1},{3,2},{4,3},{5,4},{6,5},{7,6},{8,7},{9,8},{10,9},{11,1... | collective-permute-start | bytes 9437192 | tf_op jit(solution)/shard_map/ppermute | solution.py:17
  83.0 4.6 %copy-start = (bf16[2,3,512,512]{3,2,1,0:T(8,128)(2,1)S(1)}, bf16[2,3,512,512]{3,2,1,0:T(8,128)(2,1)}, u32[]{:S(2)}) copy-start(bf16[2,3,512,512]{3,2,1,0:T(8,128)(2,1)} %param.6) | copy-start | bytes 9437188
  189.1 13.3 %collective-permute-start.2 = (f32[2,512]{1,0:T(2,128)S(1)}, f32[2,512]{1,0:T(2,128)S(1)}, u32[]{:S(2)}, u32[]{:S(2)}) collective-permute-start(f32[2,512]{1,0:T(2,128)S(1)} %get-tuple-element.127), channel_id=1, source_target_pairs={{0,1},{1,2},{2,3},{3,4},{4,5},{5,6},{6,7},{7,8},{8,9},{9,10},{10,1... | collective-permute-start | bytes 12296 | tf_op jit(solution)/shard_map/ppermute | solution.py:25
  191.0 11.3 %collective-permute-start.3 = (f32[2,512]{1,0:T(2,128)S(1)}, f32[2,512]{1,0:T(2,128)S(1)}, u32[]{:S(2)}, u32[]{:S(2)}) collective-permute-start(f32[2,512]{1,0:T(2,128)S(1)} %get-tuple-element.130), channel_id=1, source_target_pairs={{1,0},{2,1},{3,2},{4,3},{5,4},{6,5},{7,6},{8,7},{9,8},{10,9},{11,1... | collective-permute-start | bytes 12296 | tf_op jit(solution)/shard_map/ppermute | solution.py:25
  193.4 8.9 %collective-permute-start.4 = (f32[2,512]{1,0:T(2,128)S(1)}, f32[2,512]{1,0:T(2,128)S(1)}, u32[]{:S(2)}, u32[]{:S(2)}) collective-permute-start(f32[2,512]{1,0:T(2,128)S(1)} %get-tuple-element.129), channel_id=1, source_target_pairs={{0,2},{1,3},{2,4},{3,5},{4,6},{5,7},{6,8},{7,9},{8,10},{9,11},{10,... | collective-permute-start | bytes 12296 | tf_op jit(solution)/shard_map/ppermute | solution.py:25
  195.6 7.4 %collective-permute-start.5 = (f32[2,512]{1,0:T(2,128)S(1)}, f32[2,512]{1,0:T(2,128)S(1)}, u32[]{:S(2)}, u32[]{:S(2)}) collective-permute-start(f32[2,512]{1,0:T(2,128)S(1)} %get-tuple-element.128), channel_id=1, source_target_pairs={{2,0},{3,1},{4,2},{5,3},{6,4},{7,5},{8,6},{9,7},{10,8},{11,9},{12,... | collective-permute-start | bytes 12296 | tf_op jit(solution)/shard_map/ppermute | solution.py:25
  203.1 17.6 %collective-permute-start.6 = (f32[2,512]{1,0:T(2,128)S(1)}, f32[2,512]{1,0:T(2,128)S(1)}, u32[]{:S(2)}, u32[]{:S(2)}) collective-permute-start(f32[2,512]{1,0:T(2,128)S(1)} %fusion.21), channel_id=1, source_target_pairs={{0,2},{1,3},{2,4},{3,5},{4,6},{5,7},{6,8},{7,9},{8,10},{9,11},{10,... | collective-permute-start | bytes 12296 | tf_op jit(solution)/shard_map/ppermute | solution.py:25
  205.0 15.6 %collective-permute-start.7 = (f32[2,512]{1,0:T(2,128)S(1)}, f32[2,512]{1,0:T(2,128)S(1)}, u32[]{:S(2)}, u32[]{:S(2)}) collective-permute-start(f32[2,512]{1,0:T(2,128)S(1)} %fusion.21), channel_id=1, source_target_pairs={{0,1},{1,2},{2,3},{3,4},{4,5},{5,6},{6,7},{7,8},{8,9},{9,10},{10,1... | collective-permute-start | bytes 12296 | tf_op jit(solution)/shard_map/ppermute | solution.py:25
  209.5 11.2 %collective-permute-start.8 = (f32[2,512]{1,0:T(2,128)S(1)}, f32[2,512]{1,0:T(2,128)S(1)}, u32[]{:S(2)}, u32[]{:S(2)}) collective-permute-start(f32[2,512]{1,0:T(2,128)S(1)} %fusion.21), channel_id=1, source_target_pairs={{1,0},{2,1},{3,2},{4,3},{5,4},{6,5},{7,6},{8,7},{9,8},{10,9},{11,1... | collective-permute-start | bytes 12296 | tf_op jit(solution)/shard_map/ppermute | solution.py:25
  213.1 8.2 %collective-permute-start.9 = (f32[2,512]{1,0:T(2,128)S(1)}, f32[2,512]{1,0:T(2,128)S(1)}, u32[]{:S(2)}, u32[]{:S(2)}) collective-permute-start(f32[2,512]{1,0:T(2,128)S(1)} %fusion.21), channel_id=1, source_target_pairs={{2,0},{3,1},{4,2},{5,3},{6,4},{7,5},{8,6},{9,7},{10,8},{11,9},{12,... | collective-permute-start | bytes 12296 | tf_op jit(solution)/shard_map/ppermute | solution.py:25
where the time goes:
time: 243 us; the launch traced here: 239 us
  local copies, waits for them, and re-layouts  69.5 us (29%)
  waiting for transfers between devices  69 us (28%)
  matrix products  43.4 us (18%)
  starting transfers between devices  36.4 us (15%)
  other arithmetic  20.1 us (8%)
    ppermute x1, waiting for transfers between devices, extended(): lax.ppermute(lax.slice_in_dim(block, block.shape[dim] - width, None, axis...  57.9 us
    reshape x2, local copies, waits for them, and re-layouts, one_row(): products.reshape(slot_count, products.shape[2], products.shape[3])  33.4 us
    ppermute x8, starting transfers between devices, shifted(): return lax.ppermute(block, axis, route)  30.7 us
    dot_general x2, matrix products, merge_slots(): jnp.einsum('op,pac->oac', weight, products, precision=lax.Precision.HIGHEST)  26.4 us
    dot_general x2, matrix products, one_row(): jnp.einsum('sab,stbc->stac', tile_row, fetched, preferred_element_type=jn...  16.7 us
    gather x2, local copies, waits for them, and re-layouts, one_row(): fetched = jnp.take(widened, targets - diagonal_gap, axis=0)  13.6 us
    dynamic_update_slice x2, other arithmetic, expand_rows(): return lax.map(one_row, (matrix_tiles, row_cols, out_cols))  11.8 us
    dynamic_update_slice x4, local copies, waits for them, and re-layouts, expand_rows(): return lax.map(one_row, (matrix_tiles, row_cols, out_cols))  10.2 us
  transfers between devices with their start and end apart: 10, of which 4 were waited for; matrix products, arithmetic and copies ran while one was open for 1% of the time, Pallas kernels for 0%

commit v1 on v0

v1 whole, which is shorter than its diff:
```python
import functools

import jax
import jax.numpy as jnp
from jax import lax
from jax.experimental import pallas as pl
from jax.experimental.pallas import tpu as pltpu
from jax.sharding import PartitionSpec as P

W = 2
AXES = ("row", "col", "depth")
CHUNKS = 4
FIELDS = 24


def both_ways(pairs):
    return pairs + [(b, a) for a, b in pairs]


def plan(pattern, start, rows_here, core):
    row_cols = lax.dynamic_slice_in_dim(pattern, start, rows_here, 0)
    slots = pattern.shape[1]
    out_cols = jnp.take(pattern, row_cols, axis=0).reshape(rows_here, slots * slots)
    offset = row_cols - start
    inside = (offset >= 0) & (offset < rows_here)
    above = offset >= rows_here
    beside = jnp.where(core == 0, above, offset < 0)
    source = jnp.where(inside, 0, jnp.where(beside, 1, 2))
    line = jnp.where(inside, offset, jnp.where(above, offset - rows_here, offset + rows_here))
    positions = jnp.arange(slots * slots, dtype=jnp.int32)
    matched = out_cols[:, :, None] == out_cols[:, None, :]
    lead = jnp.min(jnp.where(matched, positions[None, None, :], slots * slots), axis=2)
    window = out_cols - (start - core * rows_here - 2 * W)
    return jnp.concatenate([source, line, lead, window], axis=1).astype(jnp.int32).reshape(-1)


def expand_kernel(q, rows_here, slots, meta, own, beside, across, before, out, win, acc, right):
    del before
    width = across.shape[3]
    cols = slice(q * width, (q + 1) * width)
    win[...] = jnp.zeros_like(win)
    for r in range(rows_here):
        base = r * FIELDS
        for s in range(slots):
            if s == 0:
                for t in range(slots):
                    right[:, t * width : (t + 1) * width] = own[r, t, :, cols]
            else:
                source = meta[base + s]
                line = meta[base + slots + s]

                @pl.when(source == 0)
                def _():
                    for t in range(slots):
                        right[:, t * width : (t + 1) * width] = own[line, t, :, cols]

                @pl.when(source == 1)
                def _():
                    for t in range(slots):
                        right[:, t * width : (t + 1) * width] = beside[line, t, :, cols]

                @pl.when(source == 2)
                def _():
                    for t in range(slots):
                        right[:, t * width : (t + 1) * width] = across[line, t]

            product = jnp.dot(own[r, s], right[...], preferred_element_type=jnp.float32)
            for t in range(slots):
                part = product[:, t * width : (t + 1) * width]
                slot = s * slots + t
                if s == 0:
                    acc[slot] = part
                else:
                    lead = meta[base + 2 * slots + slot]

                    @pl.when(lead == slot)
                    def _():
                        acc[slot] = part

                    @pl.when(lead != slot)
                    def _():
                        acc[lead] += part
                        acc[slot] = jnp.zeros_like(part)

        for slot in range(slots * slots):
            values = acc[slot].astype(jnp.bfloat16)
            out[r, slot] = values
            wide = values.astype(jnp.float32)
            place = meta[base + 2 * slots + slots * slots + slot]
            win[pl.ds(place, 1), :] += jnp.sum(wide * wide, axis=0, keepdims=True)


def expand(q, meta, own, beside, across, before):
    rows_here, slots, side, width = across.shape
    vmem = pl.BlockSpec(memory_space=pltpu.VMEM)
    return pl.pallas_call(
        functools.partial(expand_kernel, q, rows_here, slots),
        in_specs=[pl.BlockSpec(memory_space=pltpu.SMEM), vmem, vmem, vmem, pl.BlockSpec(memory_space=pl.ANY)],
        out_specs=[vmem, vmem],
        out_shape=[
            jax.ShapeDtypeStruct((rows_here, slots * slots, side, width), jnp.bfloat16),
            jax.ShapeDtypeStruct((16, width), jnp.float32),
        ],
        scratch_shapes=[
            pltpu.VMEM((slots * slots, side, width), jnp.float32),
            pltpu.VMEM((side, slots * width), jnp.bfloat16),
        ],
        compiler_params=pltpu.CompilerParams(vmem_limit_bytes=24 * 2**20),
        cost_estimate=pl.CostEstimate(
            flops=2 * rows_here * slots * slots * side * side * width,
            bytes_accessed=12 * 2**20,
            transcendentals=0,
        ),
        name=f"expand{q}",
    )(meta, own, beside, across, before)


def inflate_kernel(scale, slots, group, meta, totals, *refs):
    parts, out = refs[:-1], refs[-1]
    width = parts[0].shape[3]
    r = pl.program_id(0)
    g = pl.program_id(1)
    for o in range(group):
        slot = g * group + o
        place = meta[r * FIELDS + 2 * slots + slots * slots + slot]
        factor = scale / totals[pl.ds(place, 1), :]
        for q, part in enumerate(parts):
            wide = part[r, slot].astype(jnp.float32)
            cols = slice(q * width, (q + 1) * width)
            out[0, o, :, cols] = (wide * wide * factor[:, cols]).astype(jnp.bfloat16)


def inflate(scale, slots, meta, totals, parts):
    rows_here, slot_total, side, width = parts[0].shape
    group = 3
    vmem = pl.BlockSpec(memory_space=pltpu.VMEM)
    return pl.pallas_call(
        functools.partial(inflate_kernel, scale, slots, group),
        grid=(rows_here, slot_total // group),
        in_specs=[pl.BlockSpec(memory_space=pltpu.SMEM), vmem] + [vmem] * len(parts),
        out_specs=pl.BlockSpec((1, group, side, width * len(parts)), lambda r, g: (r, g, 0, 0)),
        out_shape=jax.ShapeDtypeStruct((rows_here, slot_total, side, width * len(parts)), jnp.bfloat16),
        compiler_params=pltpu.CompilerParams(vmem_limit_bytes=24 * 2**20),
        cost_estimate=pl.CostEstimate(flops=2**24, bytes_accessed=18 * 2**20, transcendentals=0),
        name="inflate",
    )(meta, totals, *parts)


def shift_lines(block, distance):
    lines = block.shape[0]
    pad = jnp.zeros((abs(distance), block.shape[1]), block.dtype)
    if distance > 0:
        return jnp.concatenate([pad, block[: lines - distance]], axis=0)
    return jnp.concatenate([block[-distance:], pad], axis=0)


def body(matrix_tiles, pattern):
    rows_here, slots, side, _ = matrix_tiles.shape
    scale = float(slots * slots * side)
    devices = lax.axis_size(AXES)
    assert rows_here == W and lax.axis_size("depth") == 2
    core = lax.axis_index("depth")
    start = lax.axis_index(AXES) * rows_here
    chips = devices // 2
    swap = both_ways([(2 * c, 2 * c + 1) for c in range(chips)])
    next_chip = both_ways([(2 * c + 1, 2 * c + 2) for c in range(chips - 1)])
    second_chip = both_ways([(2 * c + 1, 2 * c + 4) for c in range(chips - 2)])

    width = side // CHUNKS
    across = [
        lax.ppermute(matrix_tiles[..., q * width : (q + 1) * width], AXES, next_chip)
        for q in range(CHUNKS)
    ]
    beside = lax.ppermute(matrix_tiles, AXES, swap)
    meta = plan(pattern, start, rows_here, core)
    parts, windows = [], []
    for q in range(CHUNKS):
        before = windows[-1] if windows else meta
        part, window = expand(q, meta, matrix_tiles, beside, across[q], before)
        parts.append(part)
        windows.append(window)
    window = jnp.concatenate(windows, axis=1)

    chip_rows = 2 * rows_here
    used = chip_rows + 4 * W
    window = window[:used]
    chip = window + lax.ppermute(window, AXES, swap)
    first = lax.ppermute(chip, AXES, next_chip)
    second = lax.ppermute(chip, AXES, second_chip)
    gathered = jnp.where(
        core == 0,
        shift_lines(first, -chip_rows) + shift_lines(second, -2 * chip_rows),
        shift_lines(first, chip_rows) + shift_lines(second, 2 * chip_rows),
    )
    totals = chip + gathered + lax.ppermute(gathered, AXES, swap)
    return inflate(scale, slots, meta, totals, parts)


def solution(mesh):
    return jax.shard_map(
        body,
        mesh=mesh,
        in_specs=(P(AXES, None, None, None), P()),
        out_specs=P(AXES, None, None, None),
        check_vma=False,
    )
```

time: 243 us -> 106 us (0.44); the launches traced: 239 us -> 105 us
  local copies, waits for them, and re-layouts: 69.5 us -> 5.11 us
  matrix products: 43.4 us -> 0 us
  Pallas kernels: 0 us -> 30.3 us
  waiting for transfers between devices: 69 us -> 42.9 us
  other arithmetic: 20.1 us -> 0.47 us
  starting transfers between devices: 36.4 us -> 26.5 us
    dot_general x5 -> x0, matrix products: 43.4 us -> none  [the longest x2 26.4 us: merge_slots(): jnp.einsum('op,pac->oac', weight, products, precision=lax.Precision.HIGHEST)]
    reshape x4 -> x1, local copies, waits for them, and re-layouts: 33.4 us -> 0.08 us  [plan(): jnp.concatenate([source, line, lead, window], axis=1).astype(jnp.int32)]
    pallas_call x0 -> x5, Pallas kernels: none -> 30.3 us  [the longest x4 24.5 us: expand(): pl.pallas_call(functools.partial(expand_kernel, q, rows_here, slots), in_...]
    ppermute x10 -> x9, waiting for transfers between devices: 69 us -> 42.9 us  [the longest x4 39.4 us: body(): lax.ppermute(matrix_tiles[..., q * width:(q + 1) * width], AXES, next_chip)]
    gather x7 -> x3, local copies, waits for them, and re-layouts: 15 us -> 0.73 us  [plan(): jnp.take(pattern, row_cols, axis=0).reshape(rows_here, slots * slots)]
    dynamic_update_slice x2 -> x0, other arithmetic: 11.8 us -> none  [expand_rows(): return lax.map(one_row, (matrix_tiles, row_cols, out_cols))]
    dynamic_update_slice x4 -> x0, local copies, waits for them, and re-layouts: 10.2 us -> none  [expand_rows(): return lax.map(one_row, (matrix_tiles, row_cols, out_cols))]
    ppermute x10 -> x9, starting transfers between devices: 36.4 us -> 26.5 us  [the longest x4 11.1 us: body(): lax.ppermute(matrix_tiles[..., q * width:(q + 1) * width], AXES, next_chip)]
  transfers between devices with their start and end apart: 10 -> 9, of which waited for: 4 -> 7; matrix products, arithmetic and copies ran while one was open for 1% -> 5% of each run, Pallas kernels for 0% -> 17%
where the time goes in v1:
time: 106 us; the launch traced here: 105 us
  waiting for transfers between devices  42.9 us (40%)
  Pallas kernels  30.3 us (29%)
  starting transfers between devices  26.5 us (25%)
  local copies, waits for them, and re-layouts  5.11 us (5%)
    ppermute x4, waiting for transfers between devices, body(): lax.ppermute(matrix_tiles[..., q * width:(q + 1) * width], AXES, next_chip)  39.4 us
    pallas_call x4, Pallas kernels, expand(): pl.pallas_call(functools.partial(expand_kernel, q, rows_here, slots), in_...  24.5 us
    ppermute x4, starting transfers between devices, body(): lax.ppermute(matrix_tiles[..., q * width:(q + 1) * width], AXES, next_chip)  11.1 us
    pallas_call x1, Pallas kernels, inflate(): pl.pallas_call(functools.partial(inflate_kernel, scale, slots, group), gr...  5.78 us
    ppermute x1, starting transfers between devices, body(): chip = window + lax.ppermute(window, AXES, swap)  5.43 us
    slice x1, local copies, waits for them, and re-layouts, body(): matrix_tiles[..., q * width:(q + 1) * width]  3.73 us
    ppermute x1, starting transfers between devices, body(): totals = chip + gathered + lax.ppermute(gathered, AXES, swap)  3.71 us
    ppermute x1, starting transfers between devices, body(): first = lax.ppermute(chip, AXES, next_chip)  3.65 us
  transfers between devices with their start and end apart: 9, of which 7 were waited for; matrix products, arithmetic and copies ran while one was open for 5% of the time, Pallas kernels for 17%

profile of v1, /device:TPU:5, one launch (start us, length us, event | category | flops | bytes accessed | tf_op | source)
XLA Modules:
  0.0 105.4 jit_solution(16764230755752771289)
XLA Ops:
  0.0 0.7 collective-permute-start
  0.7 3.7 %fusion.3 = (bf16[2,3,512,128]{3,2,1,0:T(8,128)(2,1)}, bf16[2,3,512,128]{3,2,1,0:T(8,128)(2,1)}, bf16[2,3,512,128]{3,2,1,0:T(8,128)(2,1)}, bf16[2,3,512,128]{3,2,1,0:T(8,128)(2,1)}) fusion(bf16[2,3,512,512]{3,2,1,0:T(8,128)(2,1)} %own.7), kind=kLoop, calls=%fused_computation.21 | loop fusion | bytes 6291456 | tf_op jit(solution)/shard_map/slice | solution.py:171
  4.4 3.1 %collective-permute-start.1 = (bf16[2,3,512,128]{3,2,1,0:T(8,128)(2,1)}, bf16[2,3,512,128]{3,2,1,0:T(8,128)(2,1)}, u32[]{:S(2)}, u32[]{:S(2)}) collective-permute-start(bf16[2,3,512,128]{3,2,1,0:T(8,128)(2,1)} %get-tuple-element.23), channel_id=1, source_target_pairs={{1,2},{3,4},{5,6},{7,8},{9,10},{11,12},{13,14},{15,16},{17,18},{19... | collective-permute-start | bytes 2359304 | tf_op jit(solution)/shard_map/ppermute | solution.py:171
  7.6 2.4 %collective-permute-start.3 = (bf16[2,3,512,128]{3,2,1,0:T(8,128)(2,1)}, bf16[2,3,512,128]{3,2,1,0:T(8,128)(2,1)}, u32[]{:S(2)}, u32[]{:S(2)}) collective-permute-start(bf16[2,3,512,128]{3,2,1,0:T(8,128)(2,1)} %get-tuple-element.24), channel_id=1, source_target_pairs={{1,2},{3,4},{5,6},{7,8},{9,10},{11,12},{13,14},{15,16},{17,18},{19... | collective-permute-start | bytes 2359304 | tf_op jit(solution)/shard_map/ppermute | solution.py:171
  10.0 3.1 %collective-permute-start.2 = (bf16[2,3,512,128]{3,2,1,0:T(8,128)(2,1)}, bf16[2,3,512,128]{3,2,1,0:T(8,128)(2,1)}, u32[]{:S(2)}, u32[]{:S(2)}) collective-permute-start(bf16[2,3,512,128]{3,2,1,0:T(8,128)(2,1)} %get-tuple-element.25), channel_id=1, source_target_pairs={{1,2},{3,4},{5,6},{7,8},{9,10},{11,12},{13,14},{15,16},{17,18},{19... | collective-permute-start | bytes 2359304 | tf_op jit(solution)/shard_map/ppermute | solution.py:171
  13.1 2.4 %collective-permute-start.4 = (bf16[2,3,512,128]{3,2,1,0:T(8,128)(2,1)}, bf16[2,3,512,128]{3,2,1,0:T(8,128)(2,1)}, u32[]{:S(2)}, u32[]{:S(2)}) collective-permute-start(bf16[2,3,512,128]{3,2,1,0:T(8,128)(2,1)} %get-tuple-element.26), channel_id=1, source_target_pairs={{1,2},{3,4},{5,6},{7,8},{9,10},{11,12},{13,14},{15,16},{17,18},{19... | collective-permute-start | bytes 2359304 | tf_op jit(solution)/shard_map/ppermute | solution.py:171
  15.6 0.1 copy.19
  15.8 0.6 gather_fusion
  16.3 0.1 copy.21
  16.4 0.1 reshape.37
  16.5 0.1 copy.22
  16.6 0.1 select_n.67
  16.7 0.1 copy.23
  16.8 0.3 fusion
  17.1 0.1 copy.24
  17.3 0.1 reshape.35.meta.before
  17.4 7.2 %collective-permute-done.1.across = bf16[2,3,512,128]{3,2,1,0:T(8,128)(2,1)} collective-permute-done((bf16[2,3,512,128]{3,2,1,0:T(8,128)(2,1)}, bf16[2,3,512,128]{3,2,1,0:T(8,128)(2,1)}, u32[]{:S(2)}, u32[]{:S(2)}) %collective-permute-start.1) | collective-permute-done | bytes 786464 | tf_op jit(solution)/shard_map/ppermute | solution.py:171
  24.6 6.1 %expand0.1 = (bf16[2,9,512,128]{3,2,1,0:T(8,128)(2,1)S(1)}, f32[16,128]{1,0:T(8,128)S(1)}) custom-call(s32[48]{0:T(128)S(1)} %reshape.35.meta.before, bf16[2,3,512,512]{3,2,1,0:T(8,128)(2,1)S(1)} %copy-done, bf16[2,3,512,512]{3,2,1,0:T(8,128)(2,1)} %collective-permute-done.beside, bf16[2,3,512,128]{3,2,1,0:T(8,128)(2,1)} %collective-permute-done.1.across, ...), custom_call_target="tpu_custom_call" | custom-call | flops 1207959552 | bytes 12582912 | tf_op jit(solution)/shard_map/expand0/pallas_call | solution.py:96
  30.7 27.6 %collective-permute-done.2.across = bf16[2,3,512,128]{3,2,1,0:T(8,128)(2,1)} collective-permute-done((bf16[2,3,512,128]{3,2,1,0:T(8,128)(2,1)}, bf16[2,3,512,128]{3,2,1,0:T(8,128)(2,1)}, u32[]{:S(2)}, u32[]{:S(2)}) %collective-permute-start.2) | collective-permute-done | bytes 786464 | tf_op jit(solution)/shard_map/ppermute | solution.py:171
  58.3 6.1 %expand1.1 = (bf16[2,9,512,128]{3,2,1,0:T(8,128)(2,1)S(1)}, f32[16,128]{1,0:T(8,128)S(1)}) custom-call(s32[48]{0:T(128)S(1)} %reshape.35.meta.before, bf16[2,3,512,512]{3,2,1,0:T(8,128)(2,1)S(1)} %copy-done, bf16[2,3,512,512]{3,2,1,0:T(8,128)(2,1)} %collective-permute-done.beside, bf16[2,3,512,128]{3,2,1,0:T(8,128)(2,1)} %collective-permute-done.2.across, ...), custom_call_target="tpu_custom_call" | custom-call | flops 1207959552 | bytes 12582912 | tf_op jit(solution)/shard_map/expand1/pallas_call | solution.py:96
  64.4 6.3 %expand2.1 = (bf16[2,9,512,128]{3,2,1,0:T(8,128)(2,1)S(1)}, f32[16,128]{1,0:T(8,128)S(1)}) custom-call(s32[48]{0:T(128)S(1)} %reshape.35.meta.before, bf16[2,3,512,512]{3,2,1,0:T(8,128)(2,1)S(1)} %copy-done, bf16[2,3,512,512]{3,2,1,0:T(8,128)(2,1)} %collective-permute-done.beside, bf16[2,3,512,128]{3,2,1,0:T(8,128)(2,1)} %collective-permute-done.3.across, ...), custom_call_target="tpu_custom_call" | custom-call | flops 1207959552 | bytes 12582912 | tf_op jit(solution)/shard_map/expand2/pallas_call | solution.py:96
  70.7 4.5 %collective-permute-done.4.across = bf16[2,3,512,128]{3,2,1,0:T(8,128)(2,1)} collective-permute-done((bf16[2,3,512,128]{3,2,1,0:T(8,128)(2,1)}, bf16[2,3,512,128]{3,2,1,0:T(8,128)(2,1)}, u32[]{:S(2)}, u32[]{:S(2)}) %collective-permute-start.4) | collective-permute-done | bytes 786464 | tf_op jit(solution)/shard_map/ppermute | solution.py:171
  75.2 6.1 %expand3.1 = (bf16[2,9,512,128]{3,2,1,0:T(8,128)(2,1)S(1)}, f32[16,128]{1,0:T(8,128)S(1)}) custom-call(s32[48]{0:T(128)S(1)} %reshape.35.meta.before, bf16[2,3,512,512]{3,2,1,0:T(8,128)(2,1)S(1)} %copy-done, bf16[2,3,512,512]{3,2,1,0:T(8,128)(2,1)} %collective-permute-done.beside, bf16[2,3,512,128]{3,2,1,0:T(8,128)(2,1)} %collective-permute-done.4.across, ...), custom_call_target="tpu_custom_call" | custom-call | flops 1207959552 | bytes 12582912 | tf_op jit(solution)/shard_map/expand3/pallas_call | solution.py:96
  81.3 5.4 %collective-permute-start.5 = (f32[12,512]{1,0:T(8,128)S(1)}, f32[12,512]{1,0:T(8,128)S(1)}, u32[]{:S(2)}, u32[]{:S(2)}) collective-permute-start(f32[12,512]{1,0:T(8,128)S(1)} %pad_maximum_fusion), channel_id=1, source_target_pairs={{0,1},{2,3},{4,5},{6,7},{8,9},{10,11},{12,13},{14,15},{16,17},{18,... | collective-permute-start | bytes 73736 | tf_op jit(solution)/shard_map/ppermute | solution.py:187
  86.7 0.9 collective-permute-done.5
  87.6 1.9 %collective-permute-start.7 = (f32[12,512]{1,0:T(8,128)S(1)}, f32[12,512]{1,0:T(8,128)S(1)}, u32[]{:S(2)}, u32[]{:S(2)}) collective-permute-start(f32[12,512]{1,0:T(8,128)S(1)} %fusion.2), channel_id=1, source_target_pairs={{1,4},{3,6},{5,8},{7,10},{9,12},{11,14},{13,16},{15,18},{17,20},{1... | collective-permute-start | bytes 73736 | tf_op jit(solution)/shard_map/ppermute | solution.py:189
  89.5 3.7 %collective-permute-start.6 = (f32[12,512]{1,0:T(8,128)S(1)}, f32[12,512]{1,0:T(8,128)S(1)}, u32[]{:S(2)}, u32[]{:S(2)}) collective-permute-start(f32[12,512]{1,0:T(8,128)S(1)} %fusion.2), channel_id=1, source_target_pairs={{1,2},{3,4},{5,6},{7,8},{9,10},{11,12},{13,14},{15,16},{17,18},{19... | collective-permute-start | bytes 73736 | tf_op jit(solution)/shard_map/ppermute | solution.py:188
  93.2 0.6 collective-permute-done.7
  93.8 1.3 %collective-permute-done.6 = f32[12,512]{1,0:T(8,128)S(1)} collective-permute-done((f32[12,512]{1,0:T(8,128)S(1)}, f32[12,512]{1,0:T(8,128)S(1)}, u32[]{:S(2)}, u32[]{:S(2)}) %collective-permute-start.6) | collective-permute-done | bytes 24608 | tf_op jit(solution)/shard_map/ppermute | solution.py:188
  95.1 3.7 %collective-permute-start.8 = (f32[12,512]{1,0:T(8,128)S(1)}, f32[12,512]{1,0:T(8,128)S(1)}, u32[]{:S(2)}, u32[]{:S(2)}) collective-permute-start(f32[12,512]{1,0:T(8,128)S(1)} %add_select_fusion), channel_id=1, source_target_pairs={{0,1},{2,3},{4,5},{6,7},{8,9},{10,11},{12,13},{14,15},{16,17},{18,... | collective-permute-start | bytes 73736 | tf_op jit(solution)/shard_map/ppermute | solution.py:195
  98.8 0.9 collective-permute-done.8
  99.6 5.8 %inflate.1 = bf16[2,9,512,512]{3,2,1,0:T(8,128)(2,1)} custom-call(s32[48]{0:T(128)S(1)} %reshape.35.meta.before, f32[12,512]{1,0:T(8,128)S(1)} %add_add_fusion.totals, bf16[2,9,512,128]{3,2,1,0:T(8,128)(2,1)S(1)} %get-tuple-element.17.refs_0_, bf16[2,9,512,128]{3,2,1,0:T(8,128)(2,1)S(1)} %get-tuple-element.18.refs_1_, ...), custom_call_target="tpu_custom_call" | custom-call | flops 16777216 | bytes 18874368 | tf_op jit(solution)/shard_map/inflate/pallas_call | solution.py:137
  (19 shorter events, 0.3 us)
Async XLA Ops:
  0.0 24.6 %copy-start = (bf16[2,3,512,512]{3,2,1,0:T(8,128)(2,1)S(1)}, bf16[2,3,512,512]{3,2,1,0:T(8,128)(2,1)}, u32[]{:S(2)}) copy-start(bf16[2,3,512,512]{3,2,1,0:T(8,128)(2,1)} %own.7) | copy-start | bytes 9437188
  0.0 15.6 %copy-start.1 = (s32[64,3]{0,1:T(4,128)S(1)}, s32[64,3]{0,1:T(4,128)}, u32[]{:S(2)}) copy-start(s32[64,3]{0,1:T(4,128)} %param.3) | copy-start | bytes 2308
  0.0 24.6 %collective-permute-start = (bf16[2,3,512,512]{3,2,1,0:T(8,128)(2,1)}, bf16[2,3,512,512]{3,2,1,0:T(8,128)(2,1)}, u32[]{:S(2)}, u32[]{:S(2)}) collective-permute-start(bf16[2,3,512,512]{3,2,1,0:T(8,128)(2,1)} %own.7), channel_id=1, source_target_pairs={{0,1},{2,3},{4,5},{6,7},{8,9},{10,11},{12,13},{14,15},{16,17},{18,... | collective-permute-start | bytes 9437192 | tf_op jit(solution)/shard_map/ppermute | solution.py:174
  4.4 20.2 %collective-permute-start.1 = (bf16[2,3,512,128]{3,2,1,0:T(8,128)(2,1)}, bf16[2,3,512,128]{3,2,1,0:T(8,128)(2,1)}, u32[]{:S(2)}, u32[]{:S(2)}) collective-permute-start(bf16[2,3,512,128]{3,2,1,0:T(8,128)(2,1)} %get-tuple-element.23), channel_id=1, source_target_pairs={{1,2},{3,4},{5,6},{7,8},{9,10},{11,12},{13,14},{15,16},{17,18},{19... | collective-permute-start | bytes 2359304 | tf_op jit(solution)/shard_map/ppermute | solution.py:171
  7.6 56.9 %collective-permute-start.3 = (bf16[2,3,512,128]{3,2,1,0:T(8,128)(2,1)}, bf16[2,3,512,128]{3,2,1,0:T(8,128)(2,1)}, u32[]{:S(2)}, u32[]{:S(2)}) collective-permute-start(bf16[2,3,512,128]{3,2,1,0:T(8,128)(2,1)} %get-tuple-element.24), channel_id=1, source_target_pairs={{1,2},{3,4},{5,6},{7,8},{9,10},{11,12},{13,14},{15,16},{17,18},{19... | collective-permute-start | bytes 2359304 | tf_op jit(solution)/shard_map/ppermute | solution.py:171
  10.0 48.4 %collective-permute-start.2 = (bf16[2,3,512,128]{3,2,1,0:T(8,128)(2,1)}, bf16[2,3,512,128]{3,2,1,0:T(8,128)(2,1)}, u32[]{:S(2)}, u32[]{:S(2)}) collective-permute-start(bf16[2,3,512,128]{3,2,1,0:T(8,128)(2,1)} %get-tuple-element.25), channel_id=1, source_target_pairs={{1,2},{3,4},{5,6},{7,8},{9,10},{11,12},{13,14},{15,16},{17,18},{19... | collective-permute-start | bytes 2359304 | tf_op jit(solution)/shard_map/ppermute | solution.py:171
  13.1 62.1 %collective-permute-start.4 = (bf16[2,3,512,128]{3,2,1,0:T(8,128)(2,1)}, bf16[2,3,512,128]{3,2,1,0:T(8,128)(2,1)}, u32[]{:S(2)}, u32[]{:S(2)}) collective-permute-start(bf16[2,3,512,128]{3,2,1,0:T(8,128)(2,1)} %get-tuple-element.26), channel_id=1, source_target_pairs={{1,2},{3,4},{5,6},{7,8},{9,10},{11,12},{13,14},{15,16},{17,18},{19... | collective-permute-start | bytes 2359304 | tf_op jit(solution)/shard_map/ppermute | solution.py:171
  81.3 6.3 %collective-permute-start.5 = (f32[12,512]{1,0:T(8,128)S(1)}, f32[12,512]{1,0:T(8,128)S(1)}, u32[]{:S(2)}, u32[]{:S(2)}) collective-permute-start(f32[12,512]{1,0:T(8,128)S(1)} %pad_maximum_fusion), channel_id=1, source_target_pairs={{0,1},{2,3},{4,5},{6,7},{8,9},{10,11},{12,13},{14,15},{16,17},{18,... | collective-permute-start | bytes 73736 | tf_op jit(solution)/shard_map/ppermute | solution.py:187
  87.6 6.2 %collective-permute-start.7 = (f32[12,512]{1,0:T(8,128)S(1)}, f32[12,512]{1,0:T(8,128)S(1)}, u32[]{:S(2)}, u32[]{:S(2)}) collective-permute-start(f32[12,512]{1,0:T(8,128)S(1)} %fusion.2), channel_id=1, source_target_pairs={{1,4},{3,6},{5,8},{7,10},{9,12},{11,14},{13,16},{15,18},{17,20},{1... | collective-permute-start | bytes 73736 | tf_op jit(solution)/shard_map/ppermute | solution.py:189
  89.5 5.5 %collective-permute-start.6 = (f32[12,512]{1,0:T(8,128)S(1)}, f32[12,512]{1,0:T(8,128)S(1)}, u32[]{:S(2)}, u32[]{:S(2)}) collective-permute-start(f32[12,512]{1,0:T(8,128)S(1)} %fusion.2), channel_id=1, source_target_pairs={{1,2},{3,4},{5,6},{7,8},{9,10},{11,12},{13,14},{15,16},{17,18},{19... | collective-permute-start | bytes 73736 | tf_op jit(solution)/shard_map/ppermute | solution.py:188
  95.1 4.6 %collective-permute-start.8 = (f32[12,512]{1,0:T(8,128)S(1)}, f32[12,512]{1,0:T(8,128)S(1)}, u32[]{:S(2)}, u32[]{:S(2)}) collective-permute-start(f32[12,512]{1,0:T(8,128)S(1)} %add_select_fusion), channel_id=1, source_target_pairs={{0,1},{2,3},{4,5},{6,7},{8,9},{10,11},{12,13},{14,15},{16,17},{18,... | collective-permute-start | bytes 73736 | tf_op jit(solution)/shard_map/ppermute | solution.py:195

commit v2 on v1

--- a/solution.py
+++ b/solution.py
@@ -17,7 +17,7 @@
     return pairs + [(b, a) for a, b in pairs]
 
 
-def plan(pattern, start, rows_here, core):
+def plan(pattern, start, rows_here, core, kind):
     row_cols = lax.dynamic_slice_in_dim(pattern, start, rows_here, 0)
     slots = pattern.shape[1]
     out_cols = jnp.take(pattern, row_cols, axis=0).reshape(rows_here, slots * slots)
@@ -31,79 +31,111 @@
     matched = out_cols[:, :, None] == out_cols[:, None, :]
     lead = jnp.min(jnp.where(matched, positions[None, None, :], slots * slots), axis=2)
     window = out_cols - (start - core * rows_here - 2 * W)
-    return jnp.concatenate([source, line, lead, window], axis=1).astype(jnp.int32).reshape(-1)
-
-
-def expand_kernel(q, rows_here, slots, meta, own, beside, across, before, out, win, acc, right):
-    del before
-    width = across.shape[3]
-    cols = slice(q * width, (q + 1) * width)
+    scalars = jnp.concatenate([source, line, lead, window], axis=1).astype(jnp.int32).reshape(-1)
+    return jnp.concatenate([scalars, kind.astype(jnp.int32)[None]])
+
+
+def detours(last_row, columns):
+    def device(row, col, core):
+        return (row * columns + col) * 2 + core
+
+    top = columns - 1
+    spare_up, spare_down = [device(0, 0, 0), device(0, 0, 1)], [device(last_row, top, 1), device(last_row, top, 0)]
+    first, second, kinds = [], [], {}
+    legs = [(first, []), (second, [])]
+    for row in range(last_row):
+        low, high = device(row, top, 1), device(row + 1, 0, 0)
+        for source, target, spare, turn in ((high, low, spare_up, row), (low, high, spare_down, last_row - 1 - row)):
+            which = turn // 2
+            stop = spare[turn % 2]
+            legs[which][0].append((source, stop))
+            legs[which][1].append((stop, target))
+            kinds[target] = which + 1
+    return legs, kinds
+
+
+def expand_kernel(q, rows_here, slots, meta, own, *refs):
+    out, win, acc, right, sems = refs[-5:]
+    beside, across = refs[0], refs[1:-6]
+    width = out.shape[3]
+    cols = pl.ds(q * width, width)
+
+    def fetch(r, s):
+        source, line = meta[r * FIELDS + s], meta[r * FIELDS + slots + s]
+        if len(across) > 1:
+            source = jnp.where(source == 2, 2 + meta[rows_here * FIELDS], source)
+        job = r * (slots - 1) + s - 1
+        places = [own.at[line, :, :, cols], beside.at[line, :, :, cols]] + [part.at[line] for part in across]
+        for number, place in enumerate(places):
+
+            @pl.when(source == number)
+            def _():
+                pltpu.make_async_copy(place, right.at[job], sems.at[job]).start()
+
+    for r in range(rows_here):
+        for s in range(1, slots):
+            fetch(r, s)
     win[...] = jnp.zeros_like(win)
+
+    def product(r, s, tiles):
+        return jnp.dot(own[r, s], jnp.concatenate(tiles, axis=1), preferred_element_type=jnp.float32)
+
+    def finish(r, slot, total):
+        values = total.astype(jnp.bfloat16)
+        out[r, slot] = values
+        wide = values.astype(jnp.float32)
+        place = meta[r * FIELDS + 2 * slots + slots * slots + slot]
+        win[pl.ds(place, 1), :] += jnp.sum(wide * wide, axis=0, keepdims=True)
+
     for r in range(rows_here):
-        base = r * FIELDS
-        for s in range(slots):
-            if s == 0:
-                for t in range(slots):
-                    right[:, t * width : (t + 1) * width] = own[r, t, :, cols]
-            else:
-                source = meta[base + s]
-                line = meta[base + slots + s]
-
-                @pl.when(source == 0)
+        first = product(r, 0, [own[r, t, :, cols] for t in range(slots)])
+        for t in range(slots):
+            acc[r, t] = first[:, t * width : (t + 1) * width]
+    for r in range(rows_here):
+        for s in range(1, slots):
+            job = r * (slots - 1) + s - 1
+            pltpu.make_async_copy(across[0].at[0], right.at[job], sems.at[job]).wait()
+            later = product(r, s, [right[job, t] for t in range(slots)])
+            for t in range(slots):
+                part = later[:, t * width : (t + 1) * width]
+                slot = s * slots + t
+                lead = meta[r * FIELDS + 2 * slots + slot]
+
+                @pl.when(lead == slot)
                 def _():
-                    for t in range(slots):
-                        right[:, t * width : (t + 1) * width] = own[line, t, :, cols]
-
-                @pl.when(source == 1)
+                    if s == slots - 1:
+                        finish(r, slot, part)
+                    else:
+                        acc[r, slot] = part
+
+                @pl.when(lead != slot)
                 def _():
-                    for t in range(slots):
-                        right[:, t * width : (t + 1) * width] = beside[line, t, :, cols]
-
-                @pl.when(source == 2)
-                def _():
-                    for t in range(slots):
-                        right[:, t * width : (t + 1) * width] = across[line, t]
-
-            product = jnp.dot(own[r, s], right[...], preferred_element_type=jnp.float32)
-            for t in range(slots):
-                part = product[:, t * width : (t + 1) * width]
-                slot = s * slots + t
-                if s == 0:
-                    acc[slot] = part
-                else:
-                    lead = meta[base + 2 * slots + slot]
-
-                    @pl.when(lead == slot)
-                    def _():
-                        acc[slot] = part
-
-                    @pl.when(lead != slot)
-                    def _():
-                        acc[lead] += part
-                        acc[slot] = jnp.zeros_like(part)
-
-        for slot in range(slots * slots):
-            values = acc[slot].astype(jnp.bfloat16)
-            out[r, slot] = values
-            wide = values.astype(jnp.float32)
-            place = meta[base + 2 * slots + slots * slots + slot]
-            win[pl.ds(place, 1), :] += jnp.sum(wide * wide, axis=0, keepdims=True)
+                    acc[r, lead] += part
+                    if s == slots - 1:
+                        out[r, slot] = jnp.zeros_like(out[r, slot])
+                    else:
+                        acc[r, slot] = jnp.zeros_like(part)
+
+        for slot in range(slots * (slots - 1)):
+            finish(r, slot, acc[r, slot])
 
 
 def expand(q, meta, own, beside, across, before):
-    rows_here, slots, side, width = across.shape
-    vmem = pl.BlockSpec(memory_space=pltpu.VMEM)
+    rows_here, slots, side, width = across[0].shape
+    vmem, anywhere = pl.BlockSpec(memory_space=pltpu.VMEM), pl.BlockSpec(memory_space=pl.ANY)
+    jobs = rows_here * (slots - 1)
     return pl.pallas_call(
         functools.partial(expand_kernel, q, rows_here, slots),
-        in_specs=[pl.BlockSpec(memory_space=pltpu.SMEM), vmem, vmem, vmem, pl.BlockSpec(memory_space=pl.ANY)],
+        in_specs=[pl.BlockSpec(memory_space=pltpu.SMEM), vmem] + [anywhere] * (len(across) + 2),
         out_specs=[vmem, vmem],
         out_shape=[
             jax.ShapeDtypeStruct((rows_here, slots * slots, side, width), jnp.bfloat16),
             jax.ShapeDtypeStruct((16, width), jnp.float32),
         ],
         scratch_shapes=[
-            pltpu.VMEM((slots * slots, side, width), jnp.float32),
-            pltpu.VMEM((side, slots * width), jnp.bfloat16),
+            pltpu.VMEM((rows_here, slots * (slots - 1), side, width), jnp.float32),
+            pltpu.VMEM((jobs, slots, side, width), jnp.bfloat16),
+            pltpu.SemaphoreType.DMA((jobs,)),
         ],
         compiler_params=pltpu.CompilerParams(vmem_limit_bytes=24 * 2**20),
         cost_estimate=pl.CostEstimate(
@@ -112,7 +144,7 @@
             transcendentals=0,
         ),
         name=f"expand{q}",
-    )(meta, own, beside, across, before)
+    )(meta, own, beside, *across, before)
 
 
 def inflate_kernel(scale, slots, group, meta, totals, *refs):
@@ -167,12 +199,25 @@
     second_chip = both_ways([(2 * c + 1, 2 * c + 4) for c in range(chips - 2)])
 
     width = side // CHUNKS
-    across = [
-        lax.ppermute(matrix_tiles[..., q * width : (q + 1) * width], AXES, next_chip)
-        for q in range(CHUNKS)
-    ]
+    here = lax.axis_index(AXES)
+    rows, columns = lax.axis_size("row"), lax.axis_size("col")
+    pieces = [matrix_tiles[..., :width]]
+    first, held = lax.optimization_barrier((pieces[0], matrix_tiles))
+    pieces = [first] + [held[..., q * width : (q + 1) * width] for q in range(1, CHUNKS)]
     beside = lax.ppermute(matrix_tiles, AXES, swap)
-    meta = plan(pattern, start, rows_here, core)
+    across = [[lax.ppermute(piece, AXES, next_chip)] for piece in pieces[:-1]]
+    kind = jnp.int32(0)
+    if rows == 4:
+        legs, kinds = detours(rows - 1, columns)
+        straight = [pair for pair in next_chip if pair[1] not in kinds]
+        across.append([lax.ppermute(pieces[-1], AXES, straight)])
+        for out_leg, home_leg in legs:
+            across[-1].append(lax.ppermute(lax.ppermute(pieces[-1], AXES, out_leg), AXES, home_leg))
+        for target, number in kinds.items():
+            kind = jnp.where(here == target, number, kind)
+    else:
+        across.append([lax.ppermute(pieces[-1], AXES, next_chip)])
+    meta = plan(pattern, start, rows_here, core, kind)
     parts, windows = [], []
     for q in range(CHUNKS):
         before = windows[-1] if windows else meta

time: 106 us -> 95.3 us (0.90)
  waiting for transfers between devices: 42.9 us -> 31.8 us
  Pallas kernels: 30.3 us -> 23.7 us
  starting transfers between devices: 26.5 us -> 30.9 us
  local copies, waits for them, and re-layouts: 5.11 us -> 6.65 us
    ppermute x4 -> x8, waiting for transfers between devices: 39.4 us -> 28.5 us  [the longest x3 22.5 us: body(): across = [[lax.ppermute(piece, AXES, next_chip)] for piece in pieces[:-1]]]
    pallas_call x4, Pallas kernels: 24.5 us -> 17.9 us  [expand(): pl.pallas_call(functools.partial(expand_kernel, q, rows_here, slots), in_...]
    ppermute x4 -> x8, starting transfers between devices: 11.1 us -> 17.4 us  [the longest x3 7.45 us: body(): across = [[lax.ppermute(piece, AXES, next_chip)] for piece in pieces[:-1]]]
    ppermute x1, starting transfers between devices: 5.43 us -> 1.97 us  [body(): chip = window + lax.ppermute(window, AXES, swap)]
    slice x1 -> x2, local copies, waits for them, and re-layouts: 3.73 us -> 5.26 us  [the longest x1 3.1 us: body(): held[..., q * width:(q + 1) * width]]
  transfers between devices with their start and end apart: 9 -> 13, of which waited for: 7 -> 7; matrix products, arithmetic and copies ran while one was open for 5% -> 8% of each run, Pallas kernels for 17% -> 14%
where the time goes in v2:
time: 95.3 us; the launch traced here: 93.8 us
  waiting for transfers between devices  31.8 us (33%)
  starting transfers between devices  30.9 us (32%)
  Pallas kernels  23.7 us (25%)
  local copies, waits for them, and re-layouts  6.65 us (7%)
    ppermute x3, waiting for transfers between devices, body(): across = [[lax.ppermute(piece, AXES, next_chip)] for piece in pieces[:-1]]  22.5 us
    pallas_call x4, Pallas kernels, expand(): pl.pallas_call(functools.partial(expand_kernel, q, rows_here, slots), in_...  17.9 us
    ppermute x3, starting transfers between devices, body(): across = [[lax.ppermute(piece, AXES, next_chip)] for piece in pieces[:-1]]  7.45 us
    ppermute x1, waiting for transfers between devices, body(): across.append([lax.ppermute(pieces[-1], AXES, straight)])  6.04 us
    pallas_call x1, Pallas kernels, inflate(): pl.pallas_call(functools.partial(inflate_kernel, scale, slots, group), gr...  5.78 us
    ppermute x1, starting transfers between devices, body(): totals = chip + gathered + lax.ppermute(gathered, AXES, swap)  4.51 us
    ppermute x1, starting transfers between devices, body(): first = lax.ppermute(chip, AXES, next_chip)  4 us
    ppermute x1, starting transfers between devices, body(): across.append([lax.ppermute(pieces[-1], AXES, straight)])  3.64 us
  transfers between devices with their start and end apart: 13, of which 7 were waited for; matrix products, arithmetic and copies ran while one was open for 8% of the time, Pallas kernels for 14%

profile of v2, /device:TPU:5, one launch (start us, length us, event | category | flops | bytes accessed | tf_op | source)
XLA Modules:
  0.0 93.8 jit_solution(12234347218037781073)
XLA Ops:
  0.0 0.7 collective-permute-start
  0.7 2.2 %slice.27 = bf16[2,3,512,128]{3,2,1,0:T(8,128)(2,1)} slice(bf16[2,3,512,512]{3,2,1,0:T(8,128)(2,1)} %own.7), slice={[0:2], [0:3], [0:512], [0:128]} | slice | bytes 1572864 | tf_op jit(solution)/shard_map/slice | solution.py:204
  2.8 3.1 %collective-permute-start.1 = (bf16[2,3,512,128]{3,2,1,0:T(8,128)(2,1)}, bf16[2,3,512,128]{3,2,1,0:T(8,128)(2,1)}, u32[]{:S(2)}, u32[]{:S(2)}) collective-permute-start(bf16[2,3,512,128]{3,2,1,0:T(8,128)(2,1)} %slice.27), channel_id=1, source_target_pairs={{1,2},{3,4},{5,6},{7,8},{9,10},{11,12},{13,14},{15,16},{17,18},{19... | collective-permute-start | bytes 2359304 | tf_op jit(solution)/shard_map/ppermute | solution.py:208
  6.0 3.1 %fusion.3 = (bf16[2,3,512,128]{3,2,1,0:T(8,128)(2,1)}, bf16[2,3,512,128]{3,2,1,0:T(8,128)(2,1)}, bf16[2,3,512,128]{3,2,1,0:T(8,128)(2,1)}) fusion(bf16[2,3,512,512]{3,2,1,0:T(8,128)(2,1)} %own.7), kind=kLoop, calls=%fused_computation.22 | loop fusion | bytes 4718592 | tf_op jit(solution)/shard_map/slice | solution.py:206
  9.1 1.6 %collective-permute-start.7 = (bf16[2,3,512,128]{3,2,1,0:T(8,128)(2,1)}, bf16[2,3,512,128]{3,2,1,0:T(8,128)(2,1)}, u32[]{:S(2)}, u32[]{:S(2)}) collective-permute-start(bf16[2,3,512,128]{3,2,1,0:T(8,128)(2,1)} %get-tuple-element.28), channel_id=1, source_target_pairs={{7,31},{24,0}} | collective-permute-start | bytes 2359304 | tf_op jit(solution)/shard_map/ppermute | solution.py:215
  10.6 1.5 %collective-permute-start.5 = (bf16[2,3,512,128]{3,2,1,0:T(8,128)(2,1)}, bf16[2,3,512,128]{3,2,1,0:T(8,128)(2,1)}, u32[]{:S(2)}, u32[]{:S(2)}) collective-permute-start(bf16[2,3,512,128]{3,2,1,0:T(8,128)(2,1)} %get-tuple-element.28), channel_id=1, source_target_pairs={{8,0},{16,1},{15,30},{23,31}} | collective-permute-start | bytes 2359304 | tf_op jit(solution)/shard_map/ppermute | solution.py:215
  12.2 2.4 %collective-permute-start.2 = (bf16[2,3,512,128]{3,2,1,0:T(8,128)(2,1)}, bf16[2,3,512,128]{3,2,1,0:T(8,128)(2,1)}, u32[]{:S(2)}, u32[]{:S(2)}) collective-permute-start(bf16[2,3,512,128]{3,2,1,0:T(8,128)(2,1)} %get-tuple-element.27), channel_id=1, source_target_pairs={{1,2},{3,4},{5,6},{7,8},{9,10},{11,12},{13,14},{15,16},{17,18},{19... | collective-permute-start | bytes 2359304 | tf_op jit(solution)/shard_map/ppermute | solution.py:208
  14.6 0.1 copy.19
  14.8 0.6 gather_fusion
  15.6 0.1 copy.22
  15.8 0.1 copy.23
  15.9 0.3 fusion
  16.3 6.8 %collective-permute-done.1.refs_1_ = bf16[2,3,512,128]{3,2,1,0:T(8,128)(2,1)} collective-permute-done((bf16[2,3,512,128]{3,2,1,0:T(8,128)(2,1)}, bf16[2,3,512,128]{3,2,1,0:T(8,128)(2,1)}, u32[]{:S(2)}, u32[]{:S(2)}) %collective-permute-start.1) | collective-permute-done | bytes 786464 | tf_op jit(solution)/shard_map/ppermute | solution.py:208
  23.1 1.9 %collective-permute-start.3 = (bf16[2,3,512,128]{3,2,1,0:T(8,128)(2,1)}, bf16[2,3,512,128]{3,2,1,0:T(8,128)(2,1)}, u32[]{:S(2)}, u32[]{:S(2)}) collective-permute-start(bf16[2,3,512,128]{3,2,1,0:T(8,128)(2,1)} %get-tuple-element.29), channel_id=1, source_target_pairs={{1,2},{3,4},{5,6},{7,8},{9,10},{11,12},{13,14},{15,16},{17,18},{19... | collective-permute-start | bytes 2359304 | tf_op jit(solution)/shard_map/ppermute | solution.py:208
  25.0 3.6 %collective-permute-start.4 = (bf16[2,3,512,128]{3,2,1,0:T(8,128)(2,1)}, bf16[2,3,512,128]{3,2,1,0:T(8,128)(2,1)}, u32[]{:S(2)}, u32[]{:S(2)}) collective-permute-start(bf16[2,3,512,128]{3,2,1,0:T(8,128)(2,1)} %get-tuple-element.28), channel_id=1, source_target_pairs={{1,2},{3,4},{5,6},{9,10},{11,12},{13,14},{17,18},{19,20},{21,22},{... | collective-permute-start | bytes 2359304 | tf_op jit(solution)/shard_map/ppermute | solution.py:213
  28.7 1.6 %collective-permute-start.8 = (bf16[2,3,512,128]{3,2,1,0:T(8,128)(2,1)}, bf16[2,3,512,128]{3,2,1,0:T(8,128)(2,1)}, u32[]{:S(2)}, u32[]{:S(2)}) collective-permute-start(bf16[2,3,512,128]{3,2,1,0:T(8,128)(2,1)} %collective-permute-done.7), channel_id=1, source_target_pairs={{31,8},{0,23}} | collective-permute-start | bytes 2359304 | tf_op jit(solution)/shard_map/ppermute | solution.py:215
  30.3 1.5 %collective-permute-start.6 = (bf16[2,3,512,128]{3,2,1,0:T(8,128)(2,1)}, bf16[2,3,512,128]{3,2,1,0:T(8,128)(2,1)}, u32[]{:S(2)}, u32[]{:S(2)}) collective-permute-start(bf16[2,3,512,128]{3,2,1,0:T(8,128)(2,1)} %collective-permute-done.5), channel_id=1, source_target_pairs={{0,7},{1,15},{30,16},{31,24}} | collective-permute-start | bytes 2359304 | tf_op jit(solution)/shard_map/ppermute | solution.py:215
  32.1 4.5 %expand0.1 = (bf16[2,9,512,128]{3,2,1,0:T(8,128)(2,1)S(1)}, f32[16,128]{1,0:T(8,128)S(1)}) custom-call(s32[49]{0:T(128)S(1)} %pad_add_fusion.1.meta.refs_2_, bf16[2,3,512,512]{3,2,1,0:T(8,128)(2,1)S(1)} %copy-done, bf16[2,3,512,512]{3,2,1,0:T(8,128)(2,1)} %collective-permute-done.refs_0_, bf16[2,3,512,128]{3,2,1,0:T(8,128)(2,1)} %collective-permute-done.1.refs_1_, ...), custom_call_target="tpu_custom_call" | custom-call | flops 1207959552 | bytes 12582912 | tf_op jit(solution)/shard_map/expand0/pallas_call | solution.py:127
  36.6 3.3 %collective-permute-done.2.refs_1_ = bf16[2,3,512,128]{3,2,1,0:T(8,128)(2,1)} collective-permute-done((bf16[2,3,512,128]{3,2,1,0:T(8,128)(2,1)}, bf16[2,3,512,128]{3,2,1,0:T(8,128)(2,1)}, u32[]{:S(2)}, u32[]{:S(2)}) %collective-permute-start.2) | collective-permute-done | bytes 786464 | tf_op jit(solution)/shard_map/ppermute | solution.py:208
  39.9 4.5 %expand1.1 = (bf16[2,9,512,128]{3,2,1,0:T(8,128)(2,1)S(1)}, f32[16,128]{1,0:T(8,128)S(1)}) custom-call(s32[49]{0:T(128)S(1)} %pad_add_fusion.1.meta.refs_2_, bf16[2,3,512,512]{3,2,1,0:T(8,128)(2,1)S(1)} %copy-done, bf16[2,3,512,512]{3,2,1,0:T(8,128)(2,1)} %collective-permute-done.refs_0_, bf16[2,3,512,128]{3,2,1,0:T(8,128)(2,1)} %collective-permute-done.2.refs_1_, ...), custom_call_target="tpu_custom_call" | custom-call | flops 1207959552 | bytes 12582912 | tf_op jit(solution)/shard_map/expand1/pallas_call | solution.py:127
  44.4 12.4 %collective-permute-done.3.refs_1_ = bf16[2,3,512,128]{3,2,1,0:T(8,128)(2,1)} collective-permute-done((bf16[2,3,512,128]{3,2,1,0:T(8,128)(2,1)}, bf16[2,3,512,128]{3,2,1,0:T(8,128)(2,1)}, u32[]{:S(2)}, u32[]{:S(2)}) %collective-permute-start.3) | collective-permute-done | bytes 786464 | tf_op jit(solution)/shard_map/ppermute | solution.py:208
  56.8 4.5 %expand2.1 = (bf16[2,9,512,128]{3,2,1,0:T(8,128)(2,1)S(1)}, f32[16,128]{1,0:T(8,128)S(1)}) custom-call(s32[49]{0:T(128)S(1)} %pad_add_fusion.1.meta.refs_2_, bf16[2,3,512,512]{3,2,1,0:T(8,128)(2,1)S(1)} %copy-done, bf16[2,3,512,512]{3,2,1,0:T(8,128)(2,1)} %collective-permute-done.refs_0_, bf16[2,3,512,128]{3,2,1,0:T(8,128)(2,1)} %collective-permute-done.3.refs_1_, ...), custom_call_target="tpu_custom_call" | custom-call | flops 1207959552 | bytes 12582912 | tf_op jit(solution)/shard_map/expand2/pallas_call | solution.py:127
  61.3 6.0 %collective-permute-done.4.refs_1_ = bf16[2,3,512,128]{3,2,1,0:T(8,128)(2,1)} collective-permute-done((bf16[2,3,512,128]{3,2,1,0:T(8,128)(2,1)}, bf16[2,3,512,128]{3,2,1,0:T(8,128)(2,1)}, u32[]{:S(2)}, u32[]{:S(2)}) %collective-permute-start.4) | collective-permute-done | bytes 786464 | tf_op jit(solution)/shard_map/ppermute | solution.py:213
  67.3 4.5 %expand3.1 = (bf16[2,9,512,128]{3,2,1,0:T(8,128)(2,1)S(1)}, f32[16,128]{1,0:T(8,128)S(1)}) custom-call(s32[49]{0:T(128)S(1)} %pad_add_fusion.1.meta.refs_2_, bf16[2,3,512,512]{3,2,1,0:T(8,128)(2,1)S(1)} %copy-done, bf16[2,3,512,512]{3,2,1,0:T(8,128)(2,1)} %collective-permute-done.refs_0_, bf16[2,3,512,128]{3,2,1,0:T(8,128)(2,1)} %collective-permute-done.4.refs_1_, ...), custom_call_target="tpu_custom_call" | custom-call | flops 1207959552 | bytes 12582912 | tf_op jit(solution)/shard_map/expand3/pallas_call | solution.py:127
  71.8 2.0 %collective-permute-start.9 = (f32[12,512]{1,0:T(8,128)S(1)}, f32[12,512]{1,0:T(8,128)S(1)}, u32[]{:S(2)}, u32[]{:S(2)}) collective-permute-start(f32[12,512]{1,0:T(8,128)S(1)} %pad_maximum_fusion), channel_id=1, source_target_pairs={{0,1},{2,3},{4,5},{6,7},{8,9},{10,11},{12,13},{14,15},{16,17},{18,... | collective-permute-start | bytes 73736 | tf_op jit(solution)/shard_map/ppermute | solution.py:232
  73.8 0.9 collective-permute-done.9
  74.7 2.3 %collective-permute-start.11 = (f32[12,512]{1,0:T(8,128)S(1)}, f32[12,512]{1,0:T(8,128)S(1)}, u32[]{:S(2)}, u32[]{:S(2)}) collective-permute-start(f32[12,512]{1,0:T(8,128)S(1)} %fusion.2), channel_id=1, source_target_pairs={{1,4},{3,6},{5,8},{7,10},{9,12},{11,14},{13,16},{15,18},{17,20},{1... | collective-permute-start | bytes 73736 | tf_op jit(solution)/shard_map/ppermute | solution.py:234
  77.0 4.0 %collective-permute-start.10 = (f32[12,512]{1,0:T(8,128)S(1)}, f32[12,512]{1,0:T(8,128)S(1)}, u32[]{:S(2)}, u32[]{:S(2)}) collective-permute-start(f32[12,512]{1,0:T(8,128)S(1)} %fusion.2), channel_id=1, source_target_pairs={{1,2},{3,4},{5,6},{7,8},{9,10},{11,12},{13,14},{15,16},{17,18},{19... | collective-permute-start | bytes 73736 | tf_op jit(solution)/shard_map/ppermute | solution.py:233
  81.0 1.6 %collective-permute-done.10 = f32[12,512]{1,0:T(8,128)S(1)} collective-permute-done((f32[12,512]{1,0:T(8,128)S(1)}, f32[12,512]{1,0:T(8,128)S(1)}, u32[]{:S(2)}, u32[]{:S(2)}) %collective-permute-start.10) | collective-permute-done | bytes 24608 | tf_op jit(solution)/shard_map/ppermute | solution.py:233
  82.6 4.5 %collective-permute-start.12 = (f32[12,512]{1,0:T(8,128)S(1)}, f32[12,512]{1,0:T(8,128)S(1)}, u32[]{:S(2)}, u32[]{:S(2)}) collective-permute-start(f32[12,512]{1,0:T(8,128)S(1)} %add_select_fusion), channel_id=1, source_target_pairs={{0,1},{2,3},{4,5},{6,7},{8,9},{10,11},{12,13},{14,15},{16,17},{18,... | collective-permute-start | bytes 73736 | tf_op jit(solution)/shard_map/ppermute | solution.py:240
  87.1 0.9 collective-permute-done.12
  88.0 5.8 %inflate.1 = bf16[2,9,512,512]{3,2,1,0:T(8,128)(2,1)} custom-call(s32[49]{0:T(128)S(1)} %pad_add_fusion.1.meta.refs_2_, f32[12,512]{1,0:T(8,128)S(1)} %add_add_fusion.totals, bf16[2,9,512,128]{3,2,1,0:T(8,128)(2,1)S(1)} %get-tuple-element.21.refs_0_, bf16[2,9,512,128]{3,2,1,0:T(8,128)(2,1)S(1)} %get-tuple-element.22.refs_1_, ...), custom_call_target="tpu_custom_call" | custom-call | flops 16777216 | bytes 18874368 | tf_op jit(solution)/shard_map/inflate/pallas_call | solution.py:169
  (29 shorter events, 0.8 us)
Async XLA Ops:
  0.0 32.1 %copy-start = (bf16[2,3,512,512]{3,2,1,0:T(8,128)(2,1)S(1)}, bf16[2,3,512,512]{3,2,1,0:T(8,128)(2,1)}, u32[]{:S(2)}) copy-start(bf16[2,3,512,512]{3,2,1,0:T(8,128)(2,1)} %own.7) | copy-start | bytes 9437188
  0.0 14.6 %copy-start.1 = (s32[64,3]{0,1:T(4,128)S(1)}, s32[64,3]{0,1:T(4,128)}, u32[]{:S(2)}) copy-start(s32[64,3]{0,1:T(4,128)} %param.3) | copy-start | bytes 2308
  0.0 30.3 %collective-permute-start = (bf16[2,3,512,512]{3,2,1,0:T(8,128)(2,1)}, bf16[2,3,512,512]{3,2,1,0:T(8,128)(2,1)}, u32[]{:S(2)}, u32[]{:S(2)}) collective-permute-start(bf16[2,3,512,512]{3,2,1,0:T(8,128)(2,1)} %own.7), channel_id=1, source_target_pairs={{0,1},{2,3},{4,5},{6,7},{8,9},{10,11},{12,13},{14,15},{16,17},{18,... | collective-permute-start | bytes 9437192 | tf_op jit(solution)/shard_map/ppermute | solution.py:207
  2.8 20.2 %collective-permute-start.1 = (bf16[2,3,512,128]{3,2,1,0:T(8,128)(2,1)}, bf16[2,3,512,128]{3,2,1,0:T(8,128)(2,1)}, u32[]{:S(2)}, u32[]{:S(2)}) collective-permute-start(bf16[2,3,512,128]{3,2,1,0:T(8,128)(2,1)} %slice.27), channel_id=1, source_target_pairs={{1,2},{3,4},{5,6},{7,8},{9,10},{11,12},{13,14},{15,16},{17,18},{19... | collective-permute-start | bytes 2359304 | tf_op jit(solution)/shard_map/ppermute | solution.py:208
  9.1 15.9 %collective-permute-start.7 = (bf16[2,3,512,128]{3,2,1,0:T(8,128)(2,1)}, bf16[2,3,512,128]{3,2,1,0:T(8,128)(2,1)}, u32[]{:S(2)}, u32[]{:S(2)}) collective-permute-start(bf16[2,3,512,128]{3,2,1,0:T(8,128)(2,1)} %get-tuple-element.28), channel_id=1, source_target_pairs={{7,31},{24,0}} | collective-permute-start | bytes 2359304 | tf_op jit(solution)/shard_map/ppermute | solution.py:215
  10.6 18.0 %collective-permute-start.5 = (bf16[2,3,512,128]{3,2,1,0:T(8,128)(2,1)}, bf16[2,3,512,128]{3,2,1,0:T(8,128)(2,1)}, u32[]{:S(2)}, u32[]{:S(2)}) collective-permute-start(bf16[2,3,512,128]{3,2,1,0:T(8,128)(2,1)} %get-tuple-element.28), channel_id=1, source_target_pairs={{8,0},{16,1},{15,30},{23,31}} | collective-permute-start | bytes 2359304 | tf_op jit(solution)/shard_map/ppermute | solution.py:215
  12.2 27.7 %collective-permute-start.2 = (bf16[2,3,512,128]{3,2,1,0:T(8,128)(2,1)}, bf16[2,3,512,128]{3,2,1,0:T(8,128)(2,1)}, u32[]{:S(2)}, u32[]{:S(2)}) collective-permute-start(bf16[2,3,512,128]{3,2,1,0:T(8,128)(2,1)} %get-tuple-element.27), channel_id=1, source_target_pairs={{1,2},{3,4},{5,6},{7,8},{9,10},{11,12},{13,14},{15,16},{17,18},{19... | collective-permute-start | bytes 2359304 | tf_op jit(solution)/shard_map/ppermute | solution.py:208
  23.1 33.7 %collective-permute-start.3 = (bf16[2,3,512,128]{3,2,1,0:T(8,128)(2,1)}, bf16[2,3,512,128]{3,2,1,0:T(8,128)(2,1)}, u32[]{:S(2)}, u32[]{:S(2)}) collective-permute-start(bf16[2,3,512,128]{3,2,1,0:T(8,128)(2,1)} %get-tuple-element.29), channel_id=1, source_target_pairs={{1,2},{3,4},{5,6},{7,8},{9,10},{11,12},{13,14},{15,16},{17,18},{19... | collective-permute-start | bytes 2359304 | tf_op jit(solution)/shard_map/ppermute | solution.py:208
  25.0 42.3 %collective-permute-start.4 = (bf16[2,3,512,128]{3,2,1,0:T(8,128)(2,1)}, bf16[2,3,512,128]{3,2,1,0:T(8,128)(2,1)}, u32[]{:S(2)}, u32[]{:S(2)}) collective-permute-start(bf16[2,3,512,128]{3,2,1,0:T(8,128)(2,1)} %get-tuple-element.28), channel_id=1, source_target_pairs={{1,2},{3,4},{5,6},{9,10},{11,12},{13,14},{17,18},{19,20},{21,22},{... | collective-permute-start | bytes 2359304 | tf_op jit(solution)/shard_map/ppermute | solution.py:213
  28.7 38.6 %collective-permute-start.8 = (bf16[2,3,512,128]{3,2,1,0:T(8,128)(2,1)}, bf16[2,3,512,128]{3,2,1,0:T(8,128)(2,1)}, u32[]{:S(2)}, u32[]{:S(2)}) collective-permute-start(bf16[2,3,512,128]{3,2,1,0:T(8,128)(2,1)} %collective-permute-done.7), channel_id=1, source_target_pairs={{31,8},{0,23}} | collective-permute-start | bytes 2359304 | tf_op jit(solution)/shard_map/ppermute | solution.py:215
  30.3 37.0 %collective-permute-start.6 = (bf16[2,3,512,128]{3,2,1,0:T(8,128)(2,1)}, bf16[2,3,512,128]{3,2,1,0:T(8,128)(2,1)}, u32[]{:S(2)}, u32[]{:S(2)}) collective-permute-start(bf16[2,3,512,128]{3,2,1,0:T(8,128)(2,1)} %collective-permute-done.5), channel_id=1, source_target_pairs={{0,7},{1,15},{30,16},{31,24}} | collective-permute-start | bytes 2359304 | tf_op jit(solution)/shard_map/ppermute | solution.py:215
  71.8 2.8 %collective-permute-start.9 = (f32[12,512]{1,0:T(8,128)S(1)}, f32[12,512]{1,0:T(8,128)S(1)}, u32[]{:S(2)}, u32[]{:S(2)}) collective-permute-start(f32[12,512]{1,0:T(8,128)S(1)} %pad_maximum_fusion), channel_id=1, source_target_pairs={{0,1},{2,3},{4,5},{6,7},{8,9},{10,11},{12,13},{14,15},{16,17},{18,... | collective-permute-start | bytes 73736 | tf_op jit(solution)/shard_map/ppermute | solution.py:232
  74.7 6.4 %collective-permute-start.11 = (f32[12,512]{1,0:T(8,128)S(1)}, f32[12,512]{1,0:T(8,128)S(1)}, u32[]{:S(2)}, u32[]{:S(2)}) collective-permute-start(f32[12,512]{1,0:T(8,128)S(1)} %fusion.2), channel_id=1, source_target_pairs={{1,4},{3,6},{5,8},{7,10},{9,12},{11,14},{13,16},{15,18},{17,20},{1... | collective-permute-start | bytes 73736 | tf_op jit(solution)/shard_map/ppermute | solution.py:234
  77.0 5.6 %collective-permute-start.10 = (f32[12,512]{1,0:T(8,128)S(1)}, f32[12,512]{1,0:T(8,128)S(1)}, u32[]{:S(2)}, u32[]{:S(2)}) collective-permute-start(f32[12,512]{1,0:T(8,128)S(1)} %fusion.2), channel_id=1, source_target_pairs={{1,2},{3,4},{5,6},{7,8},{9,10},{11,12},{13,14},{15,16},{17,18},{19... | collective-permute-start | bytes 73736 | tf_op jit(solution)/shard_map/ppermute | solution.py:233
  82.6 5.4 %collective-permute-start.12 = (f32[12,512]{1,0:T(8,128)S(1)}, f32[12,512]{1,0:T(8,128)S(1)}, u32[]{:S(2)}, u32[]{:S(2)}) collective-permute-start(f32[12,512]{1,0:T(8,128)S(1)} %add_select_fusion), channel_id=1, source_target_pairs={{0,1},{2,3},{4,5},{6,7},{8,9},{10,11},{12,13},{14,15},{16,17},{18,... | collective-permute-start | bytes 73736 | tf_op jit(solution)/shard_map/ppermute | solution.py:240

commit v3 on v2

--- a/solution.py
+++ b/solution.py
@@ -46,8 +46,8 @@
     for row in range(last_row):
         low, high = device(row, top, 1), device(row + 1, 0, 0)
         for source, target, spare, turn in ((high, low, spare_up, row), (low, high, spare_down, last_row - 1 - row)):
-            which = turn // 2
-            stop = spare[turn % 2]
+            which = min(turn, 1)
+            stop = spare[max(turn - 1, 0)]
             legs[which][0].append((source, stop))
             legs[which][1].append((stop, target))
             kinds[target] = which + 1
@@ -100,21 +100,12 @@
                 part = later[:, t * width : (t + 1) * width]
                 slot = s * slots + t
                 lead = meta[r * FIELDS + 2 * slots + slot]
-
-                @pl.when(lead == slot)
-                def _():
-                    if s == slots - 1:
-                        finish(r, slot, part)
-                    else:
-                        acc[r, slot] = part
-
-                @pl.when(lead != slot)
-                def _():
-                    acc[r, lead] += part
-                    if s == slots - 1:
-                        out[r, slot] = jnp.zeros_like(out[r, slot])
-                    else:
-                        acc[r, slot] = jnp.zeros_like(part)
+                kept = part * jnp.where(lead == slot, 1.0, 0.0)
+                acc[r, jnp.where(lead == slot, slots * (slots - 1), lead)] += part
+                if s == slots - 1:
+                    finish(r, slot, kept)
+                else:
+                    acc[r, slot] = kept
 
         for slot in range(slots * (slots - 1)):
             finish(r, slot, acc[r, slot])
@@ -133,7 +124,7 @@
             jax.ShapeDtypeStruct((16, width), jnp.float32),
         ],
         scratch_shapes=[
-            pltpu.VMEM((rows_here, slots * (slots - 1), side, width), jnp.float32),
+            pltpu.VMEM((rows_here, slots * (slots - 1) + 1, side, width), jnp.float32),
             pltpu.VMEM((jobs, slots, side, width), jnp.bfloat16),
             pltpu.SemaphoreType.DMA((jobs,)),
         ],
@@ -147,35 +138,72 @@
     )(meta, own, beside, *across, before)
 
 
-def inflate_kernel(scale, slots, group, meta, totals, *refs):
-    parts, out = refs[:-1], refs[-1]
-    width = parts[0].shape[3]
-    r = pl.program_id(0)
-    g = pl.program_id(1)
-    for o in range(group):
-        slot = g * group + o
+def inflate_kernel(scale, slots, first, meta, totals, *refs):
+    count = len(refs) - 3 - (1 if first else 0)
+    parts, (out, made, sems) = refs[:count], refs[-3:]
+    rows_here, slot_total, side, width = parts[0].shape
+    depth = made.shape[0]
+    cols = pl.ds(first * width, count * width)
+    jobs = [(r, slot) for r in range(rows_here) for slot in range(slot_total)]
+
+    def sending(number):
+        r, slot = jobs[number]
+        at = number % depth
+        return pltpu.make_async_copy(made.at[at], out.at[r, slot, :, cols], sems.at[at])
+
+    for number, (r, slot) in enumerate(jobs):
+        if number >= depth:
+            sending(number - depth).wait()
         place = meta[r * FIELDS + 2 * slots + slots * slots + slot]
         factor = scale / totals[pl.ds(place, 1), :]
         for q, part in enumerate(parts):
             wide = part[r, slot].astype(jnp.float32)
-            cols = slice(q * width, (q + 1) * width)
-            out[0, o, :, cols] = (wide * wide * factor[:, cols]).astype(jnp.bfloat16)
-
-
-def inflate(scale, slots, meta, totals, parts):
+            here = slice(q * width, (q + 1) * width)
+            made[number % depth, :, here] = (wide * wide * factor[:, here]).astype(jnp.bfloat16)
+        sending(number).start()
+    for number in range(len(jobs) - depth, len(jobs)):
+        sending(number).wait()
+
+
+def inflate(scale, slots, meta, totals, parts, first=0, so_far=None):
     rows_here, slot_total, side, width = parts[0].shape
-    group = 3
-    vmem = pl.BlockSpec(memory_space=pltpu.VMEM)
+    vmem, anywhere = pl.BlockSpec(memory_space=pltpu.VMEM), pl.BlockSpec(memory_space=pl.ANY)
+    more = [] if so_far is None else [so_far]
     return pl.pallas_call(
-        functools.partial(inflate_kernel, scale, slots, group),
-        grid=(rows_here, slot_total // group),
-        in_specs=[pl.BlockSpec(memory_space=pltpu.SMEM), vmem] + [vmem] * len(parts),
-        out_specs=pl.BlockSpec((1, group, side, width * len(parts)), lambda r, g: (r, g, 0, 0)),
-        out_shape=jax.ShapeDtypeStruct((rows_here, slot_total, side, width * len(parts)), jnp.bfloat16),
-        compiler_params=pltpu.CompilerParams(vmem_limit_bytes=24 * 2**20),
-        cost_estimate=pl.CostEstimate(flops=2**24, bytes_accessed=18 * 2**20, transcendentals=0),
-        name="inflate",
-    )(meta, totals, *parts)
+        functools.partial(inflate_kernel, scale, slots, first),
+        in_specs=[pl.BlockSpec(memory_space=pltpu.SMEM), vmem] + [vmem] * len(parts) + [anywhere] * len(more),
+        out_specs=anywhere,
+        out_shape=jax.ShapeDtypeStruct((rows_here, slot_total, side, width * CHUNKS), jnp.bfloat16),
+        scratch_shapes=[
+            pltpu.VMEM((9, side, width * len(parts)), jnp.bfloat16),
+            pltpu.SemaphoreType.DMA((9,)),
+        ],
+        input_output_aliases={2 + len(parts): 0} if more else {},
+        compiler_params=pltpu.CompilerParams(vmem_limit_bytes=12 * 2**20),
+        cost_estimate=pl.CostEstimate(flops=2**22 * len(parts), bytes_accessed=4 * 2**20 * len(parts), transcendentals=0),
+        name=f"inflate{first}",
+    )(meta, totals, *parts, *more)
+
+
+def columns_kernel(q, width, tiles, *refs):
+    out, sem = refs[-2:]
+    copy = pltpu.make_async_copy(tiles.at[:, :, :, pl.ds(q * width, width)], out, sem)
+    copy.start()
+    copy.wait()
+
+
+def columns_of(tiles, q, width, after):
+    anywhere, far = pl.BlockSpec(memory_space=pl.ANY), pl.BlockSpec(memory_space=pltpu.HBM)
+    return pl.pallas_call(
+        functools.partial(columns_kernel, q, width),
+        in_specs=[far] + [anywhere] * len(after),
+        out_specs=far,
+        out_shape=jax.ShapeDtypeStruct((*tiles.shape[:3], width), tiles.dtype),
+        scratch_shapes=[pltpu.SemaphoreType.DMA],
+        compiler_params=pltpu.CompilerParams(vmem_limit_bytes=2**20),
+        cost_estimate=pl.CostEstimate(flops=0, bytes_accessed=2**20, transcendentals=0),
+        name=f"columns{q}",
+    )(tiles, *after)
 
 
 def shift_lines(block, distance):
@@ -201,29 +229,30 @@
     width = side // CHUNKS
     here = lax.axis_index(AXES)
     rows, columns = lax.axis_size("row"), lax.axis_size("col")
-    pieces = [matrix_tiles[..., :width]]
-    first, held = lax.optimization_barrier((pieces[0], matrix_tiles))
-    pieces = [first] + [held[..., q * width : (q + 1) * width] for q in range(1, CHUNKS)]
     beside = lax.ppermute(matrix_tiles, AXES, swap)
-    across = [[lax.ppermute(piece, AXES, next_chip)] for piece in pieces[:-1]]
+    pieces = [matrix_tiles[..., :width]] + [columns_of(matrix_tiles, q, width, [beside] * (q == 2)) for q in range(1, CHUNKS - 1)]
     kind = jnp.int32(0)
     if rows == 4:
         legs, kinds = detours(rows - 1, columns)
         straight = [pair for pair in next_chip if pair[1] not in kinds]
-        across.append([lax.ppermute(pieces[-1], AXES, straight)])
-        for out_leg, home_leg in legs:
-            across[-1].append(lax.ppermute(lax.ppermute(pieces[-1], AXES, out_leg), AXES, home_leg))
+        side_leg = lax.ppermute(pieces[0], AXES, legs[1][0])
+        stops = [lax.ppermute(pieces[0], AXES, straight + legs[0][0]), side_leg]
+        first = [stops[0]] + [lax.ppermute(stop, AXES, home_leg) for stop, (_, home_leg) in zip(stops, legs)]
         for target, number in kinds.items():
             kind = jnp.where(here == target, number, kind)
+        pieces.append(columns_of(matrix_tiles, CHUNKS - 1, width, stops))
+        order = [*range(1, CHUNKS - 1), 0, CHUNKS - 1]
     else:
-        across.append([lax.ppermute(pieces[-1], AXES, next_chip)])
+        first = [lax.ppermute(pieces[0], AXES, next_chip)]
+        pieces.append(columns_of(matrix_tiles, CHUNKS - 1, width, first))
+        order = [*range(CHUNKS)]
+    across = [first] + [[lax.ppermute(piece, AXES, next_chip)] for piece in pieces[1:]]
     meta = plan(pattern, start, rows_here, core, kind)
-    parts, windows = [], []
-    for q in range(CHUNKS):
-        before = windows[-1] if windows else meta
-        part, window = expand(q, meta, matrix_tiles, beside, across[q], before)
-        parts.append(part)
-        windows.append(window)
+    parts, windows = [None] * CHUNKS, [None] * CHUNKS
+    before = meta
+    for q in order:
+        parts[q], windows[q] = expand(q, meta, matrix_tiles, beside, across[q], before)
+        before = windows[q]
     window = jnp.concatenate(windows, axis=1)
 
     chip_rows = 2 * rows_here

time: 95.3 us -> 94.1 us (0.987); the launches traced: 93.8 us -> 93.7 us
  waiting for transfers between devices: 31.8 us -> 34.2 us
  starting transfers between devices: 30.9 us -> 29.5 us
  local copies, waits for them, and re-layouts: 6.65 us -> 5.35 us
    slice x2 -> x1, local copies, waits for them, and re-layouts: 5.26 us -> 2.08 us  [body(): matrix_tiles[..., :width]]
    ppermute x8 -> x7, waiting for transfers between devices: 28.5 us -> 30.9 us  [the longest x3 30.9 us: body(): lax.ppermute(piece, AXES, next_chip)]
    unnamed x5 -> x7, local copies, waits for them, and re-layouts: 0.1 us -> 1.99 us
    ppermute x8 -> x7, starting transfers between devices: 17.4 us -> 15.9 us  [the longest x3 8.17 us: body(): lax.ppermute(piece, AXES, next_chip)]
    pallas_call x1 -> x4, Pallas kernels: 5.78 us -> 7.09 us  [the longest x1 4.35 us: inflate(): pl.pallas_call(functools.partial(inflate_kernel, scale, slots, first), in...]
    pallas_call x4, Pallas kernels: 17.9 us -> 16.7 us  [expand(): pl.pallas_call(functools.partial(expand_kernel, q, rows_here, slots), in_...]
  transfers between devices with their start and end apart: 13 -> 12, of which waited for: 7 -> 6; matrix products, arithmetic and copies ran while one was open for 8% -> 4% of each run, Pallas kernels for 14% -> 16%
where the time goes in v3:
time: 94.1 us; the launch traced here: 93.7 us
  waiting for transfers between devices  34.2 us (36%)
  starting transfers between devices  29.5 us (31%)
  Pallas kernels  23.8 us (25%)
  local copies, waits for them, and re-layouts  5.35 us (6%)
    ppermute x3, waiting for transfers between devices, body(): lax.ppermute(piece, AXES, next_chip)  30.9 us
    pallas_call x4, Pallas kernels, expand(): pl.pallas_call(functools.partial(expand_kernel, q, rows_here, slots), in_...  16.7 us
    ppermute x3, starting transfers between devices, body(): lax.ppermute(piece, AXES, next_chip)  8.17 us
    ppermute x1, starting transfers between devices, body(): first = lax.ppermute(chip, AXES, next_chip)  4.48 us
    pallas_call x1, Pallas kernels, inflate(): pl.pallas_call(functools.partial(inflate_kernel, scale, slots, first), in...  4.35 us
    ppermute x1, starting transfers between devices, body(): totals = chip + gathered + lax.ppermute(gathered, AXES, swap)  4.04 us
    ppermute x2, starting transfers between devices, body(): lax.ppermute(stop, AXES, home_leg)  3.13 us
    ppermute x1, starting transfers between devices, body(): stops = [lax.ppermute(pieces[0], AXES, straight + legs[0][0]), side_leg]  3.08 us
  transfers between devices with their start and end apart: 12, of which 6 were waited for; matrix products, arithmetic and copies ran while one was open for 4% of the time, Pallas kernels for 16%

profile of v3, /device:TPU:5, one launch (start us, length us, event | category | flops | bytes accessed | tf_op | source)
XLA Modules:
  0.0 93.7 jit_solution(9795403838390870010)
XLA Ops:
  0.0 0.7 collective-permute-start
  0.7 2.1 %slice.18 = bf16[2,3,512,128]{3,2,1,0:T(8,128)(2,1)} slice(bf16[2,3,512,512]{3,2,1,0:T(8,128)(2,1)} %own.7), slice={[0:2], [0:3], [0:512], [0:128]} | slice | bytes 1572864 | tf_op jit(solution)/shard_map/slice | solution.py:233
  2.8 1.5 %collective-permute-start.3 = (bf16[2,3,512,128]{3,2,1,0:T(8,128)(2,1)}, bf16[2,3,512,128]{3,2,1,0:T(8,128)(2,1)}, u32[]{:S(2)}, u32[]{:S(2)}) collective-permute-start(bf16[2,3,512,128]{3,2,1,0:T(8,128)(2,1)} %slice.18), channel_id=1, source_target_pairs={{7,30},{16,0},{15,31},{24,1}} | collective-permute-start | bytes 2359304 | tf_op jit(solution)/shard_map/ppermute | solution.py:238
  4.3 3.1 %collective-permute-start.1 = (bf16[2,3,512,128]{3,2,1,0:T(8,128)(2,1)}, bf16[2,3,512,128]{3,2,1,0:T(8,128)(2,1)}, u32[]{:S(2)}, u32[]{:S(2)}) collective-permute-start(bf16[2,3,512,128]{3,2,1,0:T(8,128)(2,1)} %slice.18), channel_id=1, source_target_pairs={{1,2},{3,4},{5,6},{9,10},{11,12},{13,14},{17,18},{19,20},{21,22},{... | collective-permute-start | bytes 2359304 | tf_op jit(solution)/shard_map/ppermute | solution.py:239
  7.4 1.9 %copy-done = bf16[2,3,512,512]{3,2,1,0:T(8,128)(2,1)S(1)} copy-done((bf16[2,3,512,512]{3,2,1,0:T(8,128)(2,1)S(1)}, bf16[2,3,512,512]{3,2,1,0:T(8,128)(2,1)}, u32[]{:S(2)}) %copy-start) | copy-done | bytes 3145752
  9.3 0.9 %columns1.1 = bf16[2,3,512,128]{3,2,1,0:T(8,128)(2,1)} custom-call(bf16[2,3,512,512]{3,2,1,0:T(8,128)(2,1)S(1)} %copy-done), custom_call_target="tpu_custom_call" | custom-call | bytes 1048576 | tf_op jit(solution)/shard_map/columns1/pallas_call | solution.py:197
  10.2 2.6 %collective-permute-start.6 = (bf16[2,3,512,128]{3,2,1,0:T(8,128)(2,1)}, bf16[2,3,512,128]{3,2,1,0:T(8,128)(2,1)}, u32[]{:S(2)}, u32[]{:S(2)}) collective-permute-start(bf16[2,3,512,128]{3,2,1,0:T(8,128)(2,1)} %columns1.1), channel_id=1, source_target_pairs={{1,2},{3,4},{5,6},{7,8},{9,10},{11,12},{13,14},{15,16},{17,18},{19... | collective-permute-start | bytes 2359304 | tf_op jit(solution)/shard_map/ppermute | solution.py:249
  13.1 0.6 gather_fusion
  13.8 0.1 copy.22
  14.0 0.1 copy.23
  14.1 0.9 columns2.1
  15.0 3.1 %collective-permute-start.5 = (bf16[2,3,512,128]{3,2,1,0:T(8,128)(2,1)}, bf16[2,3,512,128]{3,2,1,0:T(8,128)(2,1)}, u32[]{:S(2)}, u32[]{:S(2)}) collective-permute-start(bf16[2,3,512,128]{3,2,1,0:T(8,128)(2,1)} %columns2.1), channel_id=1, source_target_pairs={{1,2},{3,4},{5,6},{7,8},{9,10},{11,12},{13,14},{15,16},{17,18},{19... | collective-permute-start | bytes 2359304 | tf_op jit(solution)/shard_map/ppermute | solution.py:249
  18.1 0.3 fusion
  18.5 1.6 %collective-permute-start.4 = (bf16[2,3,512,128]{3,2,1,0:T(8,128)(2,1)}, bf16[2,3,512,128]{3,2,1,0:T(8,128)(2,1)}, u32[]{:S(2)}, u32[]{:S(2)}) collective-permute-start(bf16[2,3,512,128]{3,2,1,0:T(8,128)(2,1)} %collective-permute-done.3.refs_1_), channel_id=1, source_target_pairs={{30,8},{0,15},{31,16},{1,23}} | collective-permute-start | bytes 2359304 | tf_op jit(solution)/shard_map/ppermute | solution.py:240
  20.1 1.6 %collective-permute-start.2 = (bf16[2,3,512,128]{3,2,1,0:T(8,128)(2,1)}, bf16[2,3,512,128]{3,2,1,0:T(8,128)(2,1)}, u32[]{:S(2)}, u32[]{:S(2)}) collective-permute-start(bf16[2,3,512,128]{3,2,1,0:T(8,128)(2,1)} %collective-permute-done.1.refs_1_.refs_0_), channel_id=1, source_target_pairs={{0,7},{31,24}} | collective-permute-start | bytes 2359304 | tf_op jit(solution)/shard_map/ppermute | solution.py:240
  21.7 0.9 columns3.1
  22.6 2.5 %collective-permute-start.7 = (bf16[2,3,512,128]{3,2,1,0:T(8,128)(2,1)}, bf16[2,3,512,128]{3,2,1,0:T(8,128)(2,1)}, u32[]{:S(2)}, u32[]{:S(2)}) collective-permute-start(bf16[2,3,512,128]{3,2,1,0:T(8,128)(2,1)} %columns3.1), channel_id=1, source_target_pairs={{1,2},{3,4},{5,6},{7,8},{9,10},{11,12},{13,14},{15,16},{17,18},{19... | collective-permute-start | bytes 2359304 | tf_op jit(solution)/shard_map/ppermute | solution.py:249
  25.3 10.0 %collective-permute-done.6.refs_1_ = bf16[2,3,512,128]{3,2,1,0:T(8,128)(2,1)} collective-permute-done((bf16[2,3,512,128]{3,2,1,0:T(8,128)(2,1)}, bf16[2,3,512,128]{3,2,1,0:T(8,128)(2,1)}, u32[]{:S(2)}, u32[]{:S(2)}) %collective-permute-start.6) | collective-permute-done | bytes 786464 | tf_op jit(solution)/shard_map/ppermute | solution.py:249
  35.4 4.2 %expand1.1 = (bf16[2,9,512,128]{3,2,1,0:T(8,128)(2,1)S(1)}, f32[16,128]{1,0:T(8,128)S(1)}) custom-call(s32[49]{0:T(128)S(1)} %pad_add_fusion.1.meta.refs_2_, bf16[2,3,512,512]{3,2,1,0:T(8,128)(2,1)S(1)} %copy-done.1, bf16[2,3,512,512]{3,2,1,0:T(8,128)(2,1)} %collective-permute-done.refs_0_, bf16[2,3,512,128]{3,2,1,0:T(8,128)(2,1)} %collective-permute-done.6.refs_1_, ...), custom_call_target="tpu_custom_call" | custom-call | flops 1207959552 | bytes 12582912 | tf_op jit(solution)/shard_map/expand1/pallas_call | solution.py:118
  39.5 12.7 %collective-permute-done.5.refs_1_ = bf16[2,3,512,128]{3,2,1,0:T(8,128)(2,1)} collective-permute-done((bf16[2,3,512,128]{3,2,1,0:T(8,128)(2,1)}, bf16[2,3,512,128]{3,2,1,0:T(8,128)(2,1)}, u32[]{:S(2)}, u32[]{:S(2)}) %collective-permute-start.5) | collective-permute-done | bytes 786464 | tf_op jit(solution)/shard_map/ppermute | solution.py:249
  52.2 4.2 %expand2.1 = (bf16[2,9,512,128]{3,2,1,0:T(8,128)(2,1)S(1)}, f32[16,128]{1,0:T(8,128)S(1)}) custom-call(s32[49]{0:T(128)S(1)} %pad_add_fusion.1.meta.refs_2_, bf16[2,3,512,512]{3,2,1,0:T(8,128)(2,1)S(1)} %copy-done.1, bf16[2,3,512,512]{3,2,1,0:T(8,128)(2,1)} %collective-permute-done.refs_0_, bf16[2,3,512,128]{3,2,1,0:T(8,128)(2,1)} %collective-permute-done.5.refs_1_, ...), custom_call_target="tpu_custom_call" | custom-call | flops 1207959552 | bytes 12582912 | tf_op jit(solution)/shard_map/expand2/pallas_call | solution.py:118
  56.4 4.2 %expand0.1 = (bf16[2,9,512,128]{3,2,1,0:T(8,128)(2,1)S(1)}, f32[16,128]{1,0:T(8,128)S(1)}) custom-call(s32[49]{0:T(128)S(1)} %pad_add_fusion.1.meta.refs_2_, bf16[2,3,512,512]{3,2,1,0:T(8,128)(2,1)S(1)} %copy-done.1, bf16[2,3,512,512]{3,2,1,0:T(8,128)(2,1)} %collective-permute-done.refs_0_, bf16[2,3,512,128]{3,2,1,0:T(8,128)(2,1)} %collective-permute-done.1.refs_1_.refs_0_, ...), custom_call_target="tpu_custom_call" | custom-call | flops 1207959552 | bytes 12582912 | tf_op jit(solution)/shard_map/expand0/pallas_call | solution.py:118
  60.6 8.2 %collective-permute-done.7.refs_1_ = bf16[2,3,512,128]{3,2,1,0:T(8,128)(2,1)} collective-permute-done((bf16[2,3,512,128]{3,2,1,0:T(8,128)(2,1)}, bf16[2,3,512,128]{3,2,1,0:T(8,128)(2,1)}, u32[]{:S(2)}, u32[]{:S(2)}) %collective-permute-start.7) | collective-permute-done | bytes 786464 | tf_op jit(solution)/shard_map/ppermute | solution.py:249
  68.8 4.2 %expand3.1 = (bf16[2,9,512,128]{3,2,1,0:T(8,128)(2,1)S(1)}, f32[16,128]{1,0:T(8,128)S(1)}) custom-call(s32[49]{0:T(128)S(1)} %pad_add_fusion.1.meta.refs_2_, bf16[2,3,512,512]{3,2,1,0:T(8,128)(2,1)S(1)} %copy-done.1, bf16[2,3,512,512]{3,2,1,0:T(8,128)(2,1)} %collective-permute-done.refs_0_, bf16[2,3,512,128]{3,2,1,0:T(8,128)(2,1)} %collective-permute-done.7.refs_1_, ...), custom_call_target="tpu_custom_call" | custom-call | flops 1207959552 | bytes 12582912 | tf_op jit(solution)/shard_map/expand3/pallas_call | solution.py:118
  73.0 1.3 %collective-permute-start.8 = (f32[12,512]{1,0:T(8,128)S(1)}, f32[12,512]{1,0:T(8,128)S(1)}, u32[]{:S(2)}, u32[]{:S(2)}) collective-permute-start(f32[12,512]{1,0:T(8,128)S(1)} %pad_maximum_fusion), channel_id=1, source_target_pairs={{0,1},{2,3},{4,5},{6,7},{8,9},{10,11},{12,13},{14,15},{16,17},{18,... | collective-permute-start | bytes 73736 | tf_op jit(solution)/shard_map/ppermute | solution.py:261
  74.3 0.9 collective-permute-done.8
  75.1 3.1 %collective-permute-start.10 = (f32[12,512]{1,0:T(8,128)S(1)}, f32[12,512]{1,0:T(8,128)S(1)}, u32[]{:S(2)}, u32[]{:S(2)}) collective-permute-start(f32[12,512]{1,0:T(8,128)S(1)} %fusion.2), channel_id=1, source_target_pairs={{1,4},{3,6},{5,8},{7,10},{9,12},{11,14},{13,16},{15,18},{17,20},{1... | collective-permute-start | bytes 73736 | tf_op jit(solution)/shard_map/ppermute | solution.py:263
  78.2 4.5 %collective-permute-start.9 = (f32[12,512]{1,0:T(8,128)S(1)}, f32[12,512]{1,0:T(8,128)S(1)}, u32[]{:S(2)}, u32[]{:S(2)}) collective-permute-start(f32[12,512]{1,0:T(8,128)S(1)} %fusion.2), channel_id=1, source_target_pairs={{1,2},{3,4},{5,6},{7,8},{9,10},{11,12},{13,14},{15,16},{17,18},{19... | collective-permute-start | bytes 73736 | tf_op jit(solution)/shard_map/ppermute | solution.py:262
  82.7 1.6 %collective-permute-done.9 = f32[12,512]{1,0:T(8,128)S(1)} collective-permute-done((f32[12,512]{1,0:T(8,128)S(1)}, f32[12,512]{1,0:T(8,128)S(1)}, u32[]{:S(2)}, u32[]{:S(2)}) %collective-permute-start.9) | collective-permute-done | bytes 24608 | tf_op jit(solution)/shard_map/ppermute | solution.py:262
  84.3 4.0 %collective-permute-start.11 = (f32[12,512]{1,0:T(8,128)S(1)}, f32[12,512]{1,0:T(8,128)S(1)}, u32[]{:S(2)}, u32[]{:S(2)}) collective-permute-start(f32[12,512]{1,0:T(8,128)S(1)} %add_select_fusion), channel_id=1, source_target_pairs={{0,1},{2,3},{4,5},{6,7},{8,9},{10,11},{12,13},{14,15},{16,17},{18,... | collective-permute-start | bytes 73736 | tf_op jit(solution)/shard_map/ppermute | solution.py:269
  88.3 0.9 collective-permute-done.11
  89.2 4.3 %inflate0.1 = bf16[2,9,512,512]{3,2,1,0:T(8,128)(2,1)} custom-call(s32[49]{0:T(128)S(1)} %pad_add_fusion.1.meta.refs_2_, f32[12,512]{1,0:T(8,128)S(1)} %add_add_fusion.totals, bf16[2,9,512,128]{3,2,1,0:T(8,128)(2,1)S(1)} %get-tuple-element.17.refs_0_, bf16[2,9,512,128]{3,2,1,0:T(8,128)(2,1)S(1)} %get-tuple-element.18.refs_1_, ...), custom_call_target="tpu_custom_call" | custom-call | flops 16777216 | bytes 16777216 | tf_op jit(solution)/shard_map/inflate0/pallas_call | solution.py:172
  (31 shorter events, 0.9 us)
Async XLA Ops:
  0.0 14.1 %collective-permute-start = (bf16[2,3,512,512]{3,2,1,0:T(8,128)(2,1)}, bf16[2,3,512,512]{3,2,1,0:T(8,128)(2,1)}, u32[]{:S(2)}, u32[]{:S(2)}) collective-permute-start(bf16[2,3,512,512]{3,2,1,0:T(8,128)(2,1)} %own.7), channel_id=1, source_target_pairs={{0,1},{2,3},{4,5},{6,7},{8,9},{10,11},{12,13},{14,15},{16,17},{18,... | collective-permute-start | bytes 9437192 | tf_op jit(solution)/shard_map/ppermute | solution.py:232
  0.7 12.2 %copy-start.2 = (s32[64,3]{0,1:T(4,128)S(1)}, s32[64,3]{0,1:T(4,128)}, u32[]{:S(2)}) copy-start(s32[64,3]{0,1:T(4,128)} %param.3) | copy-start | bytes 2308
  2.8 15.8 %collective-permute-start.3 = (bf16[2,3,512,128]{3,2,1,0:T(8,128)(2,1)}, bf16[2,3,512,128]{3,2,1,0:T(8,128)(2,1)}, u32[]{:S(2)}, u32[]{:S(2)}) collective-permute-start(bf16[2,3,512,128]{3,2,1,0:T(8,128)(2,1)} %slice.18), channel_id=1, source_target_pairs={{7,30},{16,0},{15,31},{24,1}} | collective-permute-start | bytes 2359304 | tf_op jit(solution)/shard_map/ppermute | solution.py:238
  4.3 15.8 %collective-permute-start.1 = (bf16[2,3,512,128]{3,2,1,0:T(8,128)(2,1)}, bf16[2,3,512,128]{3,2,1,0:T(8,128)(2,1)}, u32[]{:S(2)}, u32[]{:S(2)}) collective-permute-start(bf16[2,3,512,128]{3,2,1,0:T(8,128)(2,1)} %slice.18), channel_id=1, source_target_pairs={{1,2},{3,4},{5,6},{9,10},{11,12},{13,14},{17,18},{19,20},{21,22},{... | collective-permute-start | bytes 2359304 | tf_op jit(solution)/shard_map/ppermute | solution.py:239
  7.4 1.9 %copy-start = (bf16[2,3,512,512]{3,2,1,0:T(8,128)(2,1)S(1)}, bf16[2,3,512,512]{3,2,1,0:T(8,128)(2,1)}, u32[]{:S(2)}) copy-start(bf16[2,3,512,512]{3,2,1,0:T(8,128)(2,1)} %own.7) | copy-start | bytes 9437188
  9.3 4.8 %copy-start.1 = (bf16[2,3,512,512]{3,2,1,0:T(8,128)(2,1)S(1)}, bf16[2,3,512,512]{3,2,1,0:T(8,128)(2,1)}, u32[]{:S(2)}) copy-start(bf16[2,3,512,512]{3,2,1,0:T(8,128)(2,1)} %own.7) | copy-start | bytes 9437188
  10.2 25.1 %collective-permute-start.6 = (bf16[2,3,512,128]{3,2,1,0:T(8,128)(2,1)}, bf16[2,3,512,128]{3,2,1,0:T(8,128)(2,1)}, u32[]{:S(2)}, u32[]{:S(2)}) collective-permute-start(bf16[2,3,512,128]{3,2,1,0:T(8,128)(2,1)} %columns1.1), channel_id=1, source_target_pairs={{1,2},{3,4},{5,6},{7,8},{9,10},{11,12},{13,14},{15,16},{17,18},{19... | collective-permute-start | bytes 2359304 | tf_op jit(solution)/shard_map/ppermute | solution.py:249
  15.0 37.2 %collective-permute-start.5 = (bf16[2,3,512,128]{3,2,1,0:T(8,128)(2,1)}, bf16[2,3,512,128]{3,2,1,0:T(8,128)(2,1)}, u32[]{:S(2)}, u32[]{:S(2)}) collective-permute-start(bf16[2,3,512,128]{3,2,1,0:T(8,128)(2,1)} %columns2.1), channel_id=1, source_target_pairs={{1,2},{3,4},{5,6},{7,8},{9,10},{11,12},{13,14},{15,16},{17,18},{19... | collective-permute-start | bytes 2359304 | tf_op jit(solution)/shard_map/ppermute | solution.py:249
  18.5 37.9 %collective-permute-start.4 = (bf16[2,3,512,128]{3,2,1,0:T(8,128)(2,1)}, bf16[2,3,512,128]{3,2,1,0:T(8,128)(2,1)}, u32[]{:S(2)}, u32[]{:S(2)}) collective-permute-start(bf16[2,3,512,128]{3,2,1,0:T(8,128)(2,1)} %collective-permute-done.3.refs_1_), channel_id=1, source_target_pairs={{30,8},{0,15},{31,16},{1,23}} | collective-permute-start | bytes 2359304 | tf_op jit(solution)/shard_map/ppermute | solution.py:240
  20.1 36.3 %collective-permute-start.2 = (bf16[2,3,512,128]{3,2,1,0:T(8,128)(2,1)}, bf16[2,3,512,128]{3,2,1,0:T(8,128)(2,1)}, u32[]{:S(2)}, u32[]{:S(2)}) collective-permute-start(bf16[2,3,512,128]{3,2,1,0:T(8,128)(2,1)} %collective-permute-done.1.refs_1_.refs_0_), channel_id=1, source_target_pairs={{0,7},{31,24}} | collective-permute-start | bytes 2359304 | tf_op jit(solution)/shard_map/ppermute | solution.py:240
  22.6 46.2 %collective-permute-start.7 = (bf16[2,3,512,128]{3,2,1,0:T(8,128)(2,1)}, bf16[2,3,512,128]{3,2,1,0:T(8,128)(2,1)}, u32[]{:S(2)}, u32[]{:S(2)}) collective-permute-start(bf16[2,3,512,128]{3,2,1,0:T(8,128)(2,1)} %columns3.1), channel_id=1, source_target_pairs={{1,2},{3,4},{5,6},{7,8},{9,10},{11,12},{13,14},{15,16},{17,18},{19... | collective-permute-start | bytes 2359304 | tf_op jit(solution)/shard_map/ppermute | solution.py:249
  73.0 2.2 %collective-permute-start.8 = (f32[12,512]{1,0:T(8,128)S(1)}, f32[12,512]{1,0:T(8,128)S(1)}, u32[]{:S(2)}, u32[]{:S(2)}) collective-permute-start(f32[12,512]{1,0:T(8,128)S(1)} %pad_maximum_fusion), channel_id=1, source_target_pairs={{0,1},{2,3},{4,5},{6,7},{8,9},{10,11},{12,13},{14,15},{16,17},{18,... | collective-permute-start | bytes 73736 | tf_op jit(solution)/shard_map/ppermute | solution.py:261
  75.1 7.6 %collective-permute-start.10 = (f32[12,512]{1,0:T(8,128)S(1)}, f32[12,512]{1,0:T(8,128)S(1)}, u32[]{:S(2)}, u32[]{:S(2)}) collective-permute-start(f32[12,512]{1,0:T(8,128)S(1)} %fusion.2), channel_id=1, source_target_pairs={{1,4},{3,6},{5,8},{7,10},{9,12},{11,14},{13,16},{15,18},{17,20},{1... | collective-permute-start | bytes 73736 | tf_op jit(solution)/shard_map/ppermute | solution.py:263
  78.2 6.1 %collective-permute-start.9 = (f32[12,512]{1,0:T(8,128)S(1)}, f32[12,512]{1,0:T(8,128)S(1)}, u32[]{:S(2)}, u32[]{:S(2)}) collective-permute-start(f32[12,512]{1,0:T(8,128)S(1)} %fusion.2), channel_id=1, source_target_pairs={{1,2},{3,4},{5,6},{7,8},{9,10},{11,12},{13,14},{15,16},{17,18},{19... | collective-permute-start | bytes 73736 | tf_op jit(solution)/shard_map/ppermute | solution.py:262
  84.3 4.9 %collective-permute-start.11 = (f32[12,512]{1,0:T(8,128)S(1)}, f32[12,512]{1,0:T(8,128)S(1)}, u32[]{:S(2)}, u32[]{:S(2)}) collective-permute-start(f32[12,512]{1,0:T(8,128)S(1)} %add_select_fusion), channel_id=1, source_target_pairs={{0,1},{2,3},{4,5},{6,7},{8,9},{10,11},{12,13},{14,15},{16,17},{18,... | collective-permute-start | bytes 73736 | tf_op jit(solution)/shard_map/ppermute | solution.py:269

commit v4 on v3

--- a/solution.py
+++ b/solution.py
@@ -46,8 +46,8 @@
     for row in range(last_row):
         low, high = device(row, top, 1), device(row + 1, 0, 0)
         for source, target, spare, turn in ((high, low, spare_up, row), (low, high, spare_down, last_row - 1 - row)):
-            which = min(turn, 1)
-            stop = spare[max(turn - 1, 0)]
+            which = 0 if turn == last_row - 1 else 1
+            stop = spare[turn % 2]
             legs[which][0].append((source, stop))
             legs[which][1].append((stop, target))
             kinds[target] = which + 1
@@ -235,7 +235,7 @@
     if rows == 4:
         legs, kinds = detours(rows - 1, columns)
         straight = [pair for pair in next_chip if pair[1] not in kinds]
-        side_leg = lax.ppermute(pieces[0], AXES, legs[1][0])
+        side_leg = lax.ppermute(columns_of(matrix_tiles, 0, width, [pieces[1]]), AXES, legs[1][0])
         stops = [lax.ppermute(pieces[0], AXES, straight + legs[0][0]), side_leg]
         first = [stops[0]] + [lax.ppermute(stop, AXES, home_leg) for stop, (_, home_leg) in zip(stops, legs)]
         for target, number in kinds.items():

time: 94.1 us -> 92.7 us (0.985)
  waiting for transfers between devices: 34.2 us -> 30.4 us
  starting transfers between devices: 29.5 us -> 30.9 us
    ppermute x3, waiting for transfers between devices: 30.9 us -> 26.6 us  [body(): lax.ppermute(piece, AXES, next_chip)]
    ppermute x1, starting transfers between devices: 1.3 us -> 5.23 us  [body(): chip = window + lax.ppermute(window, AXES, swap)]
    ppermute x1, starting transfers between devices: 3.07 us -> 1.91 us  [body(): second = lax.ppermute(chip, AXES, second_chip)]
    ppermute x1, starting transfers between devices: 4.48 us -> 3.49 us  [body(): first = lax.ppermute(chip, AXES, next_chip)]
    pallas_call x3 -> x4, Pallas kernels: 2.74 us -> 3.67 us  [columns_of(): pl.pallas_call(functools.partial(columns_kernel, q, width), in_specs=[far...]
  transfers between devices with their start and end apart: 12 -> 12, of which waited for: 6 -> 7; matrix products, arithmetic and copies ran while one was open for 4% -> 4% of each run, Pallas kernels for 16% -> 18%
where the time goes in v4:
time: 92.7 us; the launch traced here: 92.3 us
  starting transfers between devices  30.9 us (33%)
  waiting for transfers between devices  30.4 us (33%)
  Pallas kernels  24.7 us (27%)
  local copies, waits for them, and re-layouts  5.34 us (6%)
    ppermute x3, waiting for transfers between devices, body(): lax.ppermute(piece, AXES, next_chip)  26.6 us
    pallas_call x4, Pallas kernels, expand(): pl.pallas_call(functools.partial(expand_kernel, q, rows_here, slots), in_...  16.7 us
    ppermute x3, starting transfers between devices, body(): lax.ppermute(piece, AXES, next_chip)  8.02 us
    ppermute x1, starting transfers between devices, body(): chip = window + lax.ppermute(window, AXES, swap)  5.23 us
    pallas_call x1, Pallas kernels, inflate(): pl.pallas_call(functools.partial(inflate_kernel, scale, slots, first), in...  4.35 us
    ppermute x1, starting transfers between devices, body(): totals = chip + gathered + lax.ppermute(gathered, AXES, swap)  3.71 us
    pallas_call x4, Pallas kernels, columns_of(): pl.pallas_call(functools.partial(columns_kernel, q, width), in_specs=[far...  3.67 us
    ppermute x1, starting transfers between devices, body(): first = lax.ppermute(chip, AXES, next_chip)  3.49 us
  transfers between devices with their start and end apart: 12, of which 7 were waited for; matrix products, arithmetic and copies ran while one was open for 4% of the time, Pallas kernels for 18%

profile of v4, /device:TPU:5, one launch (start us, length us, event | category | flops | bytes accessed | tf_op | source)
XLA Modules:
  0.0 92.3 jit_solution(3276499619337781374)
XLA Ops:
  0.0 0.7 collective-permute-start
  0.7 2.1 %slice.18 = bf16[2,3,512,128]{3,2,1,0:T(8,128)(2,1)} slice(bf16[2,3,512,512]{3,2,1,0:T(8,128)(2,1)} %own.7), slice={[0:2], [0:3], [0:512], [0:128]} | slice | bytes 1572864 | tf_op jit(solution)/shard_map/slice | solution.py:233
  2.7 3.1 %collective-permute-start.1 = (bf16[2,3,512,128]{3,2,1,0:T(8,128)(2,1)}, bf16[2,3,512,128]{3,2,1,0:T(8,128)(2,1)}, u32[]{:S(2)}, u32[]{:S(2)}) collective-permute-start(bf16[2,3,512,128]{3,2,1,0:T(8,128)(2,1)} %slice.18), channel_id=1, source_target_pairs={{1,2},{3,4},{5,6},{9,10},{11,12},{13,14},{17,18},{19,20},{21,22},{... | collective-permute-start | bytes 2359304 | tf_op jit(solution)/shard_map/ppermute | solution.py:239
  5.8 1.9 %copy-done = bf16[2,3,512,512]{3,2,1,0:T(8,128)(2,1)S(1)} copy-done((bf16[2,3,512,512]{3,2,1,0:T(8,128)(2,1)S(1)}, bf16[2,3,512,512]{3,2,1,0:T(8,128)(2,1)}, u32[]{:S(2)}) %copy-start) | copy-done | bytes 3145752
  7.7 0.9 columns1.1.refs_0_
  8.7 0.9 columns0.1
  9.6 1.7 %collective-permute-start.3 = (bf16[2,3,512,128]{3,2,1,0:T(8,128)(2,1)}, bf16[2,3,512,128]{3,2,1,0:T(8,128)(2,1)}, u32[]{:S(2)}, u32[]{:S(2)}) collective-permute-start(bf16[2,3,512,128]{3,2,1,0:T(8,128)(2,1)} %columns0.1), channel_id=1, source_target_pairs={{8,0},{16,1},{15,30},{23,31}} | collective-permute-start | bytes 2359304 | tf_op jit(solution)/shard_map/ppermute | solution.py:238
  11.3 2.5 %collective-permute-start.6 = (bf16[2,3,512,128]{3,2,1,0:T(8,128)(2,1)}, bf16[2,3,512,128]{3,2,1,0:T(8,128)(2,1)}, u32[]{:S(2)}, u32[]{:S(2)}) collective-permute-start(bf16[2,3,512,128]{3,2,1,0:T(8,128)(2,1)} %columns1.1.refs_0_), channel_id=1, source_target_pairs={{1,2},{3,4},{5,6},{7,8},{9,10},{11,12},{13,14},{15,16},{17,18},{19... | collective-permute-start | bytes 2359304 | tf_op jit(solution)/shard_map/ppermute | solution.py:249
  14.0 0.6 gather_fusion
  15.0 1.0 %columns2.1 = bf16[2,3,512,128]{3,2,1,0:T(8,128)(2,1)} custom-call(bf16[2,3,512,512]{3,2,1,0:T(8,128)(2,1)S(1)} %copy-done.1, bf16[2,3,512,512]{3,2,1,0:T(8,128)(2,1)} %collective-permute-done.refs_0_), custom_call_target="tpu_custom_call" | custom-call | bytes 1048576 | tf_op jit(solution)/shard_map/columns2/pallas_call | solution.py:197
  16.0 3.1 %collective-permute-start.5 = (bf16[2,3,512,128]{3,2,1,0:T(8,128)(2,1)}, bf16[2,3,512,128]{3,2,1,0:T(8,128)(2,1)}, u32[]{:S(2)}, u32[]{:S(2)}) collective-permute-start(bf16[2,3,512,128]{3,2,1,0:T(8,128)(2,1)} %columns2.1), channel_id=1, source_target_pairs={{1,2},{3,4},{5,6},{7,8},{9,10},{11,12},{13,14},{15,16},{17,18},{19... | collective-permute-start | bytes 2359304 | tf_op jit(solution)/shard_map/ppermute | solution.py:249
  19.1 0.3 fusion
  19.5 1.6 %collective-permute-start.2 = (bf16[2,3,512,128]{3,2,1,0:T(8,128)(2,1)}, bf16[2,3,512,128]{3,2,1,0:T(8,128)(2,1)}, u32[]{:S(2)}, u32[]{:S(2)}) collective-permute-start(bf16[2,3,512,128]{3,2,1,0:T(8,128)(2,1)} %collective-permute-done.1.refs_1_.refs_0_), channel_id=1, source_target_pairs={{31,8},{0,23}} | collective-permute-start | bytes 2359304 | tf_op jit(solution)/shard_map/ppermute | solution.py:240
  21.1 1.6 %collective-permute-start.4 = (bf16[2,3,512,128]{3,2,1,0:T(8,128)(2,1)}, bf16[2,3,512,128]{3,2,1,0:T(8,128)(2,1)}, u32[]{:S(2)}, u32[]{:S(2)}) collective-permute-start(bf16[2,3,512,128]{3,2,1,0:T(8,128)(2,1)} %collective-permute-done.3.refs_1_), channel_id=1, source_target_pairs={{0,7},{1,15},{30,16},{31,24}} | collective-permute-start | bytes 2359304 | tf_op jit(solution)/shard_map/ppermute | solution.py:240
  22.6 0.9 columns3.1
  23.5 2.5 %collective-permute-start.7 = (bf16[2,3,512,128]{3,2,1,0:T(8,128)(2,1)}, bf16[2,3,512,128]{3,2,1,0:T(8,128)(2,1)}, u32[]{:S(2)}, u32[]{:S(2)}) collective-permute-start(bf16[2,3,512,128]{3,2,1,0:T(8,128)(2,1)} %columns3.1), channel_id=1, source_target_pairs={{1,2},{3,4},{5,6},{7,8},{9,10},{11,12},{13,14},{15,16},{17,18},{19... | collective-permute-start | bytes 2359304 | tf_op jit(solution)/shard_map/ppermute | solution.py:249
  26.3 5.5 %collective-permute-done.6.refs_1_ = bf16[2,3,512,128]{3,2,1,0:T(8,128)(2,1)} collective-permute-done((bf16[2,3,512,128]{3,2,1,0:T(8,128)(2,1)}, bf16[2,3,512,128]{3,2,1,0:T(8,128)(2,1)}, u32[]{:S(2)}, u32[]{:S(2)}) %collective-permute-start.6) | collective-permute-done | bytes 786464 | tf_op jit(solution)/shard_map/ppermute | solution.py:249
  31.7 4.2 %expand1.1 = (bf16[2,9,512,128]{3,2,1,0:T(8,128)(2,1)S(1)}, f32[16,128]{1,0:T(8,128)S(1)}) custom-call(s32[49]{0:T(128)S(1)} %pad_add_fusion.1.meta.refs_2_, bf16[2,3,512,512]{3,2,1,0:T(8,128)(2,1)S(1)} %copy-done.1, bf16[2,3,512,512]{3,2,1,0:T(8,128)(2,1)} %collective-permute-done.refs_0_, bf16[2,3,512,128]{3,2,1,0:T(8,128)(2,1)} %collective-permute-done.6.refs_1_, ...), custom_call_target="tpu_custom_call" | custom-call | flops 1207959552 | bytes 12582912 | tf_op jit(solution)/shard_map/expand1/pallas_call | solution.py:118
  35.9 12.7 %collective-permute-done.5.refs_1_ = bf16[2,3,512,128]{3,2,1,0:T(8,128)(2,1)} collective-permute-done((bf16[2,3,512,128]{3,2,1,0:T(8,128)(2,1)}, bf16[2,3,512,128]{3,2,1,0:T(8,128)(2,1)}, u32[]{:S(2)}, u32[]{:S(2)}) %collective-permute-start.5) | collective-permute-done | bytes 786464 | tf_op jit(solution)/shard_map/ppermute | solution.py:249
  48.6 4.2 %expand2.1 = (bf16[2,9,512,128]{3,2,1,0:T(8,128)(2,1)S(1)}, f32[16,128]{1,0:T(8,128)S(1)}) custom-call(s32[49]{0:T(128)S(1)} %pad_add_fusion.1.meta.refs_2_, bf16[2,3,512,512]{3,2,1,0:T(8,128)(2,1)S(1)} %copy-done.1, bf16[2,3,512,512]{3,2,1,0:T(8,128)(2,1)} %collective-permute-done.refs_0_, bf16[2,3,512,128]{3,2,1,0:T(8,128)(2,1)} %collective-permute-done.5.refs_1_, ...), custom_call_target="tpu_custom_call" | custom-call | flops 1207959552 | bytes 12582912 | tf_op jit(solution)/shard_map/expand2/pallas_call | solution.py:118
  52.8 4.2 %expand0.1 = (bf16[2,9,512,128]{3,2,1,0:T(8,128)(2,1)S(1)}, f32[16,128]{1,0:T(8,128)S(1)}) custom-call(s32[49]{0:T(128)S(1)} %pad_add_fusion.1.meta.refs_2_, bf16[2,3,512,512]{3,2,1,0:T(8,128)(2,1)S(1)} %copy-done.1, bf16[2,3,512,512]{3,2,1,0:T(8,128)(2,1)} %collective-permute-done.refs_0_, bf16[2,3,512,128]{3,2,1,0:T(8,128)(2,1)} %collective-permute-done.1.refs_1_.refs_0_, ...), custom_call_target="tpu_custom_call" | custom-call | flops 1207959552 | bytes 12582912 | tf_op jit(solution)/shard_map/expand0/pallas_call | solution.py:118
  57.0 8.5 %collective-permute-done.7.refs_1_ = bf16[2,3,512,128]{3,2,1,0:T(8,128)(2,1)} collective-permute-done((bf16[2,3,512,128]{3,2,1,0:T(8,128)(2,1)}, bf16[2,3,512,128]{3,2,1,0:T(8,128)(2,1)}, u32[]{:S(2)}, u32[]{:S(2)}) %collective-permute-start.7) | collective-permute-done | bytes 786464 | tf_op jit(solution)/shard_map/ppermute | solution.py:249
  65.4 4.2 %expand3.1 = (bf16[2,9,512,128]{3,2,1,0:T(8,128)(2,1)S(1)}, f32[16,128]{1,0:T(8,128)S(1)}) custom-call(s32[49]{0:T(128)S(1)} %pad_add_fusion.1.meta.refs_2_, bf16[2,3,512,512]{3,2,1,0:T(8,128)(2,1)S(1)} %copy-done.1, bf16[2,3,512,512]{3,2,1,0:T(8,128)(2,1)} %collective-permute-done.refs_0_, bf16[2,3,512,128]{3,2,1,0:T(8,128)(2,1)} %collective-permute-done.7.refs_1_, ...), custom_call_target="tpu_custom_call" | custom-call | flops 1207959552 | bytes 12582912 | tf_op jit(solution)/shard_map/expand3/pallas_call | solution.py:118
  69.6 5.2 %collective-permute-start.8 = (f32[12,512]{1,0:T(8,128)S(1)}, f32[12,512]{1,0:T(8,128)S(1)}, u32[]{:S(2)}, u32[]{:S(2)}) collective-permute-start(f32[12,512]{1,0:T(8,128)S(1)} %pad_maximum_fusion), channel_id=1, source_target_pairs={{0,1},{2,3},{4,5},{6,7},{8,9},{10,11},{12,13},{14,15},{16,17},{18,... | collective-permute-start | bytes 73736 | tf_op jit(solution)/shard_map/ppermute | solution.py:261
  74.9 0.9 collective-permute-done.8
  75.7 1.9 %collective-permute-start.10 = (f32[12,512]{1,0:T(8,128)S(1)}, f32[12,512]{1,0:T(8,128)S(1)}, u32[]{:S(2)}, u32[]{:S(2)}) collective-permute-start(f32[12,512]{1,0:T(8,128)S(1)} %fusion.2), channel_id=1, source_target_pairs={{1,4},{3,6},{5,8},{7,10},{9,12},{11,14},{13,16},{15,18},{17,20},{1... | collective-permute-start | bytes 73736 | tf_op jit(solution)/shard_map/ppermute | solution.py:263
  77.6 3.5 %collective-permute-start.9 = (f32[12,512]{1,0:T(8,128)S(1)}, f32[12,512]{1,0:T(8,128)S(1)}, u32[]{:S(2)}, u32[]{:S(2)}) collective-permute-start(f32[12,512]{1,0:T(8,128)S(1)} %fusion.2), channel_id=1, source_target_pairs={{1,2},{3,4},{5,6},{7,8},{9,10},{11,12},{13,14},{15,16},{17,18},{19... | collective-permute-start | bytes 73736 | tf_op jit(solution)/shard_map/ppermute | solution.py:262
  81.1 0.7 collective-permute-done.10
  81.8 1.3 %collective-permute-done.9 = f32[12,512]{1,0:T(8,128)S(1)} collective-permute-done((f32[12,512]{1,0:T(8,128)S(1)}, f32[12,512]{1,0:T(8,128)S(1)}, u32[]{:S(2)}, u32[]{:S(2)}) %collective-permute-start.9) | collective-permute-done | bytes 24608 | tf_op jit(solution)/shard_map/ppermute | solution.py:262
  83.2 3.7 %collective-permute-start.11 = (f32[12,512]{1,0:T(8,128)S(1)}, f32[12,512]{1,0:T(8,128)S(1)}, u32[]{:S(2)}, u32[]{:S(2)}) collective-permute-start(f32[12,512]{1,0:T(8,128)S(1)} %add_select_fusion), channel_id=1, source_target_pairs={{0,1},{2,3},{4,5},{6,7},{8,9},{10,11},{12,13},{14,15},{16,17},{18,... | collective-permute-start | bytes 73736 | tf_op jit(solution)/shard_map/ppermute | solution.py:269
  86.9 0.9 collective-permute-done.11
  87.8 4.3 %inflate0.1 = bf16[2,9,512,512]{3,2,1,0:T(8,128)(2,1)} custom-call(s32[49]{0:T(128)S(1)} %pad_add_fusion.1.meta.refs_2_, f32[12,512]{1,0:T(8,128)S(1)} %add_add_fusion.totals, bf16[2,9,512,128]{3,2,1,0:T(8,128)(2,1)S(1)} %get-tuple-element.17.refs_0_, bf16[2,9,512,128]{3,2,1,0:T(8,128)(2,1)S(1)} %get-tuple-element.18.refs_1_, ...), custom_call_target="tpu_custom_call" | custom-call | flops 16777216 | bytes 16777216 | tf_op jit(solution)/shard_map/inflate0/pallas_call | solution.py:172
  (32 shorter events, 1.1 us)
Async XLA Ops:
  0.0 15.0 %collective-permute-start = (bf16[2,3,512,512]{3,2,1,0:T(8,128)(2,1)}, bf16[2,3,512,512]{3,2,1,0:T(8,128)(2,1)}, u32[]{:S(2)}, u32[]{:S(2)}) collective-permute-start(bf16[2,3,512,512]{3,2,1,0:T(8,128)(2,1)} %own.7), channel_id=1, source_target_pairs={{0,1},{2,3},{4,5},{6,7},{8,9},{10,11},{12,13},{14,15},{16,17},{18,... | collective-permute-start | bytes 9437192 | tf_op jit(solution)/shard_map/ppermute | solution.py:232
  2.7 16.7 %collective-permute-start.1 = (bf16[2,3,512,128]{3,2,1,0:T(8,128)(2,1)}, bf16[2,3,512,128]{3,2,1,0:T(8,128)(2,1)}, u32[]{:S(2)}, u32[]{:S(2)}) collective-permute-start(bf16[2,3,512,128]{3,2,1,0:T(8,128)(2,1)} %slice.18), channel_id=1, source_target_pairs={{1,2},{3,4},{5,6},{9,10},{11,12},{13,14},{17,18},{19,20},{21,22},{... | collective-permute-start | bytes 2359304 | tf_op jit(solution)/shard_map/ppermute | solution.py:239
  5.8 1.9 %copy-start = (bf16[2,3,512,512]{3,2,1,0:T(8,128)(2,1)S(1)}, bf16[2,3,512,512]{3,2,1,0:T(8,128)(2,1)}, u32[]{:S(2)}) copy-start(bf16[2,3,512,512]{3,2,1,0:T(8,128)(2,1)} %own.7) | copy-start | bytes 9437188
  8.6 5.1 %copy-start.2 = (s32[64,3]{0,1:T(4,128)S(1)}, s32[64,3]{0,1:T(4,128)}, u32[]{:S(2)}) copy-start(s32[64,3]{0,1:T(4,128)} %param.3) | copy-start | bytes 2308
  8.6 6.3 %copy-start.1 = (bf16[2,3,512,512]{3,2,1,0:T(8,128)(2,1)S(1)}, bf16[2,3,512,512]{3,2,1,0:T(8,128)(2,1)}, u32[]{:S(2)}) copy-start(bf16[2,3,512,512]{3,2,1,0:T(8,128)(2,1)} %own.7) | copy-start | bytes 9437188
  9.6 11.5 %collective-permute-start.3 = (bf16[2,3,512,128]{3,2,1,0:T(8,128)(2,1)}, bf16[2,3,512,128]{3,2,1,0:T(8,128)(2,1)}, u32[]{:S(2)}, u32[]{:S(2)}) collective-permute-start(bf16[2,3,512,128]{3,2,1,0:T(8,128)(2,1)} %columns0.1), channel_id=1, source_target_pairs={{8,0},{16,1},{15,30},{23,31}} | collective-permute-start | bytes 2359304 | tf_op jit(solution)/shard_map/ppermute | solution.py:238
  11.3 20.5 %collective-permute-start.6 = (bf16[2,3,512,128]{3,2,1,0:T(8,128)(2,1)}, bf16[2,3,512,128]{3,2,1,0:T(8,128)(2,1)}, u32[]{:S(2)}, u32[]{:S(2)}) collective-permute-start(bf16[2,3,512,128]{3,2,1,0:T(8,128)(2,1)} %columns1.1.refs_0_), channel_id=1, source_target_pairs={{1,2},{3,4},{5,6},{7,8},{9,10},{11,12},{13,14},{15,16},{17,18},{19... | collective-permute-start | bytes 2359304 | tf_op jit(solution)/shard_map/ppermute | solution.py:249
  16.0 32.6 %collective-permute-start.5 = (bf16[2,3,512,128]{3,2,1,0:T(8,128)(2,1)}, bf16[2,3,512,128]{3,2,1,0:T(8,128)(2,1)}, u32[]{:S(2)}, u32[]{:S(2)}) collective-permute-start(bf16[2,3,512,128]{3,2,1,0:T(8,128)(2,1)} %columns2.1), channel_id=1, source_target_pairs={{1,2},{3,4},{5,6},{7,8},{9,10},{11,12},{13,14},{15,16},{17,18},{19... | collective-permute-start | bytes 2359304 | tf_op jit(solution)/shard_map/ppermute | solution.py:249
  19.5 33.3 %collective-permute-start.2 = (bf16[2,3,512,128]{3,2,1,0:T(8,128)(2,1)}, bf16[2,3,512,128]{3,2,1,0:T(8,128)(2,1)}, u32[]{:S(2)}, u32[]{:S(2)}) collective-permute-start(bf16[2,3,512,128]{3,2,1,0:T(8,128)(2,1)} %collective-permute-done.1.refs_1_.refs_0_), channel_id=1, source_target_pairs={{31,8},{0,23}} | collective-permute-start | bytes 2359304 | tf_op jit(solution)/shard_map/ppermute | solution.py:240
  21.1 31.7 %collective-permute-start.4 = (bf16[2,3,512,128]{3,2,1,0:T(8,128)(2,1)}, bf16[2,3,512,128]{3,2,1,0:T(8,128)(2,1)}, u32[]{:S(2)}, u32[]{:S(2)}) collective-permute-start(bf16[2,3,512,128]{3,2,1,0:T(8,128)(2,1)} %collective-permute-done.3.refs_1_), channel_id=1, source_target_pairs={{0,7},{1,15},{30,16},{31,24}} | collective-permute-start | bytes 2359304 | tf_op jit(solution)/shard_map/ppermute | solution.py:240
  23.5 41.9 %collective-permute-start.7 = (bf16[2,3,512,128]{3,2,1,0:T(8,128)(2,1)}, bf16[2,3,512,128]{3,2,1,0:T(8,128)(2,1)}, u32[]{:S(2)}, u32[]{:S(2)}) collective-permute-start(bf16[2,3,512,128]{3,2,1,0:T(8,128)(2,1)} %columns3.1), channel_id=1, source_target_pairs={{1,2},{3,4},{5,6},{7,8},{9,10},{11,12},{13,14},{15,16},{17,18},{19... | collective-permute-start | bytes 2359304 | tf_op jit(solution)/shard_map/ppermute | solution.py:249
  69.6 6.1 %collective-permute-start.8 = (f32[12,512]{1,0:T(8,128)S(1)}, f32[12,512]{1,0:T(8,128)S(1)}, u32[]{:S(2)}, u32[]{:S(2)}) collective-permute-start(f32[12,512]{1,0:T(8,128)S(1)} %pad_maximum_fusion), channel_id=1, source_target_pairs={{0,1},{2,3},{4,5},{6,7},{8,9},{10,11},{12,13},{14,15},{16,17},{18,... | collective-permute-start | bytes 73736 | tf_op jit(solution)/shard_map/ppermute | solution.py:261
  75.7 6.1 %collective-permute-start.10 = (f32[12,512]{1,0:T(8,128)S(1)}, f32[12,512]{1,0:T(8,128)S(1)}, u32[]{:S(2)}, u32[]{:S(2)}) collective-permute-start(f32[12,512]{1,0:T(8,128)S(1)} %fusion.2), channel_id=1, source_target_pairs={{1,4},{3,6},{5,8},{7,10},{9,12},{11,14},{13,16},{15,18},{17,20},{1... | collective-permute-start | bytes 73736 | tf_op jit(solution)/shard_map/ppermute | solution.py:263
  77.6 5.5 %collective-permute-start.9 = (f32[12,512]{1,0:T(8,128)S(1)}, f32[12,512]{1,0:T(8,128)S(1)}, u32[]{:S(2)}, u32[]{:S(2)}) collective-permute-start(f32[12,512]{1,0:T(8,128)S(1)} %fusion.2), channel_id=1, source_target_pairs={{1,2},{3,4},{5,6},{7,8},{9,10},{11,12},{13,14},{15,16},{17,18},{19... | collective-permute-start | bytes 73736 | tf_op jit(solution)/shard_map/ppermute | solution.py:262
  83.2 4.6 %collective-permute-start.11 = (f32[12,512]{1,0:T(8,128)S(1)}, f32[12,512]{1,0:T(8,128)S(1)}, u32[]{:S(2)}, u32[]{:S(2)}) collective-permute-start(f32[12,512]{1,0:T(8,128)S(1)} %add_select_fusion), channel_id=1, source_target_pairs={{0,1},{2,3},{4,5},{6,7},{8,9},{10,11},{12,13},{14,15},{16,17},{18,... | collective-permute-start | bytes 73736 | tf_op jit(solution)/shard_map/ppermute | solution.py:269

commit v5 on v4

--- a/solution.py
+++ b/solution.py
@@ -10,7 +10,7 @@
 W = 2
 AXES = ("row", "col", "depth")
 CHUNKS = 4
-FIELDS = 24
+FIELDS = 33
 
 
 def both_ways(pairs):
@@ -31,7 +31,9 @@
     matched = out_cols[:, :, None] == out_cols[:, None, :]
     lead = jnp.min(jnp.where(matched, positions[None, None, :], slots * slots), axis=2)
     window = out_cols - (start - core * rows_here - 2 * W)
-    scalars = jnp.concatenate([source, line, lead, window], axis=1).astype(jnp.int32).reshape(-1)
+    far = jnp.repeat(source == 2, slots, axis=1)
+    touched = jnp.any(far[:, :, None] & (lead[:, :, None] == positions[None, None, :]), axis=1)
+    scalars = jnp.concatenate([source, line, lead, window, touched], axis=1).astype(jnp.int32).reshape(-1)
     return jnp.concatenate([scalars, kind.astype(jnp.int32)[None]])
 
 
@@ -109,6 +111,110 @@
 
         for slot in range(slots * (slots - 1)):
             finish(r, slot, acc[r, slot])
+
+
+def split_kernel(q, rows_here, slots, late, meta, own, *refs):
+    slot_total = slots * slots
+    width = refs[0].shape[3] if late else refs[2].shape[3]
+    cols = pl.ds(q * width, width)
+    if late:
+        acc_before, out_before, win_before = refs[:3]
+        out, win, acc, right, sems = refs[-5:]
+        across = refs[3:-6]
+    else:
+        beside = refs[0]
+        acc, out, win, right, sems = refs[-5:]
+    sources, lines = {}, {}
+    jobs = [(r, s) for r in range(rows_here) for s in range(1, slots)]
+    for job, (r, s) in enumerate(jobs):
+        source, line = meta[r * FIELDS + s], meta[r * FIELDS + slots + s]
+        if late:
+            mine = source == 2
+            which = meta[rows_here * FIELDS] if len(across) > 1 else 0
+            places = [(mine & (which == number), part.at[line]) for number, part in enumerate(across)]
+        else:
+            mine = source != 2
+            places = [(source == 0, own.at[line, :, :, cols]), (source == 1, beside.at[line, :, :, cols])]
+        sources[job] = mine
+        for chosen, place in places:
+
+            @pl.when(chosen)
+            def _():
+                pltpu.make_async_copy(place, right.at[job], sems.at[job]).start()
+
+    def field(r, group, slot):
+        return meta[r * FIELDS + 2 * slots + group * slot_total + slot]
+
+    def product(r, s, tiles):
+        return jnp.dot(own[r, s], jnp.concatenate(tiles, axis=1), preferred_element_type=jnp.float32)
+
+    def finish(r, slot):
+        values = acc[r, slot].astype(jnp.bfloat16)
+        out[r, slot] = values
+        wide = values.astype(jnp.float32)
+        win[pl.ds(field(r, 1, slot), 1), :] += jnp.sum(wide * wide, axis=0, keepdims=True)
+
+    if late:
+        win[...] = win_before[...]
+        for r in range(rows_here):
+            for slot in range(slot_total):
+                touched = field(r, 2, slot) == 1
+
+                @pl.when(touched)
+                def _():
+                    acc[r, slot] = acc_before[r, slot]
+
+                @pl.when(jnp.logical_not(touched))
+                def _():
+                    out[r, slot] = out_before[r, slot]
+    else:
+        win[...] = jnp.zeros_like(win)
+        for r in range(rows_here):
+            first = product(r, 0, [own[r, t, :, cols] for t in range(slots)])
+            for t in range(slots):
+                acc[r, t] = first[:, t * width : (t + 1) * width]
+            for slot in range(slots, slot_total):
+                acc[r, slot] = jnp.zeros((acc.shape[2], width), jnp.float32)
+    for job, (r, s) in enumerate(jobs):
+
+        @pl.when(sources[job])
+        def _():
+            here = right.at[job]
+            pltpu.make_async_copy(here, here, sems.at[job]).wait()
+            later = product(r, s, [right[job, t] for t in range(slots)])
+            for t in range(slots):
+                acc[r, field(r, 0, s * slots + t)] += later[:, t * width : (t + 1) * width]
+
+    for r in range(rows_here):
+        for slot in range(slot_total):
+
+            @pl.when(field(r, 2, slot) == (1 if late else 0))
+            def _():
+                finish(r, slot)
+
+
+def expand_split(q, late, meta, own, inputs, before, width):
+    rows_here, slots, side, _ = own.shape
+    vmem, anywhere = pl.BlockSpec(memory_space=pltpu.VMEM), pl.BlockSpec(memory_space=pl.ANY)
+    jobs = rows_here * (slots - 1)
+    acc = jax.ShapeDtypeStruct((rows_here, slots * slots, side, width), jnp.float32)
+    outs = [jax.ShapeDtypeStruct(acc.shape, jnp.bfloat16), jax.ShapeDtypeStruct((16, width), jnp.float32)]
+    specs = [vmem] * 3 + [anywhere] * (len(inputs) - 3) if late else [anywhere] * len(inputs)
+    return pl.pallas_call(
+        functools.partial(split_kernel, q, rows_here, slots, late),
+        in_specs=[pl.BlockSpec(memory_space=pltpu.SMEM), vmem] + specs + [anywhere],
+        out_specs=[vmem] * (2 if late else 3),
+        out_shape=outs if late else [acc] + outs,
+        scratch_shapes=([pltpu.VMEM(acc.shape, jnp.float32)] if late else [])
+        + [pltpu.VMEM((jobs, slots, side, width), jnp.bfloat16), pltpu.SemaphoreType.DMA((jobs,))],
+        compiler_params=pltpu.CompilerParams(vmem_limit_bytes=12 * 2**20),
+        cost_estimate=pl.CostEstimate(
+            flops=rows_here * slots * slots * side * side * width,
+            bytes_accessed=8 * 2**20,
+            transcendentals=0,
+        ),
+        name=f"{'late' if late else 'early'}{q}",
+    )(meta, own, *inputs, before)
 
 
 def expand(q, meta, own, beside, across, before):
@@ -230,7 +336,9 @@
     here = lax.axis_index(AXES)
     rows, columns = lax.axis_size("row"), lax.axis_size("col")
     beside = lax.ppermute(matrix_tiles, AXES, swap)
-    pieces = [matrix_tiles[..., :width]] + [columns_of(matrix_tiles, q, width, [beside] * (q == 2)) for q in range(1, CHUNKS - 1)]
+    pieces = [matrix_tiles[..., :width]]
+    pieces.append(columns_of(matrix_tiles, 1, width, [pieces[0]]))
+    pieces.append(columns_of(matrix_tiles, 2, width, [beside, pieces[1]]))
     kind = jnp.int32(0)
     if rows == 4:
         legs, kinds = detours(rows - 1, columns)
@@ -240,18 +348,28 @@
         first = [stops[0]] + [lax.ppermute(stop, AXES, home_leg) for stop, (_, home_leg) in zip(stops, legs)]
         for target, number in kinds.items():
             kind = jnp.where(here == target, number, kind)
-        pieces.append(columns_of(matrix_tiles, CHUNKS - 1, width, stops))
+        follow = stops
         order = [*range(1, CHUNKS - 1), 0, CHUNKS - 1]
     else:
         first = [lax.ppermute(pieces[0], AXES, next_chip)]
-        pieces.append(columns_of(matrix_tiles, CHUNKS - 1, width, first))
+        follow = first
         order = [*range(CHUNKS)]
     across = [first] + [[lax.ppermute(piece, AXES, next_chip)] for piece in pieces[1:]]
     meta = plan(pattern, start, rows_here, core, kind)
     parts, windows = [None] * CHUNKS, [None] * CHUNKS
     before = meta
-    for q in order:
+    halves = {}
+    for q in order[:-2]:
         parts[q], windows[q] = expand(q, meta, matrix_tiles, beside, across[q], before)
+        before = windows[q]
+        if q == order[0]:
+            last = columns_of(matrix_tiles, CHUNKS - 1, width, [before, *follow])
+            across.append([lax.ppermute(last, AXES, next_chip)])
+        split = order[-1] if q == order[0] else order[-2]
+        halves[split] = expand_split(split, False, meta, matrix_tiles, [beside], before, width)
+        before = halves[split][2]
+    for q in order[-2:]:
+        parts[q], windows[q] = expand_split(q, True, meta, matrix_tiles, [*halves[q], *across[q]], before, width)
         before = windows[q]
     window = jnp.concatenate(windows, axis=1)
 

time: 92.7 us -> 91.2 us (0.984)
  Pallas kernels: 24.7 us -> 28.8 us
  starting transfers between devices: 30.9 us -> 27.5 us
  waiting for transfers between devices: 30.4 us -> 27.7 us
    pallas_call x0 -> x4, Pallas kernels: none -> 13.2 us  [expand_split(): pl.pallas_call(functools.partial(split_kernel, q, rows_here, slots, late)...]
    pallas_call x4 -> x2, Pallas kernels: 16.7 us -> 8.33 us  [expand(): pl.pallas_call(functools.partial(expand_kernel, q, rows_here, slots), in_...]
    ppermute x3 -> x2, waiting for transfers between devices: 26.6 us -> 19.8 us  [body(): lax.ppermute(piece, AXES, next_chip)]
    ppermute x1, starting transfers between devices: 5.23 us -> 0.07 us  [body(): chip = window + lax.ppermute(window, AXES, swap)]
    ppermute x0 -> x1, waiting for transfers between devices: none -> 4.51 us  [body(): across.append([lax.ppermute(last, AXES, next_chip)])]
    ppermute x3 -> x2, starting transfers between devices: 8.02 us -> 5.7 us  [body(): lax.ppermute(piece, AXES, next_chip)]
    ppermute x1, starting transfers between devices: 1.91 us -> 4.15 us  [body(): second = lax.ppermute(chip, AXES, second_chip)]
    ppermute x0 -> x1, starting transfers between devices: none -> 1.98 us  [body(): across.append([lax.ppermute(last, AXES, next_chip)])]
  transfers between devices with their start and end apart: 12 -> 12, of which waited for: 7 -> 6; matrix products, arithmetic and copies ran while one was open for 4% -> 5% of each run, Pallas kernels for 18% -> 24%
where the time goes in v5:
time: 91.2 us; the launch traced here: 90.8 us
  Pallas kernels  28.8 us (32%)
  waiting for transfers between devices  27.7 us (30%)
  starting transfers between devices  27.5 us (30%)
  local copies, waits for them, and re-layouts  5.59 us (6%)
    ppermute x2, waiting for transfers between devices, body(): lax.ppermute(piece, AXES, next_chip)  19.8 us
    pallas_call x4, Pallas kernels, expand_split(): pl.pallas_call(functools.partial(split_kernel, q, rows_here, slots, late)...  13.2 us
    pallas_call x2, Pallas kernels, expand(): pl.pallas_call(functools.partial(expand_kernel, q, rows_here, slots), in_...  8.33 us
    ppermute x2, starting transfers between devices, body(): lax.ppermute(piece, AXES, next_chip)  5.7 us
    ppermute x1, starting transfers between devices, body(): totals = chip + gathered + lax.ppermute(gathered, AXES, swap)  4.55 us
    ppermute x1, waiting for transfers between devices, body(): across.append([lax.ppermute(last, AXES, next_chip)])  4.51 us
    ppermute x1, starting transfers between devices, body(): first = lax.ppermute(chip, AXES, next_chip)  4.35 us
    pallas_call x1, Pallas kernels, inflate(): pl.pallas_call(functools.partial(inflate_kernel, scale, slots, first), in...  4.35 us
  transfers between devices with their start and end apart: 12, of which 6 were waited for; matrix products, arithmetic and copies ran while one was open for 5% of the time, Pallas kernels for 24%

profile of v5, /device:TPU:5, one launch (start us, length us, event | category | flops | bytes accessed | tf_op | source)
XLA Modules:
  0.0 90.8 jit_solution(14430949648081366730)
XLA Ops:
  0.0 0.7 collective-permute-start
  0.7 2.1 %slice.18.refs_0_ = bf16[2,3,512,128]{3,2,1,0:T(8,128)(2,1)} slice(bf16[2,3,512,512]{3,2,1,0:T(8,128)(2,1)} %own.11), slice={[0:2], [0:3], [0:512], [0:128]} | slice | bytes 1572864 | tf_op jit(solution)/shard_map/slice | solution.py:339
  2.7 3.1 %collective-permute-start.3 = (bf16[2,3,512,128]{3,2,1,0:T(8,128)(2,1)}, bf16[2,3,512,128]{3,2,1,0:T(8,128)(2,1)}, u32[]{:S(2)}, u32[]{:S(2)}) collective-permute-start(bf16[2,3,512,128]{3,2,1,0:T(8,128)(2,1)} %slice.18.refs_0_), channel_id=1, source_target_pairs={{1,2},{3,4},{5,6},{9,10},{11,12},{13,14},{17,18},{19,20},{21,22},{... | collective-permute-start | bytes 2359304 | tf_op jit(solution)/shard_map/ppermute | solution.py:347
  5.8 1.9 %copy-done = bf16[2,3,512,512]{3,2,1,0:T(8,128)(2,1)S(1)} copy-done((bf16[2,3,512,512]{3,2,1,0:T(8,128)(2,1)S(1)}, bf16[2,3,512,512]{3,2,1,0:T(8,128)(2,1)}, u32[]{:S(2)}) %copy-start) | copy-done | bytes 3145752
  7.7 0.9 %columns1.1.refs_1_.refs_0_ = bf16[2,3,512,128]{3,2,1,0:T(8,128)(2,1)} custom-call(bf16[2,3,512,512]{3,2,1,0:T(8,128)(2,1)S(1)} %copy-done, bf16[2,3,512,128]{3,2,1,0:T(8,128)(2,1)} %slice.18.refs_0_), custom_call_target="tpu_custom_call" | custom-call | bytes 1048576 | tf_op jit(solution)/shard_map/columns1/pallas_call | solution.py:303
  8.7 2.6 %collective-permute-start.2 = (bf16[2,3,512,128]{3,2,1,0:T(8,128)(2,1)}, bf16[2,3,512,128]{3,2,1,0:T(8,128)(2,1)}, u32[]{:S(2)}, u32[]{:S(2)}) collective-permute-start(bf16[2,3,512,128]{3,2,1,0:T(8,128)(2,1)} %columns1.1.refs_1_.refs_0_), channel_id=1, source_target_pairs={{1,2},{3,4},{5,6},{7,8},{9,10},{11,12},{13,14},{15,16},{17,18},{19... | collective-permute-start | bytes 2359304 | tf_op jit(solution)/shard_map/ppermute | solution.py:357
  11.3 1.0 %columns0.1 = bf16[2,3,512,128]{3,2,1,0:T(8,128)(2,1)} custom-call(bf16[2,3,512,512]{3,2,1,0:T(8,128)(2,1)S(1)} %copy-done.1, bf16[2,3,512,128]{3,2,1,0:T(8,128)(2,1)} %columns1.1.refs_1_.refs_0_), custom_call_target="tpu_custom_call" | custom-call | bytes 1048576 | tf_op jit(solution)/shard_map/columns0/pallas_call | solution.py:303
  12.3 1.6 %collective-permute-start.5 = (bf16[2,3,512,128]{3,2,1,0:T(8,128)(2,1)}, bf16[2,3,512,128]{3,2,1,0:T(8,128)(2,1)}, u32[]{:S(2)}, u32[]{:S(2)}) collective-permute-start(bf16[2,3,512,128]{3,2,1,0:T(8,128)(2,1)} %columns0.1), channel_id=1, source_target_pairs={{8,0},{16,1},{15,30},{23,31}} | collective-permute-start | bytes 2359304 | tf_op jit(solution)/shard_map/ppermute | solution.py:346
  14.0 0.6 gather_fusion
  15.1 0.3 fusion.2
  15.8 0.9 %columns2.1 = bf16[2,3,512,128]{3,2,1,0:T(8,128)(2,1)} custom-call(bf16[2,3,512,512]{3,2,1,0:T(8,128)(2,1)S(1)} %copy-done.1, bf16[2,3,512,512]{3,2,1,0:T(8,128)(2,1)} %collective-permute-done.refs_0_, bf16[2,3,512,128]{3,2,1,0:T(8,128)(2,1)} %columns1.1.refs_1_.refs_0_), custom_call_target="tpu_custom_call" | custom-call | bytes 1048576 | tf_op jit(solution)/shard_map/columns2/pallas_call | solution.py:303
  16.7 3.1 %collective-permute-start.1 = (bf16[2,3,512,128]{3,2,1,0:T(8,128)(2,1)}, bf16[2,3,512,128]{3,2,1,0:T(8,128)(2,1)}, u32[]{:S(2)}, u32[]{:S(2)}) collective-permute-start(bf16[2,3,512,128]{3,2,1,0:T(8,128)(2,1)} %columns2.1), channel_id=1, source_target_pairs={{1,2},{3,4},{5,6},{7,8},{9,10},{11,12},{13,14},{15,16},{17,18},{19... | collective-permute-start | bytes 2359304 | tf_op jit(solution)/shard_map/ppermute | solution.py:357
  20.1 0.7 collective-permute-start.4
  20.8 0.7 collective-permute-start.6
  21.5 13.0 %collective-permute-done.2.refs_1_ = bf16[2,3,512,128]{3,2,1,0:T(8,128)(2,1)} collective-permute-done((bf16[2,3,512,128]{3,2,1,0:T(8,128)(2,1)}, bf16[2,3,512,128]{3,2,1,0:T(8,128)(2,1)}, u32[]{:S(2)}, u32[]{:S(2)}) %collective-permute-start.2) | collective-permute-done | bytes 786464 | tf_op jit(solution)/shard_map/ppermute | solution.py:357
  34.6 4.2 %expand1.1 = (bf16[2,9,512,128]{3,2,1,0:T(8,128)(2,1)S(1)}, f32[16,128]{1,0:T(8,128)S(1)}) custom-call(s32[67]{0:T(128)S(1)} %pad_add_fusion.meta.refs_2_, bf16[2,3,512,512]{3,2,1,0:T(8,128)(2,1)S(1)} %copy-done.1, bf16[2,3,512,512]{3,2,1,0:T(8,128)(2,1)} %collective-permute-done.refs_0_, bf16[2,3,512,128]{3,2,1,0:T(8,128)(2,1)} %collective-permute-done.2.refs_1_, ...), custom_call_target="tpu_custom_call" | custom-call | flops 1207959552 | bytes 12582912 | tf_op jit(solution)/shard_map/expand1/pallas_call | solution.py:224
  38.7 0.1 columns3.1
  38.9 2.0 %collective-permute-start.7 = (bf16[2,3,512,128]{3,2,1,0:T(8,128)(2,1)S(1)}, bf16[2,3,512,128]{3,2,1,0:T(8,128)(2,1)S(1)}, u32[]{:S(2)}, u32[]{:S(2)}) collective-permute-start(bf16[2,3,512,128]{3,2,1,0:T(8,128)(2,1)S(1)} %columns3.1), channel_id=1, source_target_pairs={{1,2},{3,4},{5,6},{7,8},{9,10},{11,12},{13,14},{15,16},{17,18},{19... | collective-permute-start | bytes 2359304 | tf_op jit(solution)/shard_map/ppermute | solution.py:367
  40.9 3.6 %early3.1 = (f32[2,9,512,128]{3,2,1,0:T(8,128)S(1)}, bf16[2,9,512,128]{3,2,1,0:T(8,128)(2,1)S(1)}, f32[16,128]{1,0:T(8,128)S(1)}) custom-call(s32[67]{0:T(128)S(1)} %pad_add_fusion.meta.refs_2_, bf16[2,3,512,512]{3,2,1,0:T(8,128)(2,1)S(1)} %copy-done.1, bf16[2,3,512,512]{3,2,1,0:T(8,128)(2,1)} %collective-permute-done.refs_0_, ...), custom_call_target="tpu_custom_call" | custom-call | flops 603979776 | bytes 8388608 | tf_op jit(solution)/shard_map/early3/pallas_call | solution.py:203
  44.5 6.8 %collective-permute-done.1.refs_1_ = bf16[2,3,512,128]{3,2,1,0:T(8,128)(2,1)} collective-permute-done((bf16[2,3,512,128]{3,2,1,0:T(8,128)(2,1)}, bf16[2,3,512,128]{3,2,1,0:T(8,128)(2,1)}, u32[]{:S(2)}, u32[]{:S(2)}) %collective-permute-start.1) | collective-permute-done | bytes 786464 | tf_op jit(solution)/shard_map/ppermute | solution.py:357
  51.3 4.2 %expand2.1 = (bf16[2,9,512,128]{3,2,1,0:T(8,128)(2,1)S(1)}, f32[16,128]{1,0:T(8,128)S(1)}) custom-call(s32[67]{0:T(128)S(1)} %pad_add_fusion.meta.refs_2_, bf16[2,3,512,512]{3,2,1,0:T(8,128)(2,1)S(1)} %copy-done.1, bf16[2,3,512,512]{3,2,1,0:T(8,128)(2,1)} %collective-permute-done.refs_0_, bf16[2,3,512,128]{3,2,1,0:T(8,128)(2,1)} %collective-permute-done.1.refs_1_, ...), custom_call_target="tpu_custom_call" | custom-call | flops 1207959552 | bytes 12582912 | tf_op jit(solution)/shard_map/expand2/pallas_call | solution.py:224
  55.5 3.7 %early0.1 = (f32[2,9,512,128]{3,2,1,0:T(8,128)S(1)}, bf16[2,9,512,128]{3,2,1,0:T(8,128)(2,1)S(1)}, f32[16,128]{1,0:T(8,128)S(1)}) custom-call(s32[67]{0:T(128)S(1)} %pad_add_fusion.meta.refs_2_, bf16[2,3,512,512]{3,2,1,0:T(8,128)(2,1)S(1)} %copy-done.1, bf16[2,3,512,512]{3,2,1,0:T(8,128)(2,1)} %collective-permute-done.refs_0_, ...), custom_call_target="tpu_custom_call" | custom-call | flops 603979776 | bytes 8388608 | tf_op jit(solution)/shard_map/early0/pallas_call | solution.py:203
  59.2 3.1 %late0.1 = (bf16[2,9,512,128]{3,2,1,0:T(8,128)(2,1)S(1)}, f32[16,128]{1,0:T(8,128)S(1)}) custom-call(s32[67]{0:T(128)S(1)} %pad_add_fusion.meta.refs_2_, bf16[2,3,512,512]{3,2,1,0:T(8,128)(2,1)S(1)} %copy-done.1, f32[2,9,512,128]{3,2,1,0:T(8,128)S(1)} %get-tuple-element.22.refs_0_, bf16[2,9,512,128]{3,2,1,0:T(8,128)(2,1)S(1)} %get-tuple-element.23.refs_1_, ...), custom_call_target="tpu_custom_call" | custom-call | flops 603979776 | bytes 8388608 | tf_op jit(solution)/shard_map/late0/pallas_call | solution.py:203
  62.3 4.5 %collective-permute-done.7.refs_3_ = bf16[2,3,512,128]{3,2,1,0:T(8,128)(2,1)S(1)} collective-permute-done((bf16[2,3,512,128]{3,2,1,0:T(8,128)(2,1)S(1)}, bf16[2,3,512,128]{3,2,1,0:T(8,128)(2,1)S(1)}, u32[]{:S(2)}, u32[]{:S(2)}) %collective-permute-start.7) | collective-permute-done | bytes 786464 | tf_op jit(solution)/shard_map/ppermute | solution.py:367
  66.8 2.8 %late3.1 = (bf16[2,9,512,128]{3,2,1,0:T(8,128)(2,1)S(1)}, f32[16,128]{1,0:T(8,128)S(1)}) custom-call(s32[67]{0:T(128)S(1)} %pad_add_fusion.meta.refs_2_, bf16[2,3,512,512]{3,2,1,0:T(8,128)(2,1)S(1)} %copy-done.1, f32[2,9,512,128]{3,2,1,0:T(8,128)S(1)} %get-tuple-element.26.refs_0_, bf16[2,9,512,128]{3,2,1,0:T(8,128)(2,1)S(1)} %get-tuple-element.27.refs_1_, ...), custom_call_target="tpu_custom_call" | custom-call | flops 603979776 | bytes 8388608 | tf_op jit(solution)/shard_map/late3/pallas_call | solution.py:203
  69.7 1.2 %collective-permute-done.8 = f32[12,512]{1,0:T(8,128)S(1)} collective-permute-done((f32[12,512]{1,0:T(8,128)S(1)}, f32[12,512]{1,0:T(8,128)S(1)}, u32[]{:S(2)}, u32[]{:S(2)}) %collective-permute-start.8) | collective-permute-done | bytes 24608 | tf_op jit(solution)/shard_map/ppermute | solution.py:379
  70.9 4.1 %collective-permute-start.10 = (f32[12,512]{1,0:T(8,128)S(1)}, f32[12,512]{1,0:T(8,128)S(1)}, u32[]{:S(2)}, u32[]{:S(2)}) collective-permute-start(f32[12,512]{1,0:T(8,128)S(1)} %fusion.4), channel_id=1, source_target_pairs={{1,4},{3,6},{5,8},{7,10},{9,12},{11,14},{13,16},{15,18},{17,20},{1... | collective-permute-start | bytes 73736 | tf_op jit(solution)/shard_map/ppermute | solution.py:381
  75.1 4.4 %collective-permute-start.9 = (f32[12,512]{1,0:T(8,128)S(1)}, f32[12,512]{1,0:T(8,128)S(1)}, u32[]{:S(2)}, u32[]{:S(2)}) collective-permute-start(f32[12,512]{1,0:T(8,128)S(1)} %fusion.4), channel_id=1, source_target_pairs={{1,2},{3,4},{5,6},{7,8},{9,10},{11,12},{13,14},{15,16},{17,18},{19... | collective-permute-start | bytes 73736 | tf_op jit(solution)/shard_map/ppermute | solution.py:380
  79.4 1.3 %collective-permute-done.9 = f32[12,512]{1,0:T(8,128)S(1)} collective-permute-done((f32[12,512]{1,0:T(8,128)S(1)}, f32[12,512]{1,0:T(8,128)S(1)}, u32[]{:S(2)}, u32[]{:S(2)}) %collective-permute-start.9) | collective-permute-done | bytes 24608 | tf_op jit(solution)/shard_map/ppermute | solution.py:380
  80.8 4.6 %collective-permute-start.11 = (f32[12,512]{1,0:T(8,128)S(1)}, f32[12,512]{1,0:T(8,128)S(1)}, u32[]{:S(2)}, u32[]{:S(2)}) collective-permute-start(f32[12,512]{1,0:T(8,128)S(1)} %add_select_fusion), channel_id=1, source_target_pairs={{0,1},{2,3},{4,5},{6,7},{8,9},{10,11},{12,13},{14,15},{16,17},{18,... | collective-permute-start | bytes 73736 | tf_op jit(solution)/shard_map/ppermute | solution.py:387
  85.4 0.9 collective-permute-done.11
  86.2 4.3 %inflate0.1 = bf16[2,9,512,512]{3,2,1,0:T(8,128)(2,1)} custom-call(s32[67]{0:T(128)S(1)} %pad_add_fusion.meta.refs_2_, f32[12,512]{1,0:T(8,128)S(1)} %add_add_fusion.totals, bf16[2,9,512,128]{3,2,1,0:T(8,128)(2,1)S(1)} %get-tuple-element.29.refs_0_, bf16[2,9,512,128]{3,2,1,0:T(8,128)(2,1)S(1)} %get-tuple-element.30.refs_1_, ...), custom_call_target="tpu_custom_call" | custom-call | flops 16777216 | bytes 16777216 | tf_op jit(solution)/shard_map/inflate0/pallas_call | solution.py:278
  (38 shorter events, 1.4 us)
Async XLA Ops:
  0.0 15.7 %collective-permute-start = (bf16[2,3,512,512]{3,2,1,0:T(8,128)(2,1)}, bf16[2,3,512,512]{3,2,1,0:T(8,128)(2,1)}, u32[]{:S(2)}, u32[]{:S(2)}) collective-permute-start(bf16[2,3,512,512]{3,2,1,0:T(8,128)(2,1)} %own.11), channel_id=1, source_target_pairs={{0,1},{2,3},{4,5},{6,7},{8,9},{10,11},{12,13},{14,15},{16,17},{18,... | collective-permute-start | bytes 9437192 | tf_op jit(solution)/shard_map/ppermute | solution.py:338
  2.7 17.4 %collective-permute-start.3 = (bf16[2,3,512,128]{3,2,1,0:T(8,128)(2,1)}, bf16[2,3,512,128]{3,2,1,0:T(8,128)(2,1)}, u32[]{:S(2)}, u32[]{:S(2)}) collective-permute-start(bf16[2,3,512,128]{3,2,1,0:T(8,128)(2,1)} %slice.18.refs_0_), channel_id=1, source_target_pairs={{1,2},{3,4},{5,6},{9,10},{11,12},{13,14},{17,18},{19,20},{21,22},{... | collective-permute-start | bytes 2359304 | tf_op jit(solution)/shard_map/ppermute | solution.py:347
  5.8 1.9 %copy-start = (bf16[2,3,512,512]{3,2,1,0:T(8,128)(2,1)S(1)}, bf16[2,3,512,512]{3,2,1,0:T(8,128)(2,1)}, u32[]{:S(2)}) copy-start(bf16[2,3,512,512]{3,2,1,0:T(8,128)(2,1)} %own.11) | copy-start | bytes 9437188
  7.7 3.6 %copy-start.1 = (bf16[2,3,512,512]{3,2,1,0:T(8,128)(2,1)S(1)}, bf16[2,3,512,512]{3,2,1,0:T(8,128)(2,1)}, u32[]{:S(2)}) copy-start(bf16[2,3,512,512]{3,2,1,0:T(8,128)(2,1)} %own.11) | copy-start | bytes 9437188
  8.7 5.2 %copy-start.2 = (s32[64,3]{0,1:T(4,128)S(1)}, s32[64,3]{0,1:T(4,128)}, u32[]{:S(2)}) copy-start(s32[64,3]{0,1:T(4,128)} %param.3) | copy-start | bytes 2308
  8.7 25.9 %collective-permute-start.2 = (bf16[2,3,512,128]{3,2,1,0:T(8,128)(2,1)}, bf16[2,3,512,128]{3,2,1,0:T(8,128)(2,1)}, u32[]{:S(2)}, u32[]{:S(2)}) collective-permute-start(bf16[2,3,512,128]{3,2,1,0:T(8,128)(2,1)} %columns1.1.refs_1_.refs_0_), channel_id=1, source_target_pairs={{1,2},{3,4},{5,6},{7,8},{9,10},{11,12},{13,14},{15,16},{17,18},{19... | collective-permute-start | bytes 2359304 | tf_op jit(solution)/shard_map/ppermute | solution.py:357
  12.3 8.5 %collective-permute-start.5 = (bf16[2,3,512,128]{3,2,1,0:T(8,128)(2,1)}, bf16[2,3,512,128]{3,2,1,0:T(8,128)(2,1)}, u32[]{:S(2)}, u32[]{:S(2)}) collective-permute-start(bf16[2,3,512,128]{3,2,1,0:T(8,128)(2,1)} %columns0.1), channel_id=1, source_target_pairs={{8,0},{16,1},{15,30},{23,31}} | collective-permute-start | bytes 2359304 | tf_op jit(solution)/shard_map/ppermute | solution.py:346
  16.7 34.6 %collective-permute-start.1 = (bf16[2,3,512,128]{3,2,1,0:T(8,128)(2,1)}, bf16[2,3,512,128]{3,2,1,0:T(8,128)(2,1)}, u32[]{:S(2)}, u32[]{:S(2)}) collective-permute-start(bf16[2,3,512,128]{3,2,1,0:T(8,128)(2,1)} %columns2.1), channel_id=1, source_target_pairs={{1,2},{3,4},{5,6},{7,8},{9,10},{11,12},{13,14},{15,16},{17,18},{19... | collective-permute-start | bytes 2359304 | tf_op jit(solution)/shard_map/ppermute | solution.py:357
  20.1 39.1 %collective-permute-start.4 = (bf16[2,3,512,128]{3,2,1,0:T(8,128)(2,1)}, bf16[2,3,512,128]{3,2,1,0:T(8,128)(2,1)S(1)}, u32[]{:S(2)}, u32[]{:S(2)}) collective-permute-start(bf16[2,3,512,128]{3,2,1,0:T(8,128)(2,1)} %collective-permute-done.3.refs_3_.refs_1_), channel_id=1, source_target_pairs={{31,8},{0,23}} | collective-permute-start | bytes 2359304 | tf_op jit(solution)/shard_map/ppermute | solution.py:348
  20.8 38.4 %collective-permute-start.6 = (bf16[2,3,512,128]{3,2,1,0:T(8,128)(2,1)}, bf16[2,3,512,128]{3,2,1,0:T(8,128)(2,1)S(1)}, u32[]{:S(2)}, u32[]{:S(2)}) collective-permute-start(bf16[2,3,512,128]{3,2,1,0:T(8,128)(2,1)} %collective-permute-done.5.refs_2_), channel_id=1, source_target_pairs={{0,7},{1,15},{30,16},{31,24}} | collective-permute-start | bytes 2359304 | tf_op jit(solution)/shard_map/ppermute | solution.py:348
  38.9 27.9 %collective-permute-start.7 = (bf16[2,3,512,128]{3,2,1,0:T(8,128)(2,1)S(1)}, bf16[2,3,512,128]{3,2,1,0:T(8,128)(2,1)S(1)}, u32[]{:S(2)}, u32[]{:S(2)}) collective-permute-start(bf16[2,3,512,128]{3,2,1,0:T(8,128)(2,1)S(1)} %columns3.1), channel_id=1, source_target_pairs={{1,2},{3,4},{5,6},{7,8},{9,10},{11,12},{13,14},{15,16},{17,18},{19... | collective-permute-start | bytes 2359304 | tf_op jit(solution)/shard_map/ppermute | solution.py:367
  69.6 1.3 %collective-permute-start.8 = (f32[12,512]{1,0:T(8,128)S(1)}, f32[12,512]{1,0:T(8,128)S(1)}, u32[]{:S(2)}, u32[]{:S(2)}) collective-permute-start(f32[12,512]{1,0:T(8,128)S(1)} %pad_maximum_fusion), channel_id=1, source_target_pairs={{0,1},{2,3},{4,5},{6,7},{8,9},{10,11},{12,13},{14,15},{16,17},{18,... | collective-permute-start | bytes 73736 | tf_op jit(solution)/shard_map/ppermute | solution.py:379
  70.9 8.5 %collective-permute-start.10 = (f32[12,512]{1,0:T(8,128)S(1)}, f32[12,512]{1,0:T(8,128)S(1)}, u32[]{:S(2)}, u32[]{:S(2)}) collective-permute-start(f32[12,512]{1,0:T(8,128)S(1)} %fusion.4), channel_id=1, source_target_pairs={{1,4},{3,6},{5,8},{7,10},{9,12},{11,14},{13,16},{15,18},{17,20},{1... | collective-permute-start | bytes 73736 | tf_op jit(solution)/shard_map/ppermute | solution.py:381
  75.1 5.7 %collective-permute-start.9 = (f32[12,512]{1,0:T(8,128)S(1)}, f32[12,512]{1,0:T(8,128)S(1)}, u32[]{:S(2)}, u32[]{:S(2)}) collective-permute-start(f32[12,512]{1,0:T(8,128)S(1)} %fusion.4), channel_id=1, source_target_pairs={{1,2},{3,4},{5,6},{7,8},{9,10},{11,12},{13,14},{15,16},{17,18},{19... | collective-permute-start | bytes 73736 | tf_op jit(solution)/shard_map/ppermute | solution.py:380
  80.8 5.4 %collective-permute-start.11 = (f32[12,512]{1,0:T(8,128)S(1)}, f32[12,512]{1,0:T(8,128)S(1)}, u32[]{:S(2)}, u32[]{:S(2)}) collective-permute-start(f32[12,512]{1,0:T(8,128)S(1)} %add_select_fusion), channel_id=1, source_target_pairs={{0,1},{2,3},{4,5},{6,7},{8,9},{10,11},{12,13},{14,15},{16,17},{18,... | collective-permute-start | bytes 73736 | tf_op jit(solution)/shard_map/ppermute | solution.py:387

commit v6 on v5

--- a/solution.py
+++ b/solution.py
@@ -244,8 +244,8 @@
     )(meta, own, beside, *across, before)
 
 
-def inflate_kernel(scale, slots, first, meta, totals, *refs):
-    count = len(refs) - 3 - (1 if first else 0)
+def inflate_kernel(scale, slots, first, more, meta, totals, *refs):
+    count = len(refs) - 3 - more
     parts, (out, made, sems) = refs[:count], refs[-3:]
     rows_here, slot_total, side, width = parts[0].shape
     depth = made.shape[0]
@@ -257,18 +257,32 @@
         at = number % depth
         return pltpu.make_async_copy(made.at[at], out.at[r, slot, :, cols], sems.at[at])
 
+    def leads(number):
+        r, slot = jobs[number]
+        return meta[r * FIELDS + 2 * slots + slot] == slot
+
     for number, (r, slot) in enumerate(jobs):
         if number >= depth:
-            sending(number - depth).wait()
-        place = meta[r * FIELDS + 2 * slots + slots * slots + slot]
-        factor = scale / totals[pl.ds(place, 1), :]
-        for q, part in enumerate(parts):
-            wide = part[r, slot].astype(jnp.float32)
-            here = slice(q * width, (q + 1) * width)
-            made[number % depth, :, here] = (wide * wide * factor[:, here]).astype(jnp.bfloat16)
-        sending(number).start()
+
+            @pl.when(leads(number - depth))
+            def _():
+                sending(number - depth).wait()
+
+        @pl.when(leads(number))
+        def _():
+            place = meta[r * FIELDS + 2 * slots + slots * slots + slot]
+            factor = scale / totals[pl.ds(place, 1), :]
+            for q, part in enumerate(parts):
+                wide = part[r, slot].astype(jnp.float32)
+                here = slice(q * width, (q + 1) * width)
+                made[number % depth, :, here] = (wide * wide * factor[:, here]).astype(jnp.bfloat16)
+            sending(number).start()
+
     for number in range(len(jobs) - depth, len(jobs)):
-        sending(number).wait()
+
+        @pl.when(leads(number))
+        def _():
+            sending(number).wait()
 
 
 def inflate(scale, slots, meta, totals, parts, first=0, so_far=None):
@@ -276,7 +290,7 @@
     vmem, anywhere = pl.BlockSpec(memory_space=pltpu.VMEM), pl.BlockSpec(memory_space=pl.ANY)
     more = [] if so_far is None else [so_far]
     return pl.pallas_call(
-        functools.partial(inflate_kernel, scale, slots, first),
+        functools.partial(inflate_kernel, scale, slots, first, len(more)),
         in_specs=[pl.BlockSpec(memory_space=pltpu.SMEM), vmem] + [vmem] * len(parts) + [anywhere] * len(more),
         out_specs=anywhere,
         out_shape=jax.ShapeDtypeStruct((rows_here, slot_total, side, width * CHUNKS), jnp.bfloat16),
@@ -291,6 +305,34 @@
     )(meta, totals, *parts, *more)
 
 
+def blank_kernel(slots, meta, before, out, zero, sem):
+    del before
+    zero[...] = jnp.zeros_like(zero)
+    jobs = [(r, slot) for r in range(out.shape[0]) for slot in range(out.shape[1])]
+    for finish in (False, True):
+        for number, (r, slot) in enumerate(jobs):
+
+            @pl.when(meta[r * FIELDS + 2 * slots + slot] != slot)
+            def _():
+                copy = pltpu.make_async_copy(zero, out.at[r, slot], sem.at[number])
+                copy.wait() if finish else copy.start()
+
+
+def blank_slots(meta, before, rows_here, slots, side):
+    anywhere = pl.BlockSpec(memory_space=pl.ANY)
+    shape = (rows_here, slots * slots, side, side)
+    return pl.pallas_call(
+        functools.partial(blank_kernel, slots),
+        in_specs=[pl.BlockSpec(memory_space=pltpu.SMEM), anywhere],
+        out_specs=anywhere,
+        out_shape=jax.ShapeDtypeStruct(shape, jnp.bfloat16),
+        scratch_shapes=[pltpu.VMEM(shape[2:], jnp.bfloat16), pltpu.SemaphoreType.DMA((shape[0] * shape[1],))],
+        compiler_params=pltpu.CompilerParams(vmem_limit_bytes=2 * 2**20),
+        cost_estimate=pl.CostEstimate(flops=0, bytes_accessed=2**21, transcendentals=0),
+        name="blank",
+    )(meta, before)
+
+
 def columns_kernel(q, width, tiles, *refs):
     out, sem = refs[-2:]
     copy = pltpu.make_async_copy(tiles.at[:, :, :, pl.ds(q * width, width)], out, sem)
@@ -310,14 +352,6 @@
         cost_estimate=pl.CostEstimate(flops=0, bytes_accessed=2**20, transcendentals=0),
         name=f"columns{q}",
     )(tiles, *after)
-
-
-def shift_lines(block, distance):
-    lines = block.shape[0]
-    pad = jnp.zeros((abs(distance), block.shape[1]), block.dtype)
-    if distance > 0:
-        return jnp.concatenate([pad, block[: lines - distance]], axis=0)
-    return jnp.concatenate([block[-distance:], pad], axis=0)
 
 
 def body(matrix_tiles, pattern):
@@ -365,6 +399,8 @@
         if q == order[0]:
             last = columns_of(matrix_tiles, CHUNKS - 1, width, [before, *follow])
             across.append([lax.ppermute(last, AXES, next_chip)])
+        if q == order[0]:
+            before = so_far = blank_slots(meta, last, rows_here, slots, side)
         split = order[-1] if q == order[0] else order[-2]
         halves[split] = expand_split(split, False, meta, matrix_tiles, [beside], before, width)
         before = halves[split][2]
@@ -377,15 +413,16 @@
     used = chip_rows + 4 * W
     window = window[:used]
     chip = window + lax.ppermute(window, AXES, swap)
-    first = lax.ppermute(chip, AXES, next_chip)
-    second = lax.ppermute(chip, AXES, second_chip)
-    gathered = jnp.where(
-        core == 0,
-        shift_lines(first, -chip_rows) + shift_lines(second, -2 * chip_rows),
-        shift_lines(first, chip_rows) + shift_lines(second, 2 * chip_rows),
-    )
-    totals = chip + gathered + lax.ppermute(gathered, AXES, swap)
-    return inflate(scale, slots, meta, totals, parts)
+    low = core == 0
+    near, far = 2 * chip_rows, chip_rows
+    first = lax.ppermute(jnp.where(low, chip[:near], chip[used - near :]), AXES, next_chip)
+    second = lax.ppermute(jnp.where(low, chip[:far], chip[used - far :]), AXES, second_chip)
+    blank = jnp.zeros((chip_rows, chip.shape[1]), chip.dtype)
+    gathered = first + jnp.where(low, jnp.concatenate([second, blank]), jnp.concatenate([blank, second]))
+    other = lax.ppermute(gathered, AXES, swap)
+    below, above = jnp.where(low, gathered, other), jnp.where(low, other, gathered)
+    totals = chip + jnp.concatenate([below, blank]) + jnp.concatenate([blank, above])
+    return inflate(scale, slots, meta, totals, parts, so_far=so_far)
 
 
 def solution(mesh):

time: 91.2 us -> 90.1 us (0.988)
  waiting for transfers between devices: 27.7 us -> 22.4 us
  local copies, waits for them, and re-layouts: 5.59 us -> 9.26 us
  Pallas kernels: 28.8 us -> 30.2 us
  starting transfers between devices: 27.5 us -> 26.4 us
    ppermute x2, waiting for transfers between devices: 19.8 us -> 13.9 us  [body(): lax.ppermute(piece, AXES, next_chip)]
    unnamed x7 -> x9, local copies, waits for them, and re-layouts: 1.99 us -> 5.67 us
    ppermute x3, starting transfers between devices: 13.1 us -> 11.4 us  [the longest x1 4.75 us: body(): other = lax.ppermute(gathered, AXES, swap)]
    pallas_call x1 -> x2, Pallas kernels: 4.35 us -> 5.9 us  [the longest x1 3.51 us: inflate(): pl.pallas_call(functools.partial(inflate_kernel, scale, slots, first, len...]
  transfers between devices with their start and end apart: 12 -> 12, of which waited for: 6 -> 6; matrix products, arithmetic and copies ran while one was open for 5% -> 5% of each run, Pallas kernels for 24% -> 27%
where the time goes in v6:
time: 90.1 us; the launch traced here: 89.4 us
  Pallas kernels  30.2 us (34%)
  starting transfers between devices  26.4 us (29%)
  waiting for transfers between devices  22.4 us (25%)
  local copies, waits for them, and re-layouts  9.26 us (10%)
    ppermute x2, waiting for transfers between devices, body(): lax.ppermute(piece, AXES, next_chip)  13.9 us
    pallas_call x4, Pallas kernels, expand_split(): pl.pallas_call(functools.partial(split_kernel, q, rows_here, slots, late)...  13 us
    pallas_call x2, Pallas kernels, expand(): pl.pallas_call(functools.partial(expand_kernel, q, rows_here, slots), in_...  8.33 us
    ppermute x2, starting transfers between devices, body(): lax.ppermute(piece, AXES, next_chip)  5.7 us
    unnamed x9, local copies, waits for them, and re-layouts  5.67 us
    ppermute x1, starting transfers between devices, body(): other = lax.ppermute(gathered, AXES, swap)  4.75 us
    ppermute x1, waiting for transfers between devices, body(): across.append([lax.ppermute(last, AXES, next_chip)])  4.55 us
    ppermute x1, starting transfers between devices, body(): lax.ppermute(jnp.where(low, chip[:far], chip[used - far:]), AXES, second_...  3.59 us
  transfers between devices with their start and end apart: 12, of which 6 were waited for; matrix products, arithmetic and copies ran while one was open for 5% of the time, Pallas kernels for 27%

profile of v6, /device:TPU:5, one launch (start us, length us, event | category | flops | bytes accessed | tf_op | source)
XLA Modules:
  0.0 89.4 jit_solution(4158542905545942786)
XLA Ops:
  0.0 0.7 collective-permute-start
  0.7 2.1 %slice.18.refs_0_ = bf16[2,3,512,128]{3,2,1,0:T(8,128)(2,1)} slice(bf16[2,3,512,512]{3,2,1,0:T(8,128)(2,1)} %own.11), slice={[0:2], [0:3], [0:512], [0:128]} | slice | bytes 1572864 | tf_op jit(solution)/shard_map/slice | solution.py:373
  2.7 3.1 %collective-permute-start.3 = (bf16[2,3,512,128]{3,2,1,0:T(8,128)(2,1)}, bf16[2,3,512,128]{3,2,1,0:T(8,128)(2,1)}, u32[]{:S(2)}, u32[]{:S(2)}) collective-permute-start(bf16[2,3,512,128]{3,2,1,0:T(8,128)(2,1)} %slice.18.refs_0_), channel_id=1, source_target_pairs={{1,2},{3,4},{5,6},{9,10},{11,12},{13,14},{17,18},{19,20},{21,22},{... | collective-permute-start | bytes 2359304 | tf_op jit(solution)/shard_map/ppermute | solution.py:381
  5.8 1.9 %copy-done = bf16[2,3,512,512]{3,2,1,0:T(8,128)(2,1)S(1)} copy-done((bf16[2,3,512,512]{3,2,1,0:T(8,128)(2,1)S(1)}, bf16[2,3,512,512]{3,2,1,0:T(8,128)(2,1)}, u32[]{:S(2)}) %copy-start) | copy-done | bytes 3145752
  7.7 0.9 %columns1.1.refs_1_.refs_0_ = bf16[2,3,512,128]{3,2,1,0:T(8,128)(2,1)} custom-call(bf16[2,3,512,512]{3,2,1,0:T(8,128)(2,1)S(1)} %copy-done, bf16[2,3,512,128]{3,2,1,0:T(8,128)(2,1)} %slice.18.refs_0_), custom_call_target="tpu_custom_call" | custom-call | bytes 1048576 | tf_op jit(solution)/shard_map/columns1/pallas_call | solution.py:345
  8.7 2.6 %collective-permute-start.2 = (bf16[2,3,512,128]{3,2,1,0:T(8,128)(2,1)}, bf16[2,3,512,128]{3,2,1,0:T(8,128)(2,1)}, u32[]{:S(2)}, u32[]{:S(2)}) collective-permute-start(bf16[2,3,512,128]{3,2,1,0:T(8,128)(2,1)} %columns1.1.refs_1_.refs_0_), channel_id=1, source_target_pairs={{1,2},{3,4},{5,6},{7,8},{9,10},{11,12},{13,14},{15,16},{17,18},{19... | collective-permute-start | bytes 2359304 | tf_op jit(solution)/shard_map/ppermute | solution.py:391
  11.3 1.0 %columns0.1 = bf16[2,3,512,128]{3,2,1,0:T(8,128)(2,1)} custom-call(bf16[2,3,512,512]{3,2,1,0:T(8,128)(2,1)S(1)} %copy-done.1, bf16[2,3,512,128]{3,2,1,0:T(8,128)(2,1)} %columns1.1.refs_1_.refs_0_), custom_call_target="tpu_custom_call" | custom-call | bytes 1048576 | tf_op jit(solution)/shard_map/columns0/pallas_call | solution.py:345
  12.3 1.6 %collective-permute-start.4 = (bf16[2,3,512,128]{3,2,1,0:T(8,128)(2,1)}, bf16[2,3,512,128]{3,2,1,0:T(8,128)(2,1)}, u32[]{:S(2)}, u32[]{:S(2)}) collective-permute-start(bf16[2,3,512,128]{3,2,1,0:T(8,128)(2,1)} %columns0.1), channel_id=1, source_target_pairs={{8,0},{16,1},{15,30},{23,31}} | collective-permute-start | bytes 2359304 | tf_op jit(solution)/shard_map/ppermute | solution.py:380
  15.8 0.9 %columns2.1 = bf16[2,3,512,128]{3,2,1,0:T(8,128)(2,1)} custom-call(bf16[2,3,512,512]{3,2,1,0:T(8,128)(2,1)S(1)} %copy-done.1, bf16[2,3,512,512]{3,2,1,0:T(8,128)(2,1)} %collective-permute-done.refs_0_, bf16[2,3,512,128]{3,2,1,0:T(8,128)(2,1)} %columns1.1.refs_1_.refs_0_), custom_call_target="tpu_custom_call" | custom-call | bytes 1048576 | tf_op jit(solution)/shard_map/columns2/pallas_call | solution.py:345
  16.7 3.1 %collective-permute-start.1 = (bf16[2,3,512,128]{3,2,1,0:T(8,128)(2,1)}, bf16[2,3,512,128]{3,2,1,0:T(8,128)(2,1)}, u32[]{:S(2)}, u32[]{:S(2)}) collective-permute-start(bf16[2,3,512,128]{3,2,1,0:T(8,128)(2,1)} %columns2.1), channel_id=1, source_target_pairs={{1,2},{3,4},{5,6},{7,8},{9,10},{11,12},{13,14},{15,16},{17,18},{19... | collective-permute-start | bytes 2359304 | tf_op jit(solution)/shard_map/ppermute | solution.py:391
  20.1 0.7 collective-permute-start.5
  20.8 0.7 collective-permute-start.6
  21.5 13.0 %collective-permute-done.2.refs_1_ = bf16[2,3,512,128]{3,2,1,0:T(8,128)(2,1)} collective-permute-done((bf16[2,3,512,128]{3,2,1,0:T(8,128)(2,1)}, bf16[2,3,512,128]{3,2,1,0:T(8,128)(2,1)}, u32[]{:S(2)}, u32[]{:S(2)}) %collective-permute-start.2) | collective-permute-done | bytes 786464 | tf_op jit(solution)/shard_map/ppermute | solution.py:391
  34.6 4.2 %expand1.1 = (bf16[2,9,512,128]{3,2,1,0:T(8,128)(2,1)S(1)}, f32[16,128]{1,0:T(8,128)S(1)}) custom-call(s32[67]{0:T(128)S(1)} %pad_add_fusion.1.meta.refs_2_, bf16[2,3,512,512]{3,2,1,0:T(8,128)(2,1)S(1)} %copy-done.1, bf16[2,3,512,512]{3,2,1,0:T(8,128)(2,1)} %collective-permute-done.refs_0_, bf16[2,3,512,128]{3,2,1,0:T(8,128)(2,1)} %collective-permute-done.2.refs_1_, ...), custom_call_target="tpu_custom_call" | custom-call | flops 1207959552 | bytes 12582912 | tf_op jit(solution)/shard_map/expand1/pallas_call | solution.py:224
  38.9 2.0 %collective-permute-start.7 = (bf16[2,3,512,128]{3,2,1,0:T(8,128)(2,1)S(1)}, bf16[2,3,512,128]{3,2,1,0:T(8,128)(2,1)S(1)}, u32[]{:S(2)}, u32[]{:S(2)}) collective-permute-start(bf16[2,3,512,128]{3,2,1,0:T(8,128)(2,1)S(1)} %columns3.1.before), channel_id=1, source_target_pairs={{1,2},{3,4},{5,6},{7,8},{9,10},{11,12},{13,14},{15,16},{17,18},{19... | collective-permute-start | bytes 2359304 | tf_op jit(solution)/shard_map/ppermute | solution.py:401
  40.9 2.4 %blank.1.refs_1_.refs_4_ = bf16[2,9,512,512]{3,2,1,0:T(8,128)(2,1)} custom-call(s32[67]{0:T(128)S(1)} %pad_add_fusion.1.meta.refs_2_, bf16[2,3,512,128]{3,2,1,0:T(8,128)(2,1)S(1)} %columns3.1.before), custom_call_target="tpu_custom_call" | custom-call | bytes 2097152 | tf_op jit(solution)/shard_map/blank/pallas_call | solution.py:324
  43.3 3.7 %copy-done.2 = bf16[2,9,512,512]{3,2,1,0:T(8,128)(2,1)S(1)} copy-done((bf16[2,9,512,512]{3,2,1,0:T(8,128)(2,1)S(1)}, bf16[2,9,512,512]{3,2,1,0:T(8,128)(2,1)}, u32[]{:S(2)}) %copy-start.2) | copy-done | bytes 9437208
  47.0 3.5 %early3.1 = (f32[2,9,512,128]{3,2,1,0:T(8,128)S(1)}, bf16[2,9,512,128]{3,2,1,0:T(8,128)(2,1)S(1)}, f32[16,128]{1,0:T(8,128)S(1)}) custom-call(s32[67]{0:T(128)S(1)} %pad_add_fusion.1.meta.refs_2_, bf16[2,3,512,512]{3,2,1,0:T(8,128)(2,1)S(1)} %copy-done.1, bf16[2,3,512,512]{3,2,1,0:T(8,128)(2,1)} %collective-permute-done.refs_0_, ...), custom_call_target="tpu_custom_call" | custom-call | flops 603979776 | bytes 8388608 | tf_op jit(solution)/shard_map/early3/pallas_call | solution.py:203
  50.4 0.9 collective-permute-done.1.refs_1_
  51.3 4.2 %expand2.1 = (bf16[2,9,512,128]{3,2,1,0:T(8,128)(2,1)S(1)}, f32[16,128]{1,0:T(8,128)S(1)}) custom-call(s32[67]{0:T(128)S(1)} %pad_add_fusion.1.meta.refs_2_, bf16[2,3,512,512]{3,2,1,0:T(8,128)(2,1)S(1)} %copy-done.1, bf16[2,3,512,512]{3,2,1,0:T(8,128)(2,1)} %collective-permute-done.refs_0_, bf16[2,3,512,128]{3,2,1,0:T(8,128)(2,1)} %collective-permute-done.1.refs_1_, ...), custom_call_target="tpu_custom_call" | custom-call | flops 1207959552 | bytes 12582912 | tf_op jit(solution)/shard_map/expand2/pallas_call | solution.py:224
  55.5 3.6 %early0.1 = (f32[2,9,512,128]{3,2,1,0:T(8,128)S(1)}, bf16[2,9,512,128]{3,2,1,0:T(8,128)(2,1)S(1)}, f32[16,128]{1,0:T(8,128)S(1)}) custom-call(s32[67]{0:T(128)S(1)} %pad_add_fusion.1.meta.refs_2_, bf16[2,3,512,512]{3,2,1,0:T(8,128)(2,1)S(1)} %copy-done.1, bf16[2,3,512,512]{3,2,1,0:T(8,128)(2,1)} %collective-permute-done.refs_0_, ...), custom_call_target="tpu_custom_call" | custom-call | flops 603979776 | bytes 8388608 | tf_op jit(solution)/shard_map/early0/pallas_call | solution.py:203
  59.1 3.1 %late0.1 = (bf16[2,9,512,128]{3,2,1,0:T(8,128)(2,1)S(1)}, f32[16,128]{1,0:T(8,128)S(1)}) custom-call(s32[67]{0:T(128)S(1)} %pad_add_fusion.1.meta.refs_2_, bf16[2,3,512,512]{3,2,1,0:T(8,128)(2,1)S(1)} %copy-done.1, f32[2,9,512,128]{3,2,1,0:T(8,128)S(1)} %get-tuple-element.22.refs_0_, bf16[2,9,512,128]{3,2,1,0:T(8,128)(2,1)S(1)} %get-tuple-element.23.refs_1_, ...), custom_call_target="tpu_custom_call" | custom-call | flops 603979776 | bytes 8388608 | tf_op jit(solution)/shard_map/late0/pallas_call | solution.py:203
  62.3 4.5 %collective-permute-done.7.refs_3_ = bf16[2,3,512,128]{3,2,1,0:T(8,128)(2,1)S(1)} collective-permute-done((bf16[2,3,512,128]{3,2,1,0:T(8,128)(2,1)S(1)}, bf16[2,3,512,128]{3,2,1,0:T(8,128)(2,1)S(1)}, u32[]{:S(2)}, u32[]{:S(2)}) %collective-permute-start.7) | collective-permute-done | bytes 786464 | tf_op jit(solution)/shard_map/ppermute | solution.py:401
  66.8 2.9 %late3.1 = (bf16[2,9,512,128]{3,2,1,0:T(8,128)(2,1)S(1)}, f32[16,128]{1,0:T(8,128)S(1)}) custom-call(s32[67]{0:T(128)S(1)} %pad_add_fusion.1.meta.refs_2_, bf16[2,3,512,512]{3,2,1,0:T(8,128)(2,1)S(1)} %copy-done.1, f32[2,9,512,128]{3,2,1,0:T(8,128)S(1)} %get-tuple-element.26.refs_0_, bf16[2,9,512,128]{3,2,1,0:T(8,128)(2,1)S(1)} %get-tuple-element.27.refs_1_, ...), custom_call_target="tpu_custom_call" | custom-call | flops 603979776 | bytes 8388608 | tf_op jit(solution)/shard_map/late3/pallas_call | solution.py:203
  69.7 0.6 collective-permute-start.8
  70.3 0.9 collective-permute-done.8
  71.2 3.0 %collective-permute-start.9 = (f32[8,512]{1,0:T(8,128)S(1)}, f32[8,512]{1,0:T(8,128)S(1)}, u32[]{:S(2)}, u32[]{:S(2)}) collective-permute-start(f32[8,512]{1,0:T(8,128)S(1)} %slice_select_fusion), channel_id=1, source_target_pairs={{1,2},{3,4},{5,6},{7,8},{9,10},{11,12},{13,14},{15,16},{17,18},{19... | collective-permute-start | bytes 49160 | tf_op jit(solution)/shard_map/ppermute | solution.py:418
  74.2 3.6 %collective-permute-start.10 = (f32[4,512]{1,0:T(4,128)S(1)}, f32[4,512]{1,0:T(4,128)S(1)}, u32[]{:S(2)}, u32[]{:S(2)}) collective-permute-start(f32[4,512]{1,0:T(4,128)S(1)} %slice_select_fusion.1), channel_id=1, source_target_pairs={{1,4},{3,6},{5,8},{7,10},{9,12},{11,14},{13,16},{15,18},{17,20},{1... | collective-permute-start | bytes 24584 | tf_op jit(solution)/shard_map/ppermute | solution.py:419
  77.8 2.3 %collective-permute-done.10 = f32[4,512]{1,0:T(4,128)S(1)} collective-permute-done((f32[4,512]{1,0:T(4,128)S(1)}, f32[4,512]{1,0:T(4,128)S(1)}, u32[]{:S(2)}, u32[]{:S(2)}) %collective-permute-start.10) | collective-permute-done | bytes 8224 | tf_op jit(solution)/shard_map/ppermute | solution.py:419
  80.1 4.8 %collective-permute-start.11 = (f32[8,512]{1,0:T(8,128)S(1)}, f32[8,512]{1,0:T(8,128)S(1)}, u32[]{:S(2)}, u32[]{:S(2)}) collective-permute-start(f32[8,512]{1,0:T(8,128)S(1)} %select_add_fusion), channel_id=1, source_target_pairs={{0,1},{2,3},{4,5},{6,7},{8,9},{10,11},{12,13},{14,15},{16,17},{18,... | collective-permute-start | bytes 49160 | tf_op jit(solution)/shard_map/ppermute | solution.py:422
  84.9 0.8 collective-permute-done.11
  85.7 3.5 %inflate0.1 = bf16[2,9,512,512]{3,2,1,0:T(8,128)(2,1)} custom-call(s32[67]{0:T(128)S(1)} %pad_add_fusion.1.meta.refs_2_, f32[12,512]{1,0:T(8,128)S(1)} %pad_add_fusion.totals, bf16[2,9,512,128]{3,2,1,0:T(8,128)(2,1)S(1)} %get-tuple-element.29.refs_0_, bf16[2,9,512,128]{3,2,1,0:T(8,128)(2,1)S(1)} %get-tuple-element.30.refs_1_, ...), custom_call_target="tpu_custom_call", output_to_operand_aliasing={{}: (6, {})} | custom-call | flops 16777216 | bytes 16777216 | tf_op jit(solution)/shard_map/inflate0/pallas_call | solution.py:292
  (42 shorter events, 2.4 us)
Async XLA Ops:
  0.0 15.7 %collective-permute-start = (bf16[2,3,512,512]{3,2,1,0:T(8,128)(2,1)}, bf16[2,3,512,512]{3,2,1,0:T(8,128)(2,1)}, u32[]{:S(2)}, u32[]{:S(2)}) collective-permute-start(bf16[2,3,512,512]{3,2,1,0:T(8,128)(2,1)} %own.11), channel_id=1, source_target_pairs={{0,1},{2,3},{4,5},{6,7},{8,9},{10,11},{12,13},{14,15},{16,17},{18,... | collective-permute-start | bytes 9437192 | tf_op jit(solution)/shard_map/ppermute | solution.py:372
  2.7 17.4 %collective-permute-start.3 = (bf16[2,3,512,128]{3,2,1,0:T(8,128)(2,1)}, bf16[2,3,512,128]{3,2,1,0:T(8,128)(2,1)}, u32[]{:S(2)}, u32[]{:S(2)}) collective-permute-start(bf16[2,3,512,128]{3,2,1,0:T(8,128)(2,1)} %slice.18.refs_0_), channel_id=1, source_target_pairs={{1,2},{3,4},{5,6},{9,10},{11,12},{13,14},{17,18},{19,20},{21,22},{... | collective-permute-start | bytes 2359304 | tf_op jit(solution)/shard_map/ppermute | solution.py:381
  5.8 1.9 %copy-start = (bf16[2,3,512,512]{3,2,1,0:T(8,128)(2,1)S(1)}, bf16[2,3,512,512]{3,2,1,0:T(8,128)(2,1)}, u32[]{:S(2)}) copy-start(bf16[2,3,512,512]{3,2,1,0:T(8,128)(2,1)} %own.11) | copy-start | bytes 9437188
  7.7 3.6 %copy-start.1 = (bf16[2,3,512,512]{3,2,1,0:T(8,128)(2,1)S(1)}, bf16[2,3,512,512]{3,2,1,0:T(8,128)(2,1)}, u32[]{:S(2)}) copy-start(bf16[2,3,512,512]{3,2,1,0:T(8,128)(2,1)} %own.11) | copy-start | bytes 9437188
  8.7 5.2 %copy-start.3 = (s32[64,3]{0,1:T(4,128)S(1)}, s32[64,3]{0,1:T(4,128)}, u32[]{:S(2)}) copy-start(s32[64,3]{0,1:T(4,128)} %param.3) | copy-start | bytes 2308
  8.7 25.9 %collective-permute-start.2 = (bf16[2,3,512,128]{3,2,1,0:T(8,128)(2,1)}, bf16[2,3,512,128]{3,2,1,0:T(8,128)(2,1)}, u32[]{:S(2)}, u32[]{:S(2)}) collective-permute-start(bf16[2,3,512,128]{3,2,1,0:T(8,128)(2,1)} %columns1.1.refs_1_.refs_0_), channel_id=1, source_target_pairs={{1,2},{3,4},{5,6},{7,8},{9,10},{11,12},{13,14},{15,16},{17,18},{19... | collective-permute-start | bytes 2359304 | tf_op jit(solution)/shard_map/ppermute | solution.py:391
  12.3 8.5 %collective-permute-start.4 = (bf16[2,3,512,128]{3,2,1,0:T(8,128)(2,1)}, bf16[2,3,512,128]{3,2,1,0:T(8,128)(2,1)}, u32[]{:S(2)}, u32[]{:S(2)}) collective-permute-start(bf16[2,3,512,128]{3,2,1,0:T(8,128)(2,1)} %columns0.1), channel_id=1, source_target_pairs={{8,0},{16,1},{15,30},{23,31}} | collective-permute-start | bytes 2359304 | tf_op jit(solution)/shard_map/ppermute | solution.py:380
  16.7 34.6 %collective-permute-start.1 = (bf16[2,3,512,128]{3,2,1,0:T(8,128)(2,1)}, bf16[2,3,512,128]{3,2,1,0:T(8,128)(2,1)}, u32[]{:S(2)}, u32[]{:S(2)}) collective-permute-start(bf16[2,3,512,128]{3,2,1,0:T(8,128)(2,1)} %columns2.1), channel_id=1, source_target_pairs={{1,2},{3,4},{5,6},{7,8},{9,10},{11,12},{13,14},{15,16},{17,18},{19... | collective-permute-start | bytes 2359304 | tf_op jit(solution)/shard_map/ppermute | solution.py:391
  20.1 39.0 %collective-permute-start.5 = (bf16[2,3,512,128]{3,2,1,0:T(8,128)(2,1)}, bf16[2,3,512,128]{3,2,1,0:T(8,128)(2,1)S(1)}, u32[]{:S(2)}, u32[]{:S(2)}) collective-permute-start(bf16[2,3,512,128]{3,2,1,0:T(8,128)(2,1)} %collective-permute-done.3.refs_1_.refs_3_), channel_id=1, source_target_pairs={{31,8},{0,23}} | collective-permute-start | bytes 2359304 | tf_op jit(solution)/shard_map/ppermute | solution.py:382
  20.8 38.3 %collective-permute-start.6 = (bf16[2,3,512,128]{3,2,1,0:T(8,128)(2,1)}, bf16[2,3,512,128]{3,2,1,0:T(8,128)(2,1)S(1)}, u32[]{:S(2)}, u32[]{:S(2)}) collective-permute-start(bf16[2,3,512,128]{3,2,1,0:T(8,128)(2,1)} %collective-permute-done.4.refs_2_), channel_id=1, source_target_pairs={{0,7},{1,15},{30,16},{31,24}} | collective-permute-start | bytes 2359304 | tf_op jit(solution)/shard_map/ppermute | solution.py:382
  38.9 27.9 %collective-permute-start.7 = (bf16[2,3,512,128]{3,2,1,0:T(8,128)(2,1)S(1)}, bf16[2,3,512,128]{3,2,1,0:T(8,128)(2,1)S(1)}, u32[]{:S(2)}, u32[]{:S(2)}) collective-permute-start(bf16[2,3,512,128]{3,2,1,0:T(8,128)(2,1)S(1)} %columns3.1.before), channel_id=1, source_target_pairs={{1,2},{3,4},{5,6},{7,8},{9,10},{11,12},{13,14},{15,16},{17,18},{19... | collective-permute-start | bytes 2359304 | tf_op jit(solution)/shard_map/ppermute | solution.py:401
  43.3 3.7 %copy-start.2 = (bf16[2,9,512,512]{3,2,1,0:T(8,128)(2,1)S(1)}, bf16[2,9,512,512]{3,2,1,0:T(8,128)(2,1)}, u32[]{:S(2)}) copy-start(bf16[2,9,512,512]{3,2,1,0:T(8,128)(2,1)} %blank.1.refs_1_.refs_4_) | copy-start | bytes 28311556
  69.7 1.5 %collective-permute-start.8 = (f32[12,512]{1,0:T(8,128)S(1)}, f32[12,512]{1,0:T(8,128)S(1)}, u32[]{:S(2)}, u32[]{:S(2)}) collective-permute-start(f32[12,512]{1,0:T(8,128)S(1)} %pad_maximum_fusion), channel_id=1, source_target_pairs={{0,1},{2,3},{4,5},{6,7},{8,9},{10,11},{12,13},{14,15},{16,17},{18,... | collective-permute-start | bytes 73736 | tf_op jit(solution)/shard_map/ppermute | solution.py:415
  71.2 8.9 %collective-permute-start.9 = (f32[8,512]{1,0:T(8,128)S(1)}, f32[8,512]{1,0:T(8,128)S(1)}, u32[]{:S(2)}, u32[]{:S(2)}) collective-permute-start(f32[8,512]{1,0:T(8,128)S(1)} %slice_select_fusion), channel_id=1, source_target_pairs={{1,2},{3,4},{5,6},{7,8},{9,10},{11,12},{13,14},{15,16},{17,18},{19... | collective-permute-start | bytes 49160 | tf_op jit(solution)/shard_map/ppermute | solution.py:418
  74.2 5.9 %collective-permute-start.10 = (f32[4,512]{1,0:T(4,128)S(1)}, f32[4,512]{1,0:T(4,128)S(1)}, u32[]{:S(2)}, u32[]{:S(2)}) collective-permute-start(f32[4,512]{1,0:T(4,128)S(1)} %slice_select_fusion.1), channel_id=1, source_target_pairs={{1,4},{3,6},{5,8},{7,10},{9,12},{11,14},{13,16},{15,18},{17,20},{1... | collective-permute-start | bytes 24584 | tf_op jit(solution)/shard_map/ppermute | solution.py:419
  80.1 5.6 %collective-permute-start.11 = (f32[8,512]{1,0:T(8,128)S(1)}, f32[8,512]{1,0:T(8,128)S(1)}, u32[]{:S(2)}, u32[]{:S(2)}) collective-permute-start(f32[8,512]{1,0:T(8,128)S(1)} %select_add_fusion), channel_id=1, source_target_pairs={{0,1},{2,3},{4,5},{6,7},{8,9},{10,11},{12,13},{14,15},{16,17},{18,... | collective-permute-start | bytes 49160 | tf_op jit(solution)/shard_map/ppermute | solution.py:422

commit v7 on v6

--- a/solution.py
+++ b/solution.py
@@ -164,7 +164,7 @@
                 def _():
                     acc[r, slot] = acc_before[r, slot]
 
-                @pl.when(jnp.logical_not(touched))
+                @pl.when(jnp.logical_not(touched) & (field(r, 0, slot) == slot))
                 def _():
                     out[r, slot] = out_before[r, slot]
     else:
@@ -188,7 +188,7 @@
     for r in range(rows_here):
         for slot in range(slot_total):
 
-            @pl.when(field(r, 2, slot) == (1 if late else 0))
+            @pl.when((field(r, 2, slot) == (1 if late else 0)) & (field(r, 0, slot) == slot))
             def _():
                 finish(r, slot)
 

time: 90.1 us -> 90.3 us (level)
  waiting for transfers between devices: 22.4 us -> 23.9 us
  transfers between devices with their start and end apart: 12 -> 12, of which waited for: 6 -> 6; matrix products, arithmetic and copies ran while one was open for 5% -> 5% of each run, Pallas kernels for 27% -> 26%
where the time goes in v7:
time: 90.3 us; the launch traced here: 90.2 us
  Pallas kernels  29.3 us (32%)
  starting transfers between devices  26.6 us (29%)
  waiting for transfers between devices  23.9 us (26%)
  local copies, waits for them, and re-layouts  9.26 us (10%)
    ppermute x2, waiting for transfers between devices, body(): lax.ppermute(piece, AXES, next_chip)  14.3 us
    pallas_call x4, Pallas kernels, expand_split(): pl.pallas_call(functools.partial(split_kernel, q, rows_here, slots, late)...  12.2 us
    pallas_call x2, Pallas kernels, expand(): pl.pallas_call(functools.partial(expand_kernel, q, rows_here, slots), in_...  8.33 us
    ppermute x2, starting transfers between devices, body(): lax.ppermute(piece, AXES, next_chip)  5.7 us
    unnamed x9, local copies, waits for them, and re-layouts  5.67 us
    ppermute x1, starting transfers between devices, body(): other = lax.ppermute(gathered, AXES, swap)  5.56 us
    ppermute x1, waiting for transfers between devices, body(): across.append([lax.ppermute(last, AXES, next_chip)])  4.98 us
    pallas_call x1, Pallas kernels, inflate(): pl.pallas_call(functools.partial(inflate_kernel, scale, slots, first, len...  3.41 us
  transfers between devices with their start and end apart: 12, of which 6 were waited for; matrix products, arithmetic and copies ran while one was open for 5% of the time, Pallas kernels for 26%

profile of v7, /device:TPU:5, one launch (start us, length us, event | category | flops | bytes accessed | tf_op | source)
XLA Modules:
  0.0 90.2 jit_solution(14282000875890577422)
XLA Ops:
  0.0 0.7 collective-permute-start
  0.7 2.1 %slice.18.refs_0_ = bf16[2,3,512,128]{3,2,1,0:T(8,128)(2,1)} slice(bf16[2,3,512,512]{3,2,1,0:T(8,128)(2,1)} %own.11), slice={[0:2], [0:3], [0:512], [0:128]} | slice | bytes 1572864 | tf_op jit(solution)/shard_map/slice | solution.py:373
  2.7 3.1 %collective-permute-start.3 = (bf16[2,3,512,128]{3,2,1,0:T(8,128)(2,1)}, bf16[2,3,512,128]{3,2,1,0:T(8,128)(2,1)}, u32[]{:S(2)}, u32[]{:S(2)}) collective-permute-start(bf16[2,3,512,128]{3,2,1,0:T(8,128)(2,1)} %slice.18.refs_0_), channel_id=1, source_target_pairs={{1,2},{3,4},{5,6},{9,10},{11,12},{13,14},{17,18},{19,20},{21,22},{... | collective-permute-start | bytes 2359304 | tf_op jit(solution)/shard_map/ppermute | solution.py:381
  5.8 1.9 %copy-done = bf16[2,3,512,512]{3,2,1,0:T(8,128)(2,1)S(1)} copy-done((bf16[2,3,512,512]{3,2,1,0:T(8,128)(2,1)S(1)}, bf16[2,3,512,512]{3,2,1,0:T(8,128)(2,1)}, u32[]{:S(2)}) %copy-start) | copy-done | bytes 3145752
  7.7 0.9 %columns1.1.refs_1_.refs_0_ = bf16[2,3,512,128]{3,2,1,0:T(8,128)(2,1)} custom-call(bf16[2,3,512,512]{3,2,1,0:T(8,128)(2,1)S(1)} %copy-done, bf16[2,3,512,128]{3,2,1,0:T(8,128)(2,1)} %slice.18.refs_0_), custom_call_target="tpu_custom_call" | custom-call | bytes 1048576 | tf_op jit(solution)/shard_map/columns1/pallas_call | solution.py:345
  8.7 2.6 %collective-permute-start.2 = (bf16[2,3,512,128]{3,2,1,0:T(8,128)(2,1)}, bf16[2,3,512,128]{3,2,1,0:T(8,128)(2,1)}, u32[]{:S(2)}, u32[]{:S(2)}) collective-permute-start(bf16[2,3,512,128]{3,2,1,0:T(8,128)(2,1)} %columns1.1.refs_1_.refs_0_), channel_id=1, source_target_pairs={{1,2},{3,4},{5,6},{7,8},{9,10},{11,12},{13,14},{15,16},{17,18},{19... | collective-permute-start | bytes 2359304 | tf_op jit(solution)/shard_map/ppermute | solution.py:391
  11.3 1.0 %columns0.1 = bf16[2,3,512,128]{3,2,1,0:T(8,128)(2,1)} custom-call(bf16[2,3,512,512]{3,2,1,0:T(8,128)(2,1)S(1)} %copy-done.1, bf16[2,3,512,128]{3,2,1,0:T(8,128)(2,1)} %columns1.1.refs_1_.refs_0_), custom_call_target="tpu_custom_call" | custom-call | bytes 1048576 | tf_op jit(solution)/shard_map/columns0/pallas_call | solution.py:345
  12.3 1.6 %collective-permute-start.4 = (bf16[2,3,512,128]{3,2,1,0:T(8,128)(2,1)}, bf16[2,3,512,128]{3,2,1,0:T(8,128)(2,1)}, u32[]{:S(2)}, u32[]{:S(2)}) collective-permute-start(bf16[2,3,512,128]{3,2,1,0:T(8,128)(2,1)} %columns0.1), channel_id=1, source_target_pairs={{8,0},{16,1},{15,30},{23,31}} | collective-permute-start | bytes 2359304 | tf_op jit(solution)/shard_map/ppermute | solution.py:380
  14.0 0.6 gather_fusion
  15.8 0.9 %columns2.1 = bf16[2,3,512,128]{3,2,1,0:T(8,128)(2,1)} custom-call(bf16[2,3,512,512]{3,2,1,0:T(8,128)(2,1)S(1)} %copy-done.1, bf16[2,3,512,512]{3,2,1,0:T(8,128)(2,1)} %collective-permute-done.refs_0_, bf16[2,3,512,128]{3,2,1,0:T(8,128)(2,1)} %columns1.1.refs_1_.refs_0_), custom_call_target="tpu_custom_call" | custom-call | bytes 1048576 | tf_op jit(solution)/shard_map/columns2/pallas_call | solution.py:345
  16.7 3.1 %collective-permute-start.1 = (bf16[2,3,512,128]{3,2,1,0:T(8,128)(2,1)}, bf16[2,3,512,128]{3,2,1,0:T(8,128)(2,1)}, u32[]{:S(2)}, u32[]{:S(2)}) collective-permute-start(bf16[2,3,512,128]{3,2,1,0:T(8,128)(2,1)} %columns2.1), channel_id=1, source_target_pairs={{1,2},{3,4},{5,6},{7,8},{9,10},{11,12},{13,14},{15,16},{17,18},{19... | collective-permute-start | bytes 2359304 | tf_op jit(solution)/shard_map/ppermute | solution.py:391
  20.1 0.7 collective-permute-start.5
  20.8 0.7 collective-permute-start.6
  21.5 13.0 %collective-permute-done.2.refs_1_ = bf16[2,3,512,128]{3,2,1,0:T(8,128)(2,1)} collective-permute-done((bf16[2,3,512,128]{3,2,1,0:T(8,128)(2,1)}, bf16[2,3,512,128]{3,2,1,0:T(8,128)(2,1)}, u32[]{:S(2)}, u32[]{:S(2)}) %collective-permute-start.2) | collective-permute-done | bytes 786464 | tf_op jit(solution)/shard_map/ppermute | solution.py:391
  34.6 4.2 %expand1.1 = (bf16[2,9,512,128]{3,2,1,0:T(8,128)(2,1)S(1)}, f32[16,128]{1,0:T(8,128)S(1)}) custom-call(s32[67]{0:T(128)S(1)} %pad_add_fusion.1.meta.refs_2_, bf16[2,3,512,512]{3,2,1,0:T(8,128)(2,1)S(1)} %copy-done.1, bf16[2,3,512,512]{3,2,1,0:T(8,128)(2,1)} %collective-permute-done.refs_0_, bf16[2,3,512,128]{3,2,1,0:T(8,128)(2,1)} %collective-permute-done.2.refs_1_, ...), custom_call_target="tpu_custom_call" | custom-call | flops 1207959552 | bytes 12582912 | tf_op jit(solution)/shard_map/expand1/pallas_call | solution.py:224
  38.9 2.0 %collective-permute-start.7 = (bf16[2,3,512,128]{3,2,1,0:T(8,128)(2,1)S(1)}, bf16[2,3,512,128]{3,2,1,0:T(8,128)(2,1)S(1)}, u32[]{:S(2)}, u32[]{:S(2)}) collective-permute-start(bf16[2,3,512,128]{3,2,1,0:T(8,128)(2,1)S(1)} %columns3.1.before), channel_id=1, source_target_pairs={{1,2},{3,4},{5,6},{7,8},{9,10},{11,12},{13,14},{15,16},{17,18},{19... | collective-permute-start | bytes 2359304 | tf_op jit(solution)/shard_map/ppermute | solution.py:401
  40.9 2.4 %blank.1.refs_1_.refs_4_ = bf16[2,9,512,512]{3,2,1,0:T(8,128)(2,1)} custom-call(s32[67]{0:T(128)S(1)} %pad_add_fusion.1.meta.refs_2_, bf16[2,3,512,128]{3,2,1,0:T(8,128)(2,1)S(1)} %columns3.1.before), custom_call_target="tpu_custom_call" | custom-call | bytes 2097152 | tf_op jit(solution)/shard_map/blank/pallas_call | solution.py:324
  43.3 3.7 %copy-done.2 = bf16[2,9,512,512]{3,2,1,0:T(8,128)(2,1)S(1)} copy-done((bf16[2,9,512,512]{3,2,1,0:T(8,128)(2,1)S(1)}, bf16[2,9,512,512]{3,2,1,0:T(8,128)(2,1)}, u32[]{:S(2)}) %copy-start.2) | copy-done | bytes 9437208
  47.0 3.0 %early3.1 = (f32[2,9,512,128]{3,2,1,0:T(8,128)S(1)}, bf16[2,9,512,128]{3,2,1,0:T(8,128)(2,1)S(1)}, f32[16,128]{1,0:T(8,128)S(1)}) custom-call(s32[67]{0:T(128)S(1)} %pad_add_fusion.1.meta.refs_2_, bf16[2,3,512,512]{3,2,1,0:T(8,128)(2,1)S(1)} %copy-done.1, bf16[2,3,512,512]{3,2,1,0:T(8,128)(2,1)} %collective-permute-done.refs_0_, ...), custom_call_target="tpu_custom_call" | custom-call | flops 603979776 | bytes 8388608 | tf_op jit(solution)/shard_map/early3/pallas_call | solution.py:203
  50.0 1.3 %collective-permute-done.1.refs_1_ = bf16[2,3,512,128]{3,2,1,0:T(8,128)(2,1)} collective-permute-done((bf16[2,3,512,128]{3,2,1,0:T(8,128)(2,1)}, bf16[2,3,512,128]{3,2,1,0:T(8,128)(2,1)}, u32[]{:S(2)}, u32[]{:S(2)}) %collective-permute-start.1) | collective-permute-done | bytes 786464 | tf_op jit(solution)/shard_map/ppermute | solution.py:391
  51.3 4.2 %expand2.1 = (bf16[2,9,512,128]{3,2,1,0:T(8,128)(2,1)S(1)}, f32[16,128]{1,0:T(8,128)S(1)}) custom-call(s32[67]{0:T(128)S(1)} %pad_add_fusion.1.meta.refs_2_, bf16[2,3,512,512]{3,2,1,0:T(8,128)(2,1)S(1)} %copy-done.1, bf16[2,3,512,512]{3,2,1,0:T(8,128)(2,1)} %collective-permute-done.refs_0_, bf16[2,3,512,128]{3,2,1,0:T(8,128)(2,1)} %collective-permute-done.1.refs_1_, ...), custom_call_target="tpu_custom_call" | custom-call | flops 1207959552 | bytes 12582912 | tf_op jit(solution)/shard_map/expand2/pallas_call | solution.py:224
  55.5 3.2 %early0.1 = (f32[2,9,512,128]{3,2,1,0:T(8,128)S(1)}, bf16[2,9,512,128]{3,2,1,0:T(8,128)(2,1)S(1)}, f32[16,128]{1,0:T(8,128)S(1)}) custom-call(s32[67]{0:T(128)S(1)} %pad_add_fusion.1.meta.refs_2_, bf16[2,3,512,512]{3,2,1,0:T(8,128)(2,1)S(1)} %copy-done.1, bf16[2,3,512,512]{3,2,1,0:T(8,128)(2,1)} %collective-permute-done.refs_0_, ...), custom_call_target="tpu_custom_call" | custom-call | flops 603979776 | bytes 8388608 | tf_op jit(solution)/shard_map/early0/pallas_call | solution.py:203
  58.7 3.1 %late0.1 = (bf16[2,9,512,128]{3,2,1,0:T(8,128)(2,1)S(1)}, f32[16,128]{1,0:T(8,128)S(1)}) custom-call(s32[67]{0:T(128)S(1)} %pad_add_fusion.1.meta.refs_2_, bf16[2,3,512,512]{3,2,1,0:T(8,128)(2,1)S(1)} %copy-done.1, f32[2,9,512,128]{3,2,1,0:T(8,128)S(1)} %get-tuple-element.22.refs_0_, bf16[2,9,512,128]{3,2,1,0:T(8,128)(2,1)S(1)} %get-tuple-element.23.refs_1_, ...), custom_call_target="tpu_custom_call" | custom-call | flops 603979776 | bytes 8388608 | tf_op jit(solution)/shard_map/late0/pallas_call | solution.py:203
  61.8 5.0 %collective-permute-done.7.refs_3_ = bf16[2,3,512,128]{3,2,1,0:T(8,128)(2,1)S(1)} collective-permute-done((bf16[2,3,512,128]{3,2,1,0:T(8,128)(2,1)S(1)}, bf16[2,3,512,128]{3,2,1,0:T(8,128)(2,1)S(1)}, u32[]{:S(2)}, u32[]{:S(2)}) %collective-permute-start.7) | collective-permute-done | bytes 786464 | tf_op jit(solution)/shard_map/ppermute | solution.py:401
  66.8 2.9 %late3.1 = (bf16[2,9,512,128]{3,2,1,0:T(8,128)(2,1)S(1)}, f32[16,128]{1,0:T(8,128)S(1)}) custom-call(s32[67]{0:T(128)S(1)} %pad_add_fusion.1.meta.refs_2_, bf16[2,3,512,512]{3,2,1,0:T(8,128)(2,1)S(1)} %copy-done.1, f32[2,9,512,128]{3,2,1,0:T(8,128)S(1)} %get-tuple-element.26.refs_0_, bf16[2,9,512,128]{3,2,1,0:T(8,128)(2,1)S(1)} %get-tuple-element.27.refs_1_, ...), custom_call_target="tpu_custom_call" | custom-call | flops 603979776 | bytes 8388608 | tf_op jit(solution)/shard_map/late3/pallas_call | solution.py:203
  69.8 1.2 %collective-permute-done.8 = f32[12,512]{1,0:T(8,128)S(1)} collective-permute-done((f32[12,512]{1,0:T(8,128)S(1)}, f32[12,512]{1,0:T(8,128)S(1)}, u32[]{:S(2)}, u32[]{:S(2)}) %collective-permute-start.8) | collective-permute-done | bytes 24608 | tf_op jit(solution)/shard_map/ppermute | solution.py:415
  71.0 3.3 %collective-permute-start.9 = (f32[8,512]{1,0:T(8,128)S(1)}, f32[8,512]{1,0:T(8,128)S(1)}, u32[]{:S(2)}, u32[]{:S(2)}) collective-permute-start(f32[8,512]{1,0:T(8,128)S(1)} %slice_select_fusion), channel_id=1, source_target_pairs={{1,2},{3,4},{5,6},{7,8},{9,10},{11,12},{13,14},{15,16},{17,18},{19... | collective-permute-start | bytes 49160 | tf_op jit(solution)/shard_map/ppermute | solution.py:418
  74.3 3.3 %collective-permute-start.10 = (f32[4,512]{1,0:T(4,128)S(1)}, f32[4,512]{1,0:T(4,128)S(1)}, u32[]{:S(2)}, u32[]{:S(2)}) collective-permute-start(f32[4,512]{1,0:T(4,128)S(1)} %slice_select_fusion.1), channel_id=1, source_target_pairs={{1,4},{3,6},{5,8},{7,10},{9,12},{11,14},{13,16},{15,18},{17,20},{1... | collective-permute-start | bytes 24584 | tf_op jit(solution)/shard_map/ppermute | solution.py:419
  77.6 2.5 %collective-permute-done.10 = f32[4,512]{1,0:T(4,128)S(1)} collective-permute-done((f32[4,512]{1,0:T(4,128)S(1)}, f32[4,512]{1,0:T(4,128)S(1)}, u32[]{:S(2)}, u32[]{:S(2)}) %collective-permute-start.10) | collective-permute-done | bytes 8224 | tf_op jit(solution)/shard_map/ppermute | solution.py:419
  80.2 5.6 %collective-permute-start.11 = (f32[8,512]{1,0:T(8,128)S(1)}, f32[8,512]{1,0:T(8,128)S(1)}, u32[]{:S(2)}, u32[]{:S(2)}) collective-permute-start(f32[8,512]{1,0:T(8,128)S(1)} %select_add_fusion), channel_id=1, source_target_pairs={{0,1},{2,3},{4,5},{6,7},{8,9},{10,11},{12,13},{14,15},{16,17},{18,... | collective-permute-start | bytes 49160 | tf_op jit(solution)/shard_map/ppermute | solution.py:422
  85.8 0.8 collective-permute-done.11
  86.6 3.4 %inflate0.1 = bf16[2,9,512,512]{3,2,1,0:T(8,128)(2,1)} custom-call(s32[67]{0:T(128)S(1)} %pad_add_fusion.1.meta.refs_2_, f32[12,512]{1,0:T(8,128)S(1)} %pad_add_fusion.totals, bf16[2,9,512,128]{3,2,1,0:T(8,128)(2,1)S(1)} %get-tuple-element.29.refs_0_, bf16[2,9,512,128]{3,2,1,0:T(8,128)(2,1)S(1)} %get-tuple-element.30.refs_1_, ...), custom_call_target="tpu_custom_call", output_to_operand_aliasing={{}: (6, {})} | custom-call | flops 16777216 | bytes 16777216 | tf_op jit(solution)/shard_map/inflate0/pallas_call | solution.py:292
  (42 shorter events, 1.9 us)
Async XLA Ops:
  0.0 15.7 %collective-permute-start = (bf16[2,3,512,512]{3,2,1,0:T(8,128)(2,1)}, bf16[2,3,512,512]{3,2,1,0:T(8,128)(2,1)}, u32[]{:S(2)}, u32[]{:S(2)}) collective-permute-start(bf16[2,3,512,512]{3,2,1,0:T(8,128)(2,1)} %own.11), channel_id=1, source_target_pairs={{0,1},{2,3},{4,5},{6,7},{8,9},{10,11},{12,13},{14,15},{16,17},{18,... | collective-permute-start | bytes 9437192 | tf_op jit(solution)/shard_map/ppermute | solution.py:372
  2.7 17.4 %collective-permute-start.3 = (bf16[2,3,512,128]{3,2,1,0:T(8,128)(2,1)}, bf16[2,3,512,128]{3,2,1,0:T(8,128)(2,1)}, u32[]{:S(2)}, u32[]{:S(2)}) collective-permute-start(bf16[2,3,512,128]{3,2,1,0:T(8,128)(2,1)} %slice.18.refs_0_), channel_id=1, source_target_pairs={{1,2},{3,4},{5,6},{9,10},{11,12},{13,14},{17,18},{19,20},{21,22},{... | collective-permute-start | bytes 2359304 | tf_op jit(solution)/shard_map/ppermute | solution.py:381
  5.8 1.9 %copy-start = (bf16[2,3,512,512]{3,2,1,0:T(8,128)(2,1)S(1)}, bf16[2,3,512,512]{3,2,1,0:T(8,128)(2,1)}, u32[]{:S(2)}) copy-start(bf16[2,3,512,512]{3,2,1,0:T(8,128)(2,1)} %own.11) | copy-start | bytes 9437188
  7.7 3.6 %copy-start.1 = (bf16[2,3,512,512]{3,2,1,0:T(8,128)(2,1)S(1)}, bf16[2,3,512,512]{3,2,1,0:T(8,128)(2,1)}, u32[]{:S(2)}) copy-start(bf16[2,3,512,512]{3,2,1,0:T(8,128)(2,1)} %own.11) | copy-start | bytes 9437188
  8.7 5.2 %copy-start.3 = (s32[64,3]{0,1:T(4,128)S(1)}, s32[64,3]{0,1:T(4,128)}, u32[]{:S(2)}) copy-start(s32[64,3]{0,1:T(4,128)} %param.3) | copy-start | bytes 2308
  8.7 25.9 %collective-permute-start.2 = (bf16[2,3,512,128]{3,2,1,0:T(8,128)(2,1)}, bf16[2,3,512,128]{3,2,1,0:T(8,128)(2,1)}, u32[]{:S(2)}, u32[]{:S(2)}) collective-permute-start(bf16[2,3,512,128]{3,2,1,0:T(8,128)(2,1)} %columns1.1.refs_1_.refs_0_), channel_id=1, source_target_pairs={{1,2},{3,4},{5,6},{7,8},{9,10},{11,12},{13,14},{15,16},{17,18},{19... | collective-permute-start | bytes 2359304 | tf_op jit(solution)/shard_map/ppermute | solution.py:391
  12.3 8.5 %collective-permute-start.4 = (bf16[2,3,512,128]{3,2,1,0:T(8,128)(2,1)}, bf16[2,3,512,128]{3,2,1,0:T(8,128)(2,1)}, u32[]{:S(2)}, u32[]{:S(2)}) collective-permute-start(bf16[2,3,512,128]{3,2,1,0:T(8,128)(2,1)} %columns0.1), channel_id=1, source_target_pairs={{8,0},{16,1},{15,30},{23,31}} | collective-permute-start | bytes 2359304 | tf_op jit(solution)/shard_map/ppermute | solution.py:380
  16.7 34.6 %collective-permute-start.1 = (bf16[2,3,512,128]{3,2,1,0:T(8,128)(2,1)}, bf16[2,3,512,128]{3,2,1,0:T(8,128)(2,1)}, u32[]{:S(2)}, u32[]{:S(2)}) collective-permute-start(bf16[2,3,512,128]{3,2,1,0:T(8,128)(2,1)} %columns2.1), channel_id=1, source_target_pairs={{1,2},{3,4},{5,6},{7,8},{9,10},{11,12},{13,14},{15,16},{17,18},{19... | collective-permute-start | bytes 2359304 | tf_op jit(solution)/shard_map/ppermute | solution.py:391
  20.1 38.6 %collective-permute-start.5 = (bf16[2,3,512,128]{3,2,1,0:T(8,128)(2,1)}, bf16[2,3,512,128]{3,2,1,0:T(8,128)(2,1)S(1)}, u32[]{:S(2)}, u32[]{:S(2)}) collective-permute-start(bf16[2,3,512,128]{3,2,1,0:T(8,128)(2,1)} %collective-permute-done.3.refs_1_.refs_3_), channel_id=1, source_target_pairs={{31,8},{0,23}} | collective-permute-start | bytes 2359304 | tf_op jit(solution)/shard_map/ppermute | solution.py:382
  20.8 37.9 %collective-permute-start.6 = (bf16[2,3,512,128]{3,2,1,0:T(8,128)(2,1)}, bf16[2,3,512,128]{3,2,1,0:T(8,128)(2,1)S(1)}, u32[]{:S(2)}, u32[]{:S(2)}) collective-permute-start(bf16[2,3,512,128]{3,2,1,0:T(8,128)(2,1)} %collective-permute-done.4.refs_2_), channel_id=1, source_target_pairs={{0,7},{1,15},{30,16},{31,24}} | collective-permute-start | bytes 2359304 | tf_op jit(solution)/shard_map/ppermute | solution.py:382
  38.9 27.9 %collective-permute-start.7 = (bf16[2,3,512,128]{3,2,1,0:T(8,128)(2,1)S(1)}, bf16[2,3,512,128]{3,2,1,0:T(8,128)(2,1)S(1)}, u32[]{:S(2)}, u32[]{:S(2)}) collective-permute-start(bf16[2,3,512,128]{3,2,1,0:T(8,128)(2,1)S(1)} %columns3.1.before), channel_id=1, source_target_pairs={{1,2},{3,4},{5,6},{7,8},{9,10},{11,12},{13,14},{15,16},{17,18},{19... | collective-permute-start | bytes 2359304 | tf_op jit(solution)/shard_map/ppermute | solution.py:401
  43.3 3.7 %copy-start.2 = (bf16[2,9,512,512]{3,2,1,0:T(8,128)(2,1)S(1)}, bf16[2,9,512,512]{3,2,1,0:T(8,128)(2,1)}, u32[]{:S(2)}) copy-start(bf16[2,9,512,512]{3,2,1,0:T(8,128)(2,1)} %blank.1.refs_1_.refs_4_) | copy-start | bytes 28311556
  69.7 1.3 %collective-permute-start.8 = (f32[12,512]{1,0:T(8,128)S(1)}, f32[12,512]{1,0:T(8,128)S(1)}, u32[]{:S(2)}, u32[]{:S(2)}) collective-permute-start(f32[12,512]{1,0:T(8,128)S(1)} %pad_maximum_fusion), channel_id=1, source_target_pairs={{0,1},{2,3},{4,5},{6,7},{8,9},{10,11},{12,13},{14,15},{16,17},{18,... | collective-permute-start | bytes 73736 | tf_op jit(solution)/shard_map/ppermute | solution.py:415
  71.0 9.2 %collective-permute-start.9 = (f32[8,512]{1,0:T(8,128)S(1)}, f32[8,512]{1,0:T(8,128)S(1)}, u32[]{:S(2)}, u32[]{:S(2)}) collective-permute-start(f32[8,512]{1,0:T(8,128)S(1)} %slice_select_fusion), channel_id=1, source_target_pairs={{1,2},{3,4},{5,6},{7,8},{9,10},{11,12},{13,14},{15,16},{17,18},{19... | collective-permute-start | bytes 49160 | tf_op jit(solution)/shard_map/ppermute | solution.py:418
  74.3 5.9 %collective-permute-start.10 = (f32[4,512]{1,0:T(4,128)S(1)}, f32[4,512]{1,0:T(4,128)S(1)}, u32[]{:S(2)}, u32[]{:S(2)}) collective-permute-start(f32[4,512]{1,0:T(4,128)S(1)} %slice_select_fusion.1), channel_id=1, source_target_pairs={{1,4},{3,6},{5,8},{7,10},{9,12},{11,14},{13,16},{15,18},{17,20},{1... | collective-permute-start | bytes 24584 | tf_op jit(solution)/shard_map/ppermute | solution.py:419
  80.2 6.4 %collective-permute-start.11 = (f32[8,512]{1,0:T(8,128)S(1)}, f32[8,512]{1,0:T(8,128)S(1)}, u32[]{:S(2)}, u32[]{:S(2)}) collective-permute-start(f32[8,512]{1,0:T(8,128)S(1)} %select_add_fusion), channel_id=1, source_target_pairs={{0,1},{2,3},{4,5},{6,7},{8,9},{10,11},{12,13},{14,15},{16,17},{18,... | collective-permute-start | bytes 49160 | tf_op jit(solution)/shard_map/ppermute | solution.py:422

commit v8 on v6

--- a/solution.py
+++ b/solution.py
@@ -295,8 +295,8 @@
         out_specs=anywhere,
         out_shape=jax.ShapeDtypeStruct((rows_here, slot_total, side, width * CHUNKS), jnp.bfloat16),
         scratch_shapes=[
-            pltpu.VMEM((9, side, width * len(parts)), jnp.bfloat16),
-            pltpu.SemaphoreType.DMA((9,)),
+            pltpu.VMEM((12, side, width * len(parts)), jnp.bfloat16),
+            pltpu.SemaphoreType.DMA((12,)),
         ],
         input_output_aliases={2 + len(parts): 0} if more else {},
         compiler_params=pltpu.CompilerParams(vmem_limit_bytes=12 * 2**20),

time: 90.1 us -> 90.4 us (level)
    ppermute x1, starting transfers between devices: 3.02 us -> 3.93 us  [body(): lax.ppermute(jnp.where(low, chip[:near], chip[used - near:]), AXES, next_...]
where the time goes in v8:
time: 90.4 us; the launch traced here: 90.1 us
  Pallas kernels  30.2 us (33%)
  starting transfers between devices  26.5 us (29%)
  waiting for transfers between devices  23.1 us (26%)
  local copies, waits for them, and re-layouts  9.26 us (10%)
    ppermute x2, waiting for transfers between devices, body(): lax.ppermute(piece, AXES, next_chip)  13.7 us
    pallas_call x4, Pallas kernels, expand_split(): pl.pallas_call(functools.partial(split_kernel, q, rows_here, slots, late)...  13 us
    pallas_call x2, Pallas kernels, expand(): pl.pallas_call(functools.partial(expand_kernel, q, rows_here, slots), in_...  8.33 us
    ppermute x2, starting transfers between devices, body(): lax.ppermute(piece, AXES, next_chip)  5.7 us
    unnamed x9, local copies, waits for them, and re-layouts  5.67 us
    ppermute x1, starting transfers between devices, body(): other = lax.ppermute(gathered, AXES, swap)  4.96 us
    ppermute x1, waiting for transfers between devices, body(): across.append([lax.ppermute(last, AXES, next_chip)])  4.62 us
    ppermute x1, starting transfers between devices, body(): lax.ppermute(jnp.where(low, chip[:near], chip[used - near:]), AXES, next_...  3.93 us
  transfers between devices with their start and end apart: 12, of which 6 were waited for; matrix products, arithmetic and copies ran while one was open for 5% of the time, Pallas kernels for 27%

profile of v8, /device:TPU:5, one launch (start us, length us, event | category | flops | bytes accessed | tf_op | source)
XLA Modules:
  0.0 90.1 jit_solution(657830739747029620)
XLA Ops:
  0.0 0.7 collective-permute-start
  0.7 2.1 %slice.18.refs_0_ = bf16[2,3,512,128]{3,2,1,0:T(8,128)(2,1)} slice(bf16[2,3,512,512]{3,2,1,0:T(8,128)(2,1)} %own.11), slice={[0:2], [0:3], [0:512], [0:128]} | slice | bytes 1572864 | tf_op jit(solution)/shard_map/slice | solution.py:373
  2.7 3.1 %collective-permute-start.3 = (bf16[2,3,512,128]{3,2,1,0:T(8,128)(2,1)}, bf16[2,3,512,128]{3,2,1,0:T(8,128)(2,1)}, u32[]{:S(2)}, u32[]{:S(2)}) collective-permute-start(bf16[2,3,512,128]{3,2,1,0:T(8,128)(2,1)} %slice.18.refs_0_), channel_id=1, source_target_pairs={{1,2},{3,4},{5,6},{9,10},{11,12},{13,14},{17,18},{19,20},{21,22},{... | collective-permute-start | bytes 2359304 | tf_op jit(solution)/shard_map/ppermute | solution.py:381
  5.8 1.9 %copy-done = bf16[2,3,512,512]{3,2,1,0:T(8,128)(2,1)S(1)} copy-done((bf16[2,3,512,512]{3,2,1,0:T(8,128)(2,1)S(1)}, bf16[2,3,512,512]{3,2,1,0:T(8,128)(2,1)}, u32[]{:S(2)}) %copy-start) | copy-done | bytes 3145752
  7.7 0.9 %columns1.1.refs_1_.refs_0_ = bf16[2,3,512,128]{3,2,1,0:T(8,128)(2,1)} custom-call(bf16[2,3,512,512]{3,2,1,0:T(8,128)(2,1)S(1)} %copy-done, bf16[2,3,512,128]{3,2,1,0:T(8,128)(2,1)} %slice.18.refs_0_), custom_call_target="tpu_custom_call" | custom-call | bytes 1048576 | tf_op jit(solution)/shard_map/columns1/pallas_call | solution.py:345
  8.7 2.6 %collective-permute-start.2 = (bf16[2,3,512,128]{3,2,1,0:T(8,128)(2,1)}, bf16[2,3,512,128]{3,2,1,0:T(8,128)(2,1)}, u32[]{:S(2)}, u32[]{:S(2)}) collective-permute-start(bf16[2,3,512,128]{3,2,1,0:T(8,128)(2,1)} %columns1.1.refs_1_.refs_0_), channel_id=1, source_target_pairs={{1,2},{3,4},{5,6},{7,8},{9,10},{11,12},{13,14},{15,16},{17,18},{19... | collective-permute-start | bytes 2359304 | tf_op jit(solution)/shard_map/ppermute | solution.py:391
  11.3 1.0 %columns0.1 = bf16[2,3,512,128]{3,2,1,0:T(8,128)(2,1)} custom-call(bf16[2,3,512,512]{3,2,1,0:T(8,128)(2,1)S(1)} %copy-done.1, bf16[2,3,512,128]{3,2,1,0:T(8,128)(2,1)} %columns1.1.refs_1_.refs_0_), custom_call_target="tpu_custom_call" | custom-call | bytes 1048576 | tf_op jit(solution)/shard_map/columns0/pallas_call | solution.py:345
  12.3 1.6 %collective-permute-start.4 = (bf16[2,3,512,128]{3,2,1,0:T(8,128)(2,1)}, bf16[2,3,512,128]{3,2,1,0:T(8,128)(2,1)}, u32[]{:S(2)}, u32[]{:S(2)}) collective-permute-start(bf16[2,3,512,128]{3,2,1,0:T(8,128)(2,1)} %columns0.1), channel_id=1, source_target_pairs={{8,0},{16,1},{15,30},{23,31}} | collective-permute-start | bytes 2359304 | tf_op jit(solution)/shard_map/ppermute | solution.py:380
  14.0 0.6 gather_fusion
  15.8 0.9 %columns2.1 = bf16[2,3,512,128]{3,2,1,0:T(8,128)(2,1)} custom-call(bf16[2,3,512,512]{3,2,1,0:T(8,128)(2,1)S(1)} %copy-done.1, bf16[2,3,512,512]{3,2,1,0:T(8,128)(2,1)} %collective-permute-done.refs_0_, bf16[2,3,512,128]{3,2,1,0:T(8,128)(2,1)} %columns1.1.refs_1_.refs_0_), custom_call_target="tpu_custom_call" | custom-call | bytes 1048576 | tf_op jit(solution)/shard_map/columns2/pallas_call | solution.py:345
  16.7 3.1 %collective-permute-start.1 = (bf16[2,3,512,128]{3,2,1,0:T(8,128)(2,1)}, bf16[2,3,512,128]{3,2,1,0:T(8,128)(2,1)}, u32[]{:S(2)}, u32[]{:S(2)}) collective-permute-start(bf16[2,3,512,128]{3,2,1,0:T(8,128)(2,1)} %columns2.1), channel_id=1, source_target_pairs={{1,2},{3,4},{5,6},{7,8},{9,10},{11,12},{13,14},{15,16},{17,18},{19... | collective-permute-start | bytes 2359304 | tf_op jit(solution)/shard_map/ppermute | solution.py:391
  20.1 0.7 collective-permute-start.5
  20.8 0.7 collective-permute-start.6
  21.5 13.0 %collective-permute-done.2.refs_1_ = bf16[2,3,512,128]{3,2,1,0:T(8,128)(2,1)} collective-permute-done((bf16[2,3,512,128]{3,2,1,0:T(8,128)(2,1)}, bf16[2,3,512,128]{3,2,1,0:T(8,128)(2,1)}, u32[]{:S(2)}, u32[]{:S(2)}) %collective-permute-start.2) | collective-permute-done | bytes 786464 | tf_op jit(solution)/shard_map/ppermute | solution.py:391
  34.6 4.2 %expand1.1 = (bf16[2,9,512,128]{3,2,1,0:T(8,128)(2,1)S(1)}, f32[16,128]{1,0:T(8,128)S(1)}) custom-call(s32[67]{0:T(128)S(1)} %pad_add_fusion.1.meta.refs_2_, bf16[2,3,512,512]{3,2,1,0:T(8,128)(2,1)S(1)} %copy-done.1, bf16[2,3,512,512]{3,2,1,0:T(8,128)(2,1)} %collective-permute-done.refs_0_, bf16[2,3,512,128]{3,2,1,0:T(8,128)(2,1)} %collective-permute-done.2.refs_1_, ...), custom_call_target="tpu_custom_call" | custom-call | flops 1207959552 | bytes 12582912 | tf_op jit(solution)/shard_map/expand1/pallas_call | solution.py:224
  38.9 2.0 %collective-permute-start.7 = (bf16[2,3,512,128]{3,2,1,0:T(8,128)(2,1)S(1)}, bf16[2,3,512,128]{3,2,1,0:T(8,128)(2,1)S(1)}, u32[]{:S(2)}, u32[]{:S(2)}) collective-permute-start(bf16[2,3,512,128]{3,2,1,0:T(8,128)(2,1)S(1)} %columns3.1.before), channel_id=1, source_target_pairs={{1,2},{3,4},{5,6},{7,8},{9,10},{11,12},{13,14},{15,16},{17,18},{19... | collective-permute-start | bytes 2359304 | tf_op jit(solution)/shard_map/ppermute | solution.py:401
  40.9 2.6 %blank.1.refs_1_.refs_4_ = bf16[2,9,512,512]{3,2,1,0:T(8,128)(2,1)} custom-call(s32[67]{0:T(128)S(1)} %pad_add_fusion.1.meta.refs_2_, bf16[2,3,512,128]{3,2,1,0:T(8,128)(2,1)S(1)} %columns3.1.before), custom_call_target="tpu_custom_call" | custom-call | bytes 2097152 | tf_op jit(solution)/shard_map/blank/pallas_call | solution.py:324
  43.5 3.7 %copy-done.2 = bf16[2,9,512,512]{3,2,1,0:T(8,128)(2,1)S(1)} copy-done((bf16[2,9,512,512]{3,2,1,0:T(8,128)(2,1)S(1)}, bf16[2,9,512,512]{3,2,1,0:T(8,128)(2,1)}, u32[]{:S(2)}) %copy-start.2) | copy-done | bytes 9437208
  47.1 3.5 %early3.1 = (f32[2,9,512,128]{3,2,1,0:T(8,128)S(1)}, bf16[2,9,512,128]{3,2,1,0:T(8,128)(2,1)S(1)}, f32[16,128]{1,0:T(8,128)S(1)}) custom-call(s32[67]{0:T(128)S(1)} %pad_add_fusion.1.meta.refs_2_, bf16[2,3,512,512]{3,2,1,0:T(8,128)(2,1)S(1)} %copy-done.1, bf16[2,3,512,512]{3,2,1,0:T(8,128)(2,1)} %collective-permute-done.refs_0_, ...), custom_call_target="tpu_custom_call" | custom-call | flops 603979776 | bytes 8388608 | tf_op jit(solution)/shard_map/early3/pallas_call | solution.py:203
  50.7 0.6 collective-permute-done.1.refs_1_
  51.3 4.2 %expand2.1 = (bf16[2,9,512,128]{3,2,1,0:T(8,128)(2,1)S(1)}, f32[16,128]{1,0:T(8,128)S(1)}) custom-call(s32[67]{0:T(128)S(1)} %pad_add_fusion.1.meta.refs_2_, bf16[2,3,512,512]{3,2,1,0:T(8,128)(2,1)S(1)} %copy-done.1, bf16[2,3,512,512]{3,2,1,0:T(8,128)(2,1)} %collective-permute-done.refs_0_, bf16[2,3,512,128]{3,2,1,0:T(8,128)(2,1)} %collective-permute-done.1.refs_1_, ...), custom_call_target="tpu_custom_call" | custom-call | flops 1207959552 | bytes 12582912 | tf_op jit(solution)/shard_map/expand2/pallas_call | solution.py:224
  55.5 3.6 %early0.1 = (f32[2,9,512,128]{3,2,1,0:T(8,128)S(1)}, bf16[2,9,512,128]{3,2,1,0:T(8,128)(2,1)S(1)}, f32[16,128]{1,0:T(8,128)S(1)}) custom-call(s32[67]{0:T(128)S(1)} %pad_add_fusion.1.meta.refs_2_, bf16[2,3,512,512]{3,2,1,0:T(8,128)(2,1)S(1)} %copy-done.1, bf16[2,3,512,512]{3,2,1,0:T(8,128)(2,1)} %collective-permute-done.refs_0_, ...), custom_call_target="tpu_custom_call" | custom-call | flops 603979776 | bytes 8388608 | tf_op jit(solution)/shard_map/early0/pallas_call | solution.py:203
  59.1 3.1 %late0.1 = (bf16[2,9,512,128]{3,2,1,0:T(8,128)(2,1)S(1)}, f32[16,128]{1,0:T(8,128)S(1)}) custom-call(s32[67]{0:T(128)S(1)} %pad_add_fusion.1.meta.refs_2_, bf16[2,3,512,512]{3,2,1,0:T(8,128)(2,1)S(1)} %copy-done.1, f32[2,9,512,128]{3,2,1,0:T(8,128)S(1)} %get-tuple-element.22.refs_0_, bf16[2,9,512,128]{3,2,1,0:T(8,128)(2,1)S(1)} %get-tuple-element.23.refs_1_, ...), custom_call_target="tpu_custom_call" | custom-call | flops 603979776 | bytes 8388608 | tf_op jit(solution)/shard_map/late0/pallas_call | solution.py:203
  62.2 4.6 %collective-permute-done.7.refs_3_ = bf16[2,3,512,128]{3,2,1,0:T(8,128)(2,1)S(1)} collective-permute-done((bf16[2,3,512,128]{3,2,1,0:T(8,128)(2,1)S(1)}, bf16[2,3,512,128]{3,2,1,0:T(8,128)(2,1)S(1)}, u32[]{:S(2)}, u32[]{:S(2)}) %collective-permute-start.7) | collective-permute-done | bytes 786464 | tf_op jit(solution)/shard_map/ppermute | solution.py:401
  66.8 2.8 %late3.1 = (bf16[2,9,512,128]{3,2,1,0:T(8,128)(2,1)S(1)}, f32[16,128]{1,0:T(8,128)S(1)}) custom-call(s32[67]{0:T(128)S(1)} %pad_add_fusion.1.meta.refs_2_, bf16[2,3,512,512]{3,2,1,0:T(8,128)(2,1)S(1)} %copy-done.1, f32[2,9,512,128]{3,2,1,0:T(8,128)S(1)} %get-tuple-element.26.refs_0_, bf16[2,9,512,128]{3,2,1,0:T(8,128)(2,1)S(1)} %get-tuple-element.27.refs_1_, ...), custom_call_target="tpu_custom_call" | custom-call | flops 603979776 | bytes 8388608 | tf_op jit(solution)/shard_map/late3/pallas_call | solution.py:203
  69.8 1.2 %collective-permute-done.8 = f32[12,512]{1,0:T(8,128)S(1)} collective-permute-done((f32[12,512]{1,0:T(8,128)S(1)}, f32[12,512]{1,0:T(8,128)S(1)}, u32[]{:S(2)}, u32[]{:S(2)}) %collective-permute-start.8) | collective-permute-done | bytes 24608 | tf_op jit(solution)/shard_map/ppermute | solution.py:415
  71.0 3.9 %collective-permute-start.9 = (f32[8,512]{1,0:T(8,128)S(1)}, f32[8,512]{1,0:T(8,128)S(1)}, u32[]{:S(2)}, u32[]{:S(2)}) collective-permute-start(f32[8,512]{1,0:T(8,128)S(1)} %slice_select_fusion), channel_id=1, source_target_pairs={{1,2},{3,4},{5,6},{7,8},{9,10},{11,12},{13,14},{15,16},{17,18},{19... | collective-permute-start | bytes 49160 | tf_op jit(solution)/shard_map/ppermute | solution.py:418
  74.9 3.1 %collective-permute-start.10 = (f32[4,512]{1,0:T(4,128)S(1)}, f32[4,512]{1,0:T(4,128)S(1)}, u32[]{:S(2)}, u32[]{:S(2)}) collective-permute-start(f32[4,512]{1,0:T(4,128)S(1)} %slice_select_fusion.1), channel_id=1, source_target_pairs={{1,4},{3,6},{5,8},{7,10},{9,12},{11,14},{13,16},{15,18},{17,20},{1... | collective-permute-start | bytes 24584 | tf_op jit(solution)/shard_map/ppermute | solution.py:419
  78.1 2.7 %collective-permute-done.10 = f32[4,512]{1,0:T(4,128)S(1)} collective-permute-done((f32[4,512]{1,0:T(4,128)S(1)}, f32[4,512]{1,0:T(4,128)S(1)}, u32[]{:S(2)}, u32[]{:S(2)}) %collective-permute-start.10) | collective-permute-done | bytes 8224 | tf_op jit(solution)/shard_map/ppermute | solution.py:419
  80.8 5.0 %collective-permute-start.11 = (f32[8,512]{1,0:T(8,128)S(1)}, f32[8,512]{1,0:T(8,128)S(1)}, u32[]{:S(2)}, u32[]{:S(2)}) collective-permute-start(f32[8,512]{1,0:T(8,128)S(1)} %select_add_fusion), channel_id=1, source_target_pairs={{0,1},{2,3},{4,5},{6,7},{8,9},{10,11},{12,13},{14,15},{16,17},{18,... | collective-permute-start | bytes 49160 | tf_op jit(solution)/shard_map/ppermute | solution.py:422
  85.8 0.8 collective-permute-done.11
  86.6 3.3 %inflate0.1 = bf16[2,9,512,512]{3,2,1,0:T(8,128)(2,1)} custom-call(s32[67]{0:T(128)S(1)} %pad_add_fusion.1.meta.refs_2_, f32[12,512]{1,0:T(8,128)S(1)} %pad_add_fusion.totals, bf16[2,9,512,128]{3,2,1,0:T(8,128)(2,1)S(1)} %get-tuple-element.29.refs_0_, bf16[2,9,512,128]{3,2,1,0:T(8,128)(2,1)S(1)} %get-tuple-element.30.refs_1_, ...), custom_call_target="tpu_custom_call", output_to_operand_aliasing={{}: (6, {})} | custom-call | flops 16777216 | bytes 16777216 | tf_op jit(solution)/shard_map/inflate0/pallas_call | solution.py:292
  (42 shorter events, 1.9 us)
Async XLA Ops:
  0.0 15.7 %collective-permute-start = (bf16[2,3,512,512]{3,2,1,0:T(8,128)(2,1)}, bf16[2,3,512,512]{3,2,1,0:T(8,128)(2,1)}, u32[]{:S(2)}, u32[]{:S(2)}) collective-permute-start(bf16[2,3,512,512]{3,2,1,0:T(8,128)(2,1)} %own.11), channel_id=1, source_target_pairs={{0,1},{2,3},{4,5},{6,7},{8,9},{10,11},{12,13},{14,15},{16,17},{18,... | collective-permute-start | bytes 9437192 | tf_op jit(solution)/shard_map/ppermute | solution.py:372
  2.7 17.4 %collective-permute-start.3 = (bf16[2,3,512,128]{3,2,1,0:T(8,128)(2,1)}, bf16[2,3,512,128]{3,2,1,0:T(8,128)(2,1)}, u32[]{:S(2)}, u32[]{:S(2)}) collective-permute-start(bf16[2,3,512,128]{3,2,1,0:T(8,128)(2,1)} %slice.18.refs_0_), channel_id=1, source_target_pairs={{1,2},{3,4},{5,6},{9,10},{11,12},{13,14},{17,18},{19,20},{21,22},{... | collective-permute-start | bytes 2359304 | tf_op jit(solution)/shard_map/ppermute | solution.py:381
  5.8 1.9 %copy-start = (bf16[2,3,512,512]{3,2,1,0:T(8,128)(2,1)S(1)}, bf16[2,3,512,512]{3,2,1,0:T(8,128)(2,1)}, u32[]{:S(2)}) copy-start(bf16[2,3,512,512]{3,2,1,0:T(8,128)(2,1)} %own.11) | copy-start | bytes 9437188
  7.7 3.6 %copy-start.1 = (bf16[2,3,512,512]{3,2,1,0:T(8,128)(2,1)S(1)}, bf16[2,3,512,512]{3,2,1,0:T(8,128)(2,1)}, u32[]{:S(2)}) copy-start(bf16[2,3,512,512]{3,2,1,0:T(8,128)(2,1)} %own.11) | copy-start | bytes 9437188
  8.7 5.2 %copy-start.3 = (s32[64,3]{0,1:T(4,128)S(1)}, s32[64,3]{0,1:T(4,128)}, u32[]{:S(2)}) copy-start(s32[64,3]{0,1:T(4,128)} %param.3) | copy-start | bytes 2308
  8.7 25.9 %collective-permute-start.2 = (bf16[2,3,512,128]{3,2,1,0:T(8,128)(2,1)}, bf16[2,3,512,128]{3,2,1,0:T(8,128)(2,1)}, u32[]{:S(2)}, u32[]{:S(2)}) collective-permute-start(bf16[2,3,512,128]{3,2,1,0:T(8,128)(2,1)} %columns1.1.refs_1_.refs_0_), channel_id=1, source_target_pairs={{1,2},{3,4},{5,6},{7,8},{9,10},{11,12},{13,14},{15,16},{17,18},{19... | collective-permute-start | bytes 2359304 | tf_op jit(solution)/shard_map/ppermute | solution.py:391
  12.3 8.5 %collective-permute-start.4 = (bf16[2,3,512,128]{3,2,1,0:T(8,128)(2,1)}, bf16[2,3,512,128]{3,2,1,0:T(8,128)(2,1)}, u32[]{:S(2)}, u32[]{:S(2)}) collective-permute-start(bf16[2,3,512,128]{3,2,1,0:T(8,128)(2,1)} %columns0.1), channel_id=1, source_target_pairs={{8,0},{16,1},{15,30},{23,31}} | collective-permute-start | bytes 2359304 | tf_op jit(solution)/shard_map/ppermute | solution.py:380
  16.7 34.6 %collective-permute-start.1 = (bf16[2,3,512,128]{3,2,1,0:T(8,128)(2,1)}, bf16[2,3,512,128]{3,2,1,0:T(8,128)(2,1)}, u32[]{:S(2)}, u32[]{:S(2)}) collective-permute-start(bf16[2,3,512,128]{3,2,1,0:T(8,128)(2,1)} %columns2.1), channel_id=1, source_target_pairs={{1,2},{3,4},{5,6},{7,8},{9,10},{11,12},{13,14},{15,16},{17,18},{19... | collective-permute-start | bytes 2359304 | tf_op jit(solution)/shard_map/ppermute | solution.py:391
  20.1 39.0 %collective-permute-start.5 = (bf16[2,3,512,128]{3,2,1,0:T(8,128)(2,1)}, bf16[2,3,512,128]{3,2,1,0:T(8,128)(2,1)S(1)}, u32[]{:S(2)}, u32[]{:S(2)}) collective-permute-start(bf16[2,3,512,128]{3,2,1,0:T(8,128)(2,1)} %collective-permute-done.3.refs_1_.refs_3_), channel_id=1, source_target_pairs={{31,8},{0,23}} | collective-permute-start | bytes 2359304 | tf_op jit(solution)/shard_map/ppermute | solution.py:382
  20.8 38.3 %collective-permute-start.6 = (bf16[2,3,512,128]{3,2,1,0:T(8,128)(2,1)}, bf16[2,3,512,128]{3,2,1,0:T(8,128)(2,1)S(1)}, u32[]{:S(2)}, u32[]{:S(2)}) collective-permute-start(bf16[2,3,512,128]{3,2,1,0:T(8,128)(2,1)} %collective-permute-done.4.refs_2_), channel_id=1, source_target_pairs={{0,7},{1,15},{30,16},{31,24}} | collective-permute-start | bytes 2359304 | tf_op jit(solution)/shard_map/ppermute | solution.py:382
  38.9 27.9 %collective-permute-start.7 = (bf16[2,3,512,128]{3,2,1,0:T(8,128)(2,1)S(1)}, bf16[2,3,512,128]{3,2,1,0:T(8,128)(2,1)S(1)}, u32[]{:S(2)}, u32[]{:S(2)}) collective-permute-start(bf16[2,3,512,128]{3,2,1,0:T(8,128)(2,1)S(1)} %columns3.1.before), channel_id=1, source_target_pairs={{1,2},{3,4},{5,6},{7,8},{9,10},{11,12},{13,14},{15,16},{17,18},{19... | collective-permute-start | bytes 2359304 | tf_op jit(solution)/shard_map/ppermute | solution.py:401
  43.5 3.7 %copy-start.2 = (bf16[2,9,512,512]{3,2,1,0:T(8,128)(2,1)S(1)}, bf16[2,9,512,512]{3,2,1,0:T(8,128)(2,1)}, u32[]{:S(2)}) copy-start(bf16[2,9,512,512]{3,2,1,0:T(8,128)(2,1)} %blank.1.refs_1_.refs_4_) | copy-start | bytes 28311556
  69.7 1.3 %collective-permute-start.8 = (f32[12,512]{1,0:T(8,128)S(1)}, f32[12,512]{1,0:T(8,128)S(1)}, u32[]{:S(2)}, u32[]{:S(2)}) collective-permute-start(f32[12,512]{1,0:T(8,128)S(1)} %pad_maximum_fusion), channel_id=1, source_target_pairs={{0,1},{2,3},{4,5},{6,7},{8,9},{10,11},{12,13},{14,15},{16,17},{18,... | collective-permute-start | bytes 73736 | tf_op jit(solution)/shard_map/ppermute | solution.py:415
  71.0 9.8 %collective-permute-start.9 = (f32[8,512]{1,0:T(8,128)S(1)}, f32[8,512]{1,0:T(8,128)S(1)}, u32[]{:S(2)}, u32[]{:S(2)}) collective-permute-start(f32[8,512]{1,0:T(8,128)S(1)} %slice_select_fusion), channel_id=1, source_target_pairs={{1,2},{3,4},{5,6},{7,8},{9,10},{11,12},{13,14},{15,16},{17,18},{19... | collective-permute-start | bytes 49160 | tf_op jit(solution)/shard_map/ppermute | solution.py:418
  74.9 5.9 %collective-permute-start.10 = (f32[4,512]{1,0:T(4,128)S(1)}, f32[4,512]{1,0:T(4,128)S(1)}, u32[]{:S(2)}, u32[]{:S(2)}) collective-permute-start(f32[4,512]{1,0:T(4,128)S(1)} %slice_select_fusion.1), channel_id=1, source_target_pairs={{1,4},{3,6},{5,8},{7,10},{9,12},{11,14},{13,16},{15,18},{17,20},{1... | collective-permute-start | bytes 24584 | tf_op jit(solution)/shard_map/ppermute | solution.py:419
  80.8 5.8 %collective-permute-start.11 = (f32[8,512]{1,0:T(8,128)S(1)}, f32[8,512]{1,0:T(8,128)S(1)}, u32[]{:S(2)}, u32[]{:S(2)}) collective-permute-start(f32[8,512]{1,0:T(8,128)S(1)} %select_add_fusion), channel_id=1, source_target_pairs={{0,1},{2,3},{4,5},{6,7},{8,9},{10,11},{12,13},{14,15},{16,17},{18,... | collective-permute-start | bytes 49160 | tf_op jit(solution)/shard_map/ppermute | solution.py:422
